TPU v7x, 128 devices: a whole 4x4x4 slice. The times are simulated.
128 devices in a mesh: row: 8 (over y_hi, x), col: 16 (over z, y_lo, core).
Axes of the slice: x: 4, y: 4 (y_hi: 2, y_lo: 2; y = y_hi * 2 + y_lo), z: 4, core: 2. Of those that a mesh axis runs over, the one named last changes fastest.
Arguments:
- psi_val: bfloat16 [16, 48, 2304], P(None, 'row'), may hold values from -6 to 6
- psi_cond: bfloat16 [256, 48, 2304], P('col', 'row'), may hold values from -6 to 6
- energy_val: float32 [16], replicated, may hold values from -12 to -1
- energy_cond: float32 [256], P('col'), may hold values from 0.5 to 12
- stick_map: int32 [1536], replicated, may hold values from 0 to 2303, as said below
- gvec_map: int32 [40960], P('row'), may hold values from 0 to 9215, as said below
- slab_index: int32 [1024], replicated, may hold values from 0 to 40959, as said below
Outputs:
- chi_slab: float32 [40960, 1024], P(('row', 'col'))
Inputs may be any that keep to these rules, and one draw needn't show every extreme that they name: `stick_map`: distinct values. `gvec_map`: within each aligned block of 5120 entries the values are distinct. `slab_index`: distinct values.
All inputs are finite; a program needn't handle non-finite values.
Results may differ from a plain program's by a relative error of at most 0.022.
Values may be sent and summed in bfloat16 or wider, within the bound.
A program may use at most 128 MiB of HBM per device.

v0:
```python
import math

import jax
import jax.numpy as jnp
from jax import lax
from jax.sharding import PartitionSpec as P

NX = 48
NY = 48
NZ = 48
NC = 256
NV = 16


def stick_tables(stick_map):
    flat = jnp.arange(NY * NZ, dtype=jnp.int32)
    plane_y = flat // NZ
    plane_z = flat % NZ
    freq_y = stick_map // NZ
    freq_z = stick_map % NZ
    turns = (plane_y[:, None] * freq_y[None, :] * NZ + plane_z[:, None] * freq_z[None, :] * NY) % (
        NY * NZ
    )
    angle = turns.astype(jnp.float32) * (2.0 * math.pi / (NY * NZ))
    factor = 1.0 / math.sqrt(NY * NZ)
    return (
        (jnp.cos(angle) * factor).astype(jnp.bfloat16),
        (-jnp.sin(angle) * factor).astype(jnp.bfloat16),
    )


def plane_tables():
    freq = jnp.arange(NX, dtype=jnp.int32)
    turns = freq[:, None] * freq[None, :] % NX
    angle = turns.astype(jnp.float32) * (2.0 * math.pi / NX)
    factor = 1.0 / math.sqrt(NX)
    return (
        (jnp.cos(angle) * factor).astype(jnp.bfloat16),
        (jnp.sin(angle) * factor).astype(jnp.bfloat16),
    )


def body(psi_val, psi_cond, energy_val, energy_cond, stick_map, gvec_map, slab_index):
    row_count = lax.axis_size("row")
    bands, planes, cells = psi_val.shape
    cond_local = psi_cond.shape[0]
    pairs = bands * cond_local
    sticks = stick_map.shape[0]
    stick_dev = sticks // row_count
    g_row = gvec_map.shape[0]
    scale = -1.0 / math.sqrt(NV * NC)
    weight = jnp.sqrt(2.0 / (energy_cond[None, :] - energy_val[:, None]))
    density = (
        weight[:, :, None, None]
        * psi_val[:, None].astype(jnp.float32)
        * psi_cond[None].astype(jnp.float32)
    ).astype(jnp.bfloat16)
    cos_yz, sin_yz = stick_tables(stick_map)
    table = jnp.stack(
        [cos_yz.reshape(cells, row_count, stick_dev), sin_yz.reshape(cells, row_count, stick_dev)],
        axis=2,
    )
    table = table.reshape(cells, 2 * sticks)
    spectra = jnp.dot(
        density.reshape(pairs * planes, cells), table, preferred_element_type=jnp.float32
    )
    spectra = spectra.astype(jnp.bfloat16).reshape(pairs, planes, 2 * sticks)
    cos_x, sin_x = plane_tables()
    block = lax.all_to_all(spectra, "row", split_axis=2, concat_axis=1, tiled=True)
    items = block.shape[0]
    y_real = block[:, :, :stick_dev]
    y_imag = block[:, :, stick_dev:]
    x_real = jnp.einsum(
        "kx,pxs->pks", cos_x, y_real, preferred_element_type=jnp.float32
    ) + jnp.einsum("kx,pxs->pks", sin_x, y_imag, preferred_element_type=jnp.float32)
    x_imag = jnp.einsum(
        "kx,pxs->pks", cos_x, y_imag, preferred_element_type=jnp.float32
    ) - jnp.einsum("kx,pxs->pks", sin_x, y_real, preferred_element_type=jnp.float32)
    both = jnp.stack([x_real, x_imag]).reshape(2, items, NX * stick_dev)
    picked = jnp.take(both, gvec_map, axis=2).astype(jnp.bfloat16)
    moments = picked.reshape(2 * pairs, g_row)
    owner = slab_index // g_row
    local = slab_index % g_row
    chosen = jnp.where(
        (owner == lax.axis_index("row"))[None, :],
        jnp.take(moments, local, axis=1).astype(jnp.float32),
        0.0,
    )
    slab_rows = lax.psum(chosen.astype(jnp.bfloat16), "row")
    product = lax.dot_general(
        moments, slab_rows, (((0,), (0,)), ((), ())), preferred_element_type=jnp.float32
    )
    return lax.psum_scatter(
        (product * scale).astype(jnp.bfloat16), "col", scatter_dimension=0, tiled=True
    ).astype(jnp.float32)


def solution(mesh):
    in_specs = (P(None, "row", None), P("col", "row", None), P(), P("col"), P(), P("row"), P())
    out_specs = P(("row", "col"), None)
    return jax.shard_map(body, mesh=mesh, in_specs=in_specs, out_specs=out_specs, check_vma=False)
```

profile of v0, /device:TPU:1, one launch (start us, length us, event | category | flops | bytes accessed | tf_op | source)
XLA Modules:
  0.0 788.7 jit_solution(6934806305211680469)
XLA Ops:
  10.5 5.3 multiply_convert_fusion.1
  15.8 11.6 %convert_element_type.96 = bf16[1536,2304]{1,0:T(8,128)(2,1)} reshape(bf16[16,16,6,2304]{3,2,1,0:T(8,128)(2,1)} %multiply_convert_fusion.1) | data formatting | bytes 14155776 | tf_op jit(solution)/shard_map/convert_element_type | solution.py:57
  27.4 61.5 %multiply_convert_fusion.3 = (bf16[2304,8,1,192]{0,3,2,1:T(8,128)(2,1)S(1)}, bf16[2304,8,1,192]{0,3,2,1:T(8,128)(2,1)S(1)}) fusion(s32[8,192]{1,0:T(8,128)S(1)} %mul.199, s32[2304]{0:T(1024)S(1)} %get-tuple-element.13, s32[8,192]{1,0:T(8,128)S(1)} %mul.195, s32[2304]{0:T(1024)S(1)} %get-tuple-element.14), kind=kLoop, calls=%fused_computation.10 | loop fusion | flops 60162048 | bytes 14186496 | tf_op jit(solution)/shard_map/convert_element_type | solution.py:27
  90.7 25.0 %convolution_convert_fusion = bf16[1536,3072]{1,0:T(8,128)(2,1)} fusion(bf16[1536,2304]{1,0:T(8,128)(2,1)S(1)} %bitcast.43, bf16[2304,3072]{0,1:T(8,128)(2,1)S(1)} %bitcast.41), kind=kOutput, calls=%fused_computation.15 | convolution fusion | flops 21747990528 | bytes 30670848 | tf_op jit(solution)/shard_map/dot_general | solution.py:64
  115.7 14.0 %reshape.219 = bf16[256,6,3072]{2,1,0:T(8,128)(2,1)} reshape(bf16[1536,3072]{1,0:T(8,128)(2,1)} %convolution_convert_fusion) | data formatting | bytes 18874368 | tf_op jit(solution)/shard_map/reshape | solution.py:67
  129.7 18.0 %copy.34 = bf16[256,6,3072]{0,1,2:T(8,128)(2,1)} copy(bf16[256,6,3072]{2,1,0:T(8,128)(2,1)} %reshape.219) | data formatting | bytes 18874368 | tf_op jit(solution)/shard_map/reshape | solution.py:67
  147.7 7.6 all-to-all-start
  155.5 140.9 %all-to-all-done = bf16[256,6,3072]{0,1,2:T(8,128)(2,1)} async-done(((bf16[256,6,3072]{0,1,2:T(8,128)(2,1)}), bf16[256,6,3072]{0,1,2:T(8,128)(2,1)}, u32[]{:S(2)}, u32[]{:S(2)}) %all-to-all-start) | async-done | bytes 9437216 | tf_op jit(solution)/shard_map/all_to_all | solution.py:69
  296.3 15.3 %copy.36 = bf16[256,8,6,384]{3,0,2,1:T(8,128)(2,1)} copy(bf16[256,8,6,384]{0,2,3,1:T(8,128)(2,1)} %bitcast.3) | data formatting | bytes 18874368 | tf_op jit(solution)/shard_map/all_to_all | solution.py:69
  311.7 11.8 %fusion.46 = (bf16[256,48,192]{2,0,1:T(8,128)(2,1)}, bf16[256,48,192]{2,0,1:T(8,128)(2,1)}) fusion(bf16[256,48,384]{2,0,1:T(8,128)(2,1)} %bitcast.34), kind=kLoop, calls=%fused_computation.79 | loop fusion | bytes 18874368 | tf_op jit(solution)/shard_map/slice | solution.py:71
  323.5 8.7 %copy.44 = bf16[256,48,192]{0,1,2:T(8,128)(2,1)} copy(bf16[256,48,192]{2,0,1:T(8,128)(2,1)} %get-tuple-element.5) | data formatting | bytes 9437184
  332.2 7.5 fusion.23
  339.6 8.8 %copy.45 = bf16[256,48,192]{0,1,2:T(8,128)(2,1)} copy(bf16[256,48,192]{2,0,1:T(8,128)(2,1)} %get-tuple-element.6) | data formatting | bytes 9437184
  358.6 6.2 copy.39
  364.8 8.7 %copy.41 = bf16[1,256,9216]{1,0,2:T(2,128)(2,1)S(1)} copy(bf16[1,256,9216]{1,2,0:T(8,128)(2,1)} %bitcast.39) | data formatting | bytes 9437184 | tf_op jit(solution)/shard_map/stack | solution.py:79
  377.2 4.0 copy.40
  381.2 52.5 %copy.42 = bf16[1,256,9216]{1,0,2:T(2,128)(2,1)S(1)} copy(bf16[1,256,9216]{1,2,0:T(8,128)(2,1)S(1)} %bitcast.40) | data formatting | bytes 9437184 | tf_op jit(solution)/shard_map/stack | solution.py:79
  433.7 22.7 %pad_maximum_fusion = bf16[2,256,9216]{1,0,2:T(2,128)(2,1)} fusion(bf16[1,256,9216]{1,0,2:T(2,128)(2,1)S(1)} %copy.42, bf16[1,256,9216]{1,0,2:T(2,128)(2,1)S(1)} %copy.41), kind=kLoop, calls=%fused_computation.4 | loop fusion | flops 18874368 | bytes 18874368 | tf_op jit(solution)/shard_map/stack | solution.py:79
  456.4 44.0 %gather_fusion = bf16[5120,2,256]{2,1,0:T(2,128)(2,1)} fusion(bf16[2,256,9216]{1,0,2:T(2,128)(2,1)} %pad_maximum_fusion, s32[5120]{0:T(1024)S(1)} %fusion.15), kind=kCustom, calls=%fused_computation | custom fusion | bytes 10506240 | tf_op jit(solution)/shard_map/jit(_take)/gather | solution.py:80
  503.8 4.1 select_convert_fusion
  507.9 7.1 gather_fusion.1
  516.8 131.4 %all-reduce.2.cloned.1.call-done = bf16[512,1024]{0,1:T(8,128)(2,1)} async-done(((bf16[512,1024]{0,1:T(8,128)(2,1)}), bf16[512,1024]{0,1:T(8,128)(2,1)}) %all-reduce.2.cloned.1.call-update) | async-done | bytes 1048592 | tf_op jit(solution)/shard_map/psum | solution.py:89
  648.1 11.0 %multiply_convert_fusion = bf16[5120,1024]{1,0:T(8,128)(2,1)} fusion(bf16[512,5120]{0,1:T(8,128)(2,1)} %select_convert_fusion, bf16[512,1024]{0,1:T(8,128)(2,1)} %all-reduce.2.cloned.1.call-done), kind=kOutput, calls=%fused_computation.3 | convolution fusion | flops 5379194880 | bytes 16777216 | tf_op jit(solution)/shard_map/dot_general | solution.py:90
  659.2 120.4 %reduce-scatter.2.cloned.1.call-done = bf16[320,1024]{1,0:T(8,128)(2,1)} async-done(((bf16[5120,1024]{1,0:T(8,128)(2,1)}), bf16[320,1024]{1,0:T(8,128)(2,1)}) %reduce-scatter.2.cloned.1.call-update) | async-done | bytes 655376 | tf_op jit(solution)/shard_map/reduce_scatter | solution.py:93
  (40 shorter events, 27.0 us)
Async XLA Ops:
  27.4 62.9 %slice-start.2 = ((s8[7077888]{0:T(1024)(128)(4,1)}), s8[4194304]{0:T(1024)(128)(4,1)S(1)}, s32[]{:S(2)}) async-start(s8[7077888]{0:T(1024)(128)(4,1)} %bitcast.42), calls=%async_computation.6 | async-start | bytes 8388608
  88.9 1.8 slice-start.3
  147.7 7.7 copy-start.3
  147.7 7.7 copy-start.2
  147.7 148.6 %all-to-all-start = ((bf16[256,6,3072]{0,1,2:T(8,128)(2,1)}), bf16[256,6,3072]{0,1,2:T(8,128)(2,1)}, u32[]{:S(2)}, u32[]{:S(2)}) async-start(bf16[256,6,3072]{0,1,2:T(8,128)(2,1)} %copy.34), calls=%async_computation | async-start | bytes 25165824 | tf_op jit(solution)/shard_map/all_to_all | solution.py:69
  155.3 492.8 %all-reduce.2.cloned.1.call-start = ((), (), s32[]{:S(2)}) async-start(), calls=%async_computation.2 | async-start | bytes 2097152 | tf_op jit(solution)/shard_map/psum | solution.py:89
  348.5 4.0 copy-start
  348.5 6.5 copy-start.1
  364.8 8.8 %slice-start = ((s8[4718592]{0:T(1024)(128)(4,1)}), s8[4194304]{0:T(1024)(128)(4,1)S(1)}, s32[]{:S(2)}) async-start(s8[4718592]{0:T(1024)(128)(4,1)} %bitcast.35), calls=%async_computation.4 | async-start | bytes 8388608
  364.8 8.8 %slice-start.1 = ((s8[4718592]{0:T(1024)(128)(4,1)}), s8[524288]{0:T(1024)(128)(4,1)S(1)}, s32[]{:S(2)}) async-start(s8[4718592]{0:T(1024)(128)(4,1)} %bitcast.35), calls=%async_computation.5 | async-start | bytes 1048576
  516.7 262.9 %reduce-scatter.2.cloned.1.call-start = ((), (), s32[]{:S(2)}) async-start(), calls=%async_computation.3 | async-start | bytes 11141120 | tf_op jit(solution)/shard_map/reduce_scatter | solution.py:93
Sparse Core Ops, SparseCore 0:
  516.8 131.2 all-reduce.1
  659.3 120.2 reduce-scatter.1
where the time goes:
time: 792 us; the launch traced here: 789 us
  waiting for transfers between devices  393 us (50%)
  local copies, waits for them, and re-layouts  220 us (28%)
  other arithmetic  100 us (13%)
  matrix products  54.6 us (7%)
  between operations  13.6 us (2%)
    all_to_all x1, waiting for transfers between devices, body(): lax.all_to_all(spectra, 'row', split_axis=2, concat_axis=1, tiled=True)  141 us
    psum x1, waiting for transfers between devices, body(): slab_rows = lax.psum(chosen.astype(jnp.bfloat16), 'row')  131 us
    reduce_scatter x1, waiting for transfers between devices, body(): lax.psum_scatter((product * scale).astype(jnp.bfloat16), 'col', scatter_d...  120 us
    convert_element_type x1, other arithmetic, stick_tables(): (jnp.cos(angle) * factor).astype(jnp.bfloat16)  61.5 us
    another operation x2, local copies, waits for them, and re-layouts, body(): both = jnp.stack([x_real, x_imag]).reshape(2, items, NX * stick_dev)  61.3 us
    gather x1, local copies, waits for them, and re-layouts, body(): picked = jnp.take(both, gvec_map, axis=2).astype(jnp.bfloat16)  44 us
    reshape x2, local copies, waits for them, and re-layouts, body(): spectra = spectra.astype(jnp.bfloat16).reshape(pairs, planes, 2 * sticks)  32 us
    dot_general x1, matrix products, body(): jnp.dot(density.reshape(pairs * planes, cells), table, preferred_element_...  25 us
  transfers between devices with their start and end apart: 3, of which 3 were waited for; matrix products, arithmetic and copies ran while one was open for 0% of the time, Pallas kernels for 0%

commit v1 on v0

v1 whole, which is shorter than its diff:
```python
import functools
import math

import jax
import jax.numpy as jnp
from jax import lax
from jax.experimental import pallas as pl
from jax.experimental.pallas import tpu as pltpu
from jax.sharding import PartitionSpec as P

NX = 48
NY = 48
NZ = 48
CELLS = NY * NZ
HALF = CELLS // 2
NC = 256
NV = 16
CL = 16
PAIRS = NV * CL
STK = 192
G_ROW = 5120
NS = 1024
JS = 128
XB = 4
LANES = 256
VMEM_LIMIT = 60 * 1024 * 1024


def half_phase(ky, kz):
    unit = math.pi / 48.0
    y = 2 * jnp.arange(NY // 2, dtype=jnp.int32) + 1
    z = 2 * jnp.arange(NZ, dtype=jnp.int32) + 1
    ay = ((y[:, None] * ky[None, :]) % 96).astype(jnp.float32) * unit
    az = ((z[:, None] * kz[None, :]) % 96).astype(jnp.float32) * unit
    cy, sy = jnp.cos(ay)[:, None, :], jnp.sin(ay)[:, None, :]
    cz, sz = jnp.cos(az)[None, :, :], jnp.sin(az)[None, :, :]
    cos = (cy * cz - sy * sz).reshape(HALF, -1)
    sin = -(sy * cz + cy * sz).reshape(HALF, -1)
    return cos.astype(jnp.bfloat16), sin.astype(jnp.bfloat16)


def planes_kernel(psi_ref, tc_ref, ts_ref, rot_ref, ph_ref, w_ref, y_ref, s_ref, pvf, ev, od, sacc):
    step = pl.program_id(0)

    @pl.when(step == 0)
    def _():
        sacc[...] = jnp.zeros_like(sacc)

    for xi in range(XB):
        pvf[xi] = psi_ref[xi, :NV, :].astype(jnp.float32)

    for xi in range(XB):

        def one(v, carry, xi=xi):
            row = pvf[xi, pl.ds(v, 1), :]
            d = jnp.broadcast_to(row, (CL, CELLS)).astype(jnp.bfloat16) * psi_ref[xi, NV:, :]
            lo, hi = d[:, :HALF], d[:, HALF:]
            at = pl.ds(pl.multiple_of(xi * PAIRS + v * CL, CL), CL)
            ev[at, :] = lo + hi
            od[at, :] = lo - hi
            return carry

        lax.fori_loop(0, NV, one, 0, unroll=2)

    cosr = rot_ref[0:1, :]
    sinr = rot_ref[1:2, :]
    for xi in range(XB):
        rows = pl.ds(xi * PAIRS, PAIRS)
        a = jnp.dot(ev[rows, :], tc_ref[...], preferred_element_type=jnp.float32)
        b = jnp.dot(od[rows, :], ts_ref[...], preferred_element_type=jnp.float32)
        am, bm = a[:, :LANES], b[:, :LANES]
        y_ref[xi, 0] = (cosr * am - sinr * bm).astype(jnp.bfloat16)
        y_ref[xi, 1] = (cosr * bm + sinr * am).astype(jnp.bfloat16)
        asl, bsl = a[:, LANES:], b[:, LANES:]
        cp = ph_ref[xi, 0:1, :]
        sp = ph_ref[xi, 1:2, :]
        sacc[0] += cp * asl - sp * bsl
        sacc[1] += cp * bsl + sp * asl

    @pl.when(step == pl.num_programs(0) - 1)
    def _():
        s_ref[0] = (sacc[0] * w_ref[...]).astype(jnp.bfloat16)
        s_ref[1] = (sacc[1] * w_ref[...]).astype(jnp.bfloat16)


def planes(psi, tc, ts, rot, ph, wide):
    full = lambda *shape: pl.BlockSpec(shape, lambda i: (0,) * len(shape))
    return pl.pallas_call(
        planes_kernel,
        grid=(NX // XB,),
        in_specs=[
            pl.BlockSpec((XB, NV + CL, CELLS), lambda i: (i, 0, 0)),
            full(HALF, LANES + JS),
            full(HALF, LANES + JS),
            full(2, LANES),
            pl.BlockSpec((XB, 2, JS), lambda i: (i, 0, 0)),
            full(PAIRS, JS),
        ],
        out_specs=[
            pl.BlockSpec((XB, 2, PAIRS, LANES), lambda i: (i, 0, 0, 0)),
            full(2, PAIRS, JS),
        ],
        out_shape=[
            jax.ShapeDtypeStruct((NX, 2, PAIRS, LANES), jnp.bfloat16),
            jax.ShapeDtypeStruct((2, PAIRS, JS), jnp.bfloat16),
        ],
        scratch_shapes=[
            pltpu.VMEM((XB, NV, CELLS), jnp.float32),
            pltpu.VMEM((XB * PAIRS, HALF), jnp.bfloat16),
            pltpu.VMEM((XB * PAIRS, HALF), jnp.bfloat16),
            pltpu.VMEM((2, PAIRS, JS), jnp.float32),
        ],
        compiler_params=pltpu.CompilerParams(vmem_limit_bytes=VMEM_LIMIT),
        name="planes",
    )(psi, tc, ts, rot, ph, wide)


PB = 16


def lines_kernel(w_ref, y_ref, t_ref, m_ref, yr, yi, mo):
    base = pl.program_id(0) * PB
    for h in range(LANES // 128):
        lanes = slice(h * 128, h * 128 + 128)
        yr[h] = y_ref[:, 0, :, lanes].astype(jnp.float32).reshape(NX * PB, 128)
        yi[h] = y_ref[:, 1, :, lanes].astype(jnp.float32).reshape(NX * PB, 128)
    for p in range(PB):
        at = pl.ds(p, NX, stride=PB)
        real = jnp.concatenate([yr[0, at, :], yr[1, at, :]], axis=1)
        imag = jnp.concatenate([yi[0, at, :], yi[1, at, :]], axis=1)
        rhs = jnp.concatenate([real, imag], axis=0).astype(jnp.bfloat16)
        out = jnp.dot(t_ref[...], rhs, preferred_element_type=jnp.float32) * w_ref[base + p]
        for h in range(LANES // 128):
            mo[h, pl.ds(p, 2 * NX, stride=PB), :] = out[:, h * 128 : h * 128 + 128]
    for h in range(LANES // 128):
        lanes = slice(h * 128, h * 128 + 128)
        m_ref[:, :, lanes] = mo[h].reshape(2 * NX, PB, 128).astype(jnp.bfloat16)


def lines(weights, y, table):
    return pl.pallas_call(
        lines_kernel,
        grid_spec=pltpu.PrefetchScalarGridSpec(
            num_scalar_prefetch=1,
            grid=(PAIRS // PB,),
            in_specs=[
                pl.BlockSpec((NX, 2, PB, LANES), lambda i, w: (0, 0, i, 0)),
                pl.BlockSpec((2 * NX, 2 * NX), lambda i, w: (0, 0)),
            ],
            out_specs=pl.BlockSpec((2 * NX, PB, LANES), lambda i, w: (0, i, 0)),
            scratch_shapes=[
                pltpu.VMEM((2, NX * PB, 128), jnp.float32),
                pltpu.VMEM((2, NX * PB, 128), jnp.float32),
                pltpu.VMEM((2, 2 * NX * PB, 128), jnp.float32),
            ],
        ),
        out_shape=jax.ShapeDtypeStruct((2 * NX, PAIRS, LANES), jnp.bfloat16),
        compiler_params=pltpu.CompilerParams(vmem_limit_bytes=VMEM_LIMIT),
        name="lines",
    )(weights, y, table)


GB = 320
QS = 2 * PAIRS // 128


def chi_kernel(g_ref, m_ref, s_ref, o_ref, mt, sel):
    step = pl.program_id(0)

    @pl.when(step < NX)
    def _():
        for h in range(2):
            for q in range(2):
                a = m_ref[h, 0, q * 128 : q * 128 + 128, :].astype(jnp.float32)
                t = a.T
                at = pl.ds(step * (STK * QS) + h * 2 + q, STK, stride=QS)
                mt[at, :] = t[:STK, :]

    @pl.when(step >= NX)
    def _():
        base = (step - NX) * GB

        def pick(i, carry):
            for u in range(8):
                g = g_ref[base + i * 8 + u]
                sel[pl.ds(pl.multiple_of(i * 32 + u * QS, QS), QS), :] = mt[
                    pl.ds(pl.multiple_of(g * QS, QS), QS), :
                ]
            return carry

        lax.fori_loop(0, GB // 8, pick, 0)
        lhs = jnp.concatenate(
            [sel[pl.ds(q, GB, stride=QS), :].astype(jnp.bfloat16) for q in range(QS)], axis=1
        )
        scale = -1.0 / math.sqrt(NV * NC)
        for r in range(NS // JS):
            out = jnp.dot(lhs, s_ref[r], preferred_element_type=jnp.float32)
            o_ref[:, r * JS : r * JS + JS] = (out * scale).astype(jnp.bfloat16)


def chi(gvec, m, s):
    return pl.pallas_call(
        chi_kernel,
        grid_spec=pltpu.PrefetchScalarGridSpec(
            num_scalar_prefetch=1,
            grid=(NX + G_ROW // GB,),
            in_specs=[
                pl.BlockSpec((2, 1, PAIRS, LANES), lambda i, g: (0, jnp.minimum(i, NX - 1), 0, 0)),
                pl.BlockSpec((NS // JS, 2 * PAIRS, JS), lambda i, g: (0, 0, 0)),
            ],
            out_specs=pl.BlockSpec((GB, NS), lambda i, g: (jnp.maximum(i - NX, 0), 0)),
            scratch_shapes=[
                pltpu.VMEM((NX * STK * QS, 128), jnp.float32),
                pltpu.VMEM((GB * QS, 128), jnp.float32),
            ],
        ),
        out_shape=jax.ShapeDtypeStruct((G_ROW, NS), jnp.bfloat16),
        compiler_params=pltpu.CompilerParams(vmem_limit_bytes=VMEM_LIMIT),
        name="chi",
    )(gvec, m, s)


def body(psi_val, psi_cond, energy_val, energy_cond, stick_map, gvec_map, slab_index):
    row = lax.axis_index("row")
    both = jnp.concatenate([psi_val, psi_cond], axis=0).transpose(1, 0, 2)
    both = jnp.concatenate([both[:, :, :HALF], jnp.flip(both[:, :, HALF:], axis=2)], axis=2)
    psi = lax.all_gather(both, "row", axis=0, tiled=True)
    maps = lax.all_gather(gvec_map, "row", axis=0, tiled=True)

    mine = lax.dynamic_slice(stick_map, (row * STK,), (STK,))
    cols = lax.dynamic_slice(slab_index, (row * JS,), (JS,))
    place = jnp.take(maps, cols)
    col_kx = place // STK
    col_stick = jnp.take(stick_map, cols // G_ROW * STK + place % STK)
    pad = jnp.zeros((LANES - STK,), jnp.int32)
    flat = jnp.concatenate([mine, pad, col_stick])
    ky, kz = flat // NZ, flat % NZ
    tc, ts = half_phase(ky, kz)
    turn = ((ky + kz) % 96).astype(jnp.float32) * (math.pi / 48.0)
    rot = jnp.stack([jnp.cos(turn[:LANES]), jnp.sin(turn[:LANES])])
    xs = jnp.arange(NX, dtype=jnp.int32)
    theta = (
        ((ky + kz)[None, LANES:] - 2 * (xs[:, None] * col_kx[None, :]) + 96 * NX) % 96
    ).astype(jnp.float32) * (math.pi / 48.0)
    ph = jnp.stack([jnp.cos(theta), jnp.sin(theta)], axis=1)

    weight = jnp.sqrt(2.0 / (energy_cond[None, :] - energy_val[:, None])) * (
        1.0 / (math.sqrt(NY * NZ) * math.sqrt(NX))
    )
    weight = weight.reshape(PAIRS)
    wide = jnp.broadcast_to(weight[:, None], (PAIRS, JS))
    ax = (xs[:, None] * xs[None, :] % NX).astype(jnp.float32) * (2.0 * math.pi / NX)
    cx, sx = jnp.cos(ax), jnp.sin(ax)
    table = jnp.concatenate(
        [jnp.concatenate([cx, sx], axis=1), jnp.concatenate([-sx, cx], axis=1)], axis=0
    ).astype(jnp.bfloat16)

    y, s_part = planes(psi, tc, ts, rot, ph, wide)
    slab = lax.all_gather(s_part.reshape(2 * PAIRS, JS), "row", axis=0, tiled=False)
    m = lines(weight, y, table)
    part = chi(gvec_map, m.reshape(2, NX, PAIRS, LANES), slab)
    return lax.psum_scatter(part, "col", scatter_dimension=0, tiled=True).astype(jnp.float32)


def solution(mesh):
    in_specs = (P(None, "row", None), P("col", "row", None), P(), P("col"), P(), P("row"), P())
    out_specs = P(("row", "col"), None)
    return jax.shard_map(body, mesh=mesh, in_specs=in_specs, out_specs=out_specs, check_vma=False)
```

time: 792 us -> 391 us (0.49)
  local copies, waits for them, and re-layouts: 220 us -> 4.36 us
  waiting for transfers between devices: 393 us -> 199 us
  Pallas kernels: 0 us -> 131 us
  other arithmetic: 100 us -> 11.6 us
  matrix products: 54.6 us -> 0 us
  blocking collectives: 0 us -> 29.6 us
    all_to_all x1 -> x0, waiting for transfers between devices: 141 us -> none  [body(): lax.all_to_all(spectra, 'row', split_axis=2, concat_axis=1, tiled=True)]
    psum x1 -> x0, waiting for transfers between devices: 131 us -> none  [body(): slab_rows = lax.psum(chosen.astype(jnp.bfloat16), 'row')]
    pallas_call x0 -> x3, Pallas kernels: none -> 131 us  [the longest x1 54.2 us: chi(): pl.pallas_call(chi_kernel, grid_spec=pltpu.PrefetchScalarGridSpec(num_sca...]
    all_gather x0 -> x2, waiting for transfers between devices: none -> 81.3 us  [the longest x1 62.1 us: body(): psi = lax.all_gather(both, 'row', axis=0, tiled=True)]
    convert_element_type x5 -> x3, other arithmetic: 74.8 us -> 4.08 us  [the longest x1 2.29 us: body(): lax.psum_scatter(part, 'col', scatter_dimension=0, tiled=True)]
    another operation x2 -> x0, local copies, waits for them, and re-layouts: 61.3 us -> none  [body(): both = jnp.stack([x_real, x_imag]).reshape(2, items, NX * stick_dev)]
    dot_general x6 -> x0, matrix products: 54.6 us -> none  [the longest x1 25 us: body(): jnp.dot(density.reshape(pairs * planes, cells), table, preferred_element_...]
    gather x2, local copies, waits for them, and re-layouts: 51.1 us -> 2.29 us  [the longest x1 1.15 us: body(): col_stick = jnp.take(stick_map, cols // G_ROW * STK + place % STK)]
  transfers between devices with their start and end apart: 3 -> 3, of which waited for: 3 -> 3; matrix products, arithmetic and copies ran while one was open for 0% -> 2% of each run, Pallas kernels for 0% -> 6%
where the time goes in v1:
time: 391 us; the launch traced here: 388 us
  waiting for transfers between devices  199 us (51%)
  Pallas kernels  131 us (34%)
  blocking collectives  29.6 us (8%)
  between operations  13.3 us (3%)
  other arithmetic  11.6 us (3%)
  local copies, waits for them, and re-layouts  4.36 us (1%)
    reduce_scatter x1, waiting for transfers between devices, body(): lax.psum_scatter(part, 'col', scatter_dimension=0, tiled=True)  117 us
    all_gather x1, waiting for transfers between devices, body(): psi = lax.all_gather(both, 'row', axis=0, tiled=True)  62.1 us
    pallas_call x1, Pallas kernels, chi(): pl.pallas_call(chi_kernel, grid_spec=pltpu.PrefetchScalarGridSpec(num_sca...  54.2 us
    pallas_call x1, Pallas kernels, planes(): pl.pallas_call(planes_kernel, grid=(NX // XB,), in_specs=[pl.BlockSpec((X...  51.8 us
    all_gather x1, blocking collectives, body(): maps = lax.all_gather(gvec_map, 'row', axis=0, tiled=True)  29.6 us
    pallas_call x1, Pallas kernels, lines(): pl.pallas_call(lines_kernel, grid_spec=pltpu.PrefetchScalarGridSpec(num_s...  24.6 us
    all_gather x1, waiting for transfers between devices, body(): lax.all_gather(s_part.reshape(2 * PAIRS, JS), 'row', axis=0, tiled=False)  19.2 us
  transfers between devices with their start and end apart: 3, of which 3 were waited for; matrix products, arithmetic and copies ran while one was open for 2% of the time, Pallas kernels for 6%

profile of v1, /device:TPU:1, one launch (start us, length us, event | category | flops | bytes accessed | tf_op | source)
XLA Modules:
  0.0 388.1 jit_solution(9392967777576261831)
XLA Ops:
  6.5 1.2 maximum_bitcast_fusion
  7.9 1.0 rev.4
  8.9 1.0 pad_maximum_fusion
  10.2 29.6 %all_gather.10 = s32[40960]{0:T(1024)S(1)} all-gather(s32[5120]{0:T(1024)S(1)} %copy-done.1), channel_id=1, replica_groups=mesh['row'=8,'col'=16] {'row'}, dimensions={0}, use_global_device_ids=true | all-gather | bytes 184320 | tf_op jit(solution)/shard_map/all_gather | solution.py:228
  39.8 0.8 compare_select_fusion.1
  40.6 1.1 gather_fusion
  41.7 0.8 and_select_fusion
  42.5 1.1 gather_fusion.1
  44.0 0.6 pad_maximum_fusion.2.rot_ref
  44.6 0.7 multiply_cosine_fusion
  45.3 0.7 pad_maximum_fusion.1.ph_ref
  46.0 0.2 fusion.12
  46.2 0.4 fusion.5
  46.6 1.8 negate_convert_fusion
  48.4 62.1 %all-gather.3.cloned.1.call-done.psi_ref = bf16[48,32,2304]{2,1,0:T(8,128)(2,1)} async-done(((bf16[6,32,2304]{2,1,0:T(8,128)(2,1)}), bf16[48,32,2304]{2,1,0:T(8,128)(2,1)}) %all-gather.3.cloned.1.call-update) | async-done | bytes 7077904 | tf_op jit(solution)/shard_map/all_gather | solution.py:227
  110.4 0.8 broadcast_in_dim.22.w_ref
  111.2 51.8 %planes.1 = (bf16[48,2,256,256]{3,2,1,0:T(8,128)(2,1)}, bf16[2,256,128]{2,1,0:T(8,128)(2,1)}) custom-call(bf16[48,32,2304]{2,1,0:T(8,128)(2,1)} %all-gather.3.cloned.1.call-done.psi_ref, bf16[1152,384]{1,0:T(8,128)(2,1)} %bitcast.11, bf16[1152,384]{1,0:T(8,128)(2,1)} %bitcast.10, f32[2,256]{1,0:T(2,128)} %pad_maximum_fusion.2.rot_ref, ...), custom_call_target="tpu_custom_call" | custom-call | tf_op jit(solution)/shard_map/planes/pallas_call | solution.py:88
  163.2 0.1 negate_convert_fusion.1
  163.3 0.7 maximum_maximum_fusion.t_ref
  164.0 24.6 %lines.1 = bf16[96,256,256]{2,1,0:T(8,128)(2,1)} custom-call(f32[256]{0:T(256)} %copy-done.2, bf16[48,2,256,256]{3,2,1,0:T(8,128)(2,1)} %get-tuple-element.7.y_ref, bf16[96,96]{1,0:T(8,128)(2,1)} %maximum_maximum_fusion.t_ref), custom_call_target="tpu_custom_call" | custom-call | tf_op jit(solution)/shard_map/lines/pallas_call | solution.py:141
  188.6 19.2 %all-gather.5.cloned.1.call-done.s_ref = bf16[8,512,128]{2,1,0:T(8,128)(2,1)} async-done(((bf16[1,512,128]{2,1,0:T(8,128)(2,1)}), bf16[8,512,128]{2,1,0:T(8,128)(2,1)}) %all-gather.5.cloned.1.call-update) | async-done | bytes 1048592 | tf_op jit(solution)/shard_map/all_gather | solution.py:259
  207.9 54.2 %chi.1 = bf16[5120,1024]{1,0:T(8,128)(2,1)} custom-call(s32[5120]{0:T(1024)} %g_ref.1, bf16[2,48,256,256]{3,2,1,0:T(8,128)(2,1)} %bitcast.9, bf16[8,512,128]{2,1,0:T(8,128)(2,1)} %all-gather.5.cloned.1.call-done.s_ref), custom_call_target="tpu_custom_call" | custom-call | tf_op jit(solution)/shard_map/chi/pallas_call | solution.py:202
  262.1 117.2 %reduce-scatter.2.cloned.1.call-done = bf16[320,1024]{1,0:T(8,128)(2,1)} async-done(((bf16[5120,1024]{1,0:T(8,128)(2,1)}), bf16[320,1024]{1,0:T(8,128)(2,1)}) %reduce-scatter.2.cloned.1.call-update) | async-done | bytes 655376 | tf_op jit(solution)/shard_map/reduce_scatter | solution.py:262
  379.3 2.3 convert_element_type.69
  (32 shorter events, 0.9 us)
Async XLA Ops:
  6.5 103.9 %all-gather.3.cloned.1.call-start = ((), (), s32[]{:S(2)}) async-start(), calls=%async_computation.1 | async-start | bytes 7962624 | tf_op jit(solution)/shard_map/all_gather | solution.py:227
  7.8 2.1 copy-start.3
  7.8 2.1 copy-start.4
  7.9 2.3 copy-start
  7.9 2.4 copy-start.1
  9.9 198.0 %all-gather.5.cloned.1.call-start = ((), (), s32[]{:S(2)}) async-start(), calls=%async_computation.2 | async-start | bytes 1179648 | tf_op jit(solution)/shard_map/all_gather | solution.py:259
  10.1 100.3 %copy-start.2 = (f32[256]{0:T(256)}, f32[256]{0:T(256)S(1)}, u32[]{:S(2)}) copy-start(f32[256]{0:T(256)S(1)} %mul.270.w_ref) | copy-start | bytes 3076
  163.0 216.3 %reduce-scatter.2.cloned.1.call-start = ((), (), s32[]{:S(2)}) async-start(), calls=%async_computation.3 | async-start | bytes 11141120 | tf_op jit(solution)/shard_map/reduce_scatter | solution.py:262
Sparse Core Ops, SparseCore 0:
  10.0 100.3 all-gather.2
  163.1 44.7 all-gather.4
  262.2 117.0 reduce-scatter.1

commit v2 on v1

--- a/solution.py
+++ b/solution.py
@@ -220,16 +220,184 @@
     )(gvec, m, s)
 
 
+MESH = pl.DeviceIdType.MESH
+G_DEV = 320
+HR = G_DEV // 2
+
+
+def add_rows(dst, dst_at, a, b, rows, step=32):
+    def one(i, carry):
+        at = pl.ds(pl.multiple_of(dst_at + i * step, 16), step)
+        src = pl.ds(pl.multiple_of(b[1] + i * step, 16), step)
+        dst[at, :] = (a[at, :].astype(jnp.float32) + b[0][src, :].astype(jnp.float32)).astype(dst.dtype)
+        return carry
+
+    lax.fori_loop(0, rows // step, one, 0)
+
+
+def share_kernel(part, out, acc, r1, zr2, yr1, zr1, yr2, lsem, s1, d1, sz2, dz2, sy1, dy1, sz1, dz1, sy2, dy2):
+    row, col = lax.axis_index("row"), lax.axis_index("col")
+    z, yl, core = col // 4, (col // 2) % 2, col % 2
+    core_peer = {"row": row, "col": z * 4 + yl * 2 + (1 - core)}
+    y_peer = {"row": row, "col": z * 4 + (1 - yl) * 2 + core}
+    z_peer = lambda k: {"row": row, "col": ((z + k) % 4) * 4 + yl * 2 + core}
+    barrier = pltpu.get_barrier_semaphore()
+    for peer in (core_peer, y_peer, z_peer(1), z_peer(2), z_peer(3)):
+        pl.semaphore_signal(barrier, inc=1, device_id=peer, device_id_type=MESH)
+    pl.semaphore_wait(barrier, 5)
+
+    order = [(k, s) for k in (2, 1, 3, 0) for s in (0, 1)]
+    first, local = {}, {}
+    for k, s in order:
+        slot = k * 2 + s
+        q = ((z + k) % 4) * 4 + (yl if s else 1 - yl) * 2
+        first[slot] = pltpu.make_async_remote_copy(
+            part.at[q + 1 - core], r1.at[slot], s1.at[slot], d1.at[slot], device_id=core_peer, device_id_type=MESH
+        )
+        first[slot].start()
+        local[slot] = pltpu.make_async_copy(part.at[q + core], acc.at[slot], lsem.at[slot])
+        local[slot].start()
+    sends = []
+
+    def send(src, dst, ss, ds, peer):
+        copy = pltpu.make_async_remote_copy(src, dst, ss, ds, device_id=peer, device_id_type=MESH)
+        copy.start()
+        sends.append(copy)
+        return copy
+
+    lo, hi = pl.ds(0, HR), pl.ds(HR, HR)
+    along_y, along_z = {}, {}
+    for k, s in order:
+        slot = k * 2 + s
+        local[slot].wait()
+        first[slot].wait_recv()
+        add_rows(acc.at[slot], 0, acc.at[slot], (r1.at[slot], 0), G_DEV)
+        if k:
+            i = (k - 1) * 2 + s
+            along_z[k, s] = send(acc.at[slot, hi], zr2.at[i], sz2.at[i], dz2.at[i], z_peer(k))
+        if s == 0:
+            along_y[k] = send(acc.at[slot, lo], yr1.at[k], sy1.at[k], dy1.at[k], y_peer)
+    last_z = {}
+    for k in (2, 1, 3, 0):
+        along_y[k].wait_recv()
+        if k:
+            slot = k * 2 + 1
+            add_rows(acc.at[slot], 0, acc.at[slot], (yr1.at[k], 0), HR)
+            last_z[k] = send(acc.at[slot, lo], zr1.at[k - 1], sz1.at[k - 1], dz1.at[k - 1], z_peer(k))
+    for k in (1, 3, 2):
+        along_z[k, 0].wait_recv()
+
+    def total(i, base, terms):
+        at = pl.ds(pl.multiple_of(i * 16, 16), 16)
+        value = base[pl.ds(pl.multiple_of(i * 16, 16), 16), :].astype(jnp.float32)
+        for ref in terms:
+            value = value + ref[at, :].astype(jnp.float32)
+        return at, value
+
+    def turn(i, carry):
+        at, value = total(i, acc.at[0, hi], [zr2.at[0], zr2.at[2], zr2.at[4]])
+        yr2[0, at, :] = value.astype(jnp.bfloat16)
+        return carry
+
+    lax.fori_loop(0, HR // 16, turn, 0)
+    last_y = send(yr2.at[0], yr2.at[1], sy2.at[0], dy2.at[0], y_peer)
+    for k in (1, 3, 2):
+        last_z[k].wait_recv()
+
+    def low(i, carry):
+        at, value = total(i, acc.at[1, lo], [yr1.at[0], zr1.at[0], zr1.at[1], zr1.at[2]])
+        out[at, :] = value
+        return carry
+
+    lax.fori_loop(0, HR // 16, low, 0)
+    for k in (1, 3, 2):
+        along_z[k, 1].wait_recv()
+    last_y.wait_recv()
+
+    def high(i, carry):
+        at, value = total(i, acc.at[1, hi], [zr2.at[1], zr2.at[3], zr2.at[5], yr2.at[1]])
+        out[pl.ds(pl.multiple_of(HR + i * 16, 16), 16), :] = value
+        return carry
+
+    lax.fori_loop(0, HR // 16, high, 0)
+    for copy in list(first.values()) + sends:
+        copy.wait_send()
+
+
+def share(part):
+    dma = pltpu.SemaphoreType.DMA
+    half = lambda n: pltpu.VMEM((n, HR, NS), jnp.bfloat16)
+    return pl.pallas_call(
+        share_kernel,
+        in_specs=[pl.BlockSpec(memory_space=pl.ANY)],
+        out_specs=pl.BlockSpec(memory_space=pltpu.VMEM),
+        out_shape=jax.ShapeDtypeStruct((G_DEV, NS), jnp.float32),
+        scratch_shapes=[
+            pltpu.VMEM((8, G_DEV, NS), jnp.bfloat16),
+            pltpu.VMEM((8, G_DEV, NS), jnp.bfloat16),
+            half(6), half(4), half(3), half(2),
+            dma((8,)), dma((8,)), dma((8,)), dma((6,)), dma((6,)), dma((4,)), dma((4,)),
+            dma((3,)), dma((3,)), dma((1,)), dma((1,)),
+        ],
+        compiler_params=pltpu.CompilerParams(
+            collective_id=3, has_side_effects=True, vmem_limit_bytes=VMEM_LIMIT
+        ),
+        name="share",
+    )(part)
+
+
+def places_kernel(mine, out, got, send_sem, recv_sem):
+    row, col = lax.axis_index("row"), lax.axis_index("col")
+    barrier = pltpu.get_barrier_semaphore()
+    for k in range(1, 8):
+        pl.semaphore_signal(barrier, inc=1, device_id={"row": (row + k) % 8, "col": col}, device_id_type=MESH)
+    pl.semaphore_wait(barrier, 7)
+    copies = []
+    for k in range(1, 8):
+        to = (row + k) % 8
+        copies.append(
+            pltpu.make_async_remote_copy(
+                mine.at[to], got.at[k - 1], send_sem.at[k - 1], recv_sem.at[k - 1],
+                device_id={"row": to, "col": col}, device_id_type=MESH,
+            )
+        )
+        copies[-1].start()
+    total = mine[row]
+    for k in range(1, 8):
+        copies[k - 1].wait_recv()
+        total = total + got[k - 1]
+    out[...] = total
+    for copy in copies:
+        copy.wait_send()
+
+
+def places(mine):
+    return pl.pallas_call(
+        places_kernel,
+        in_specs=[pl.BlockSpec(memory_space=pltpu.VMEM)],
+        out_specs=pl.BlockSpec(memory_space=pltpu.VMEM),
+        out_shape=jax.ShapeDtypeStruct((8, JS), jnp.int32),
+        scratch_shapes=[
+            pltpu.VMEM((7, 8, JS), jnp.int32),
+            pltpu.SemaphoreType.DMA((7,)),
+            pltpu.SemaphoreType.DMA((7,)),
+        ],
+        compiler_params=pltpu.CompilerParams(collective_id=1, has_side_effects=True),
+        name="places",
+    )(mine)
+
+
 def body(psi_val, psi_cond, energy_val, energy_cond, stick_map, gvec_map, slab_index):
     row = lax.axis_index("row")
     both = jnp.concatenate([psi_val, psi_cond], axis=0).transpose(1, 0, 2)
     both = jnp.concatenate([both[:, :, :HALF], jnp.flip(both[:, :, HALF:], axis=2)], axis=2)
     psi = lax.all_gather(both, "row", axis=0, tiled=True)
-    maps = lax.all_gather(gvec_map, "row", axis=0, tiled=True)
 
     mine = lax.dynamic_slice(stick_map, (row * STK,), (STK,))
     cols = lax.dynamic_slice(slab_index, (row * JS,), (JS,))
-    place = jnp.take(maps, cols)
+    held = jnp.where(slab_index // G_ROW == row, jnp.take(gvec_map, slab_index % G_ROW), 0)
+    held = jnp.broadcast_to(held.reshape(NS // JS, 1, JS), (NS // JS, 8, JS))
+    place = places(held)[0]
     col_kx = place // STK
     col_stick = jnp.take(stick_map, cols // G_ROW * STK + place % STK)
     pad = jnp.zeros((LANES - STK,), jnp.int32)
@@ -259,7 +427,7 @@
     slab = lax.all_gather(s_part.reshape(2 * PAIRS, JS), "row", axis=0, tiled=False)
     m = lines(weight, y, table)
     part = chi(gvec_map, m.reshape(2, NX, PAIRS, LANES), slab)
-    return lax.psum_scatter(part, "col", scatter_dimension=0, tiled=True).astype(jnp.float32)
+    return share(part.reshape(G_ROW // G_DEV, G_DEV, NS))
 
 
 def solution(mesh):

time: 391 us -> 325 us (0.83)
  waiting for transfers between devices: 199 us -> 94.6 us
  Pallas kernels: 131 us -> 193 us
  blocking collectives: 29.6 us -> 0 us
  local copies, waits for them, and re-layouts: 4.36 us -> 12.5 us
    reduce_scatter x1 -> x0, waiting for transfers between devices: 117 us -> none  [body(): lax.psum_scatter(part, 'col', scatter_dimension=0, tiled=True)]
    pallas_call x0 -> x2, Pallas kernels: none -> 62.6 us  [the longest x1 52.6 us: share(): pl.pallas_call(share_kernel, in_specs=[pl.BlockSpec(memory_space=pl.ANY)]...]
    all_gather x1 -> x0, blocking collectives: 29.6 us -> none  [body(): maps = lax.all_gather(gvec_map, 'row', axis=0, tiled=True)]
    all_gather x1, waiting for transfers between devices: 62.1 us -> 75.3 us  [body(): psi = lax.all_gather(both, 'row', axis=0, tiled=True)]
    gather x1, local copies, waits for them, and re-layouts: 1.15 us -> 6.15 us  [body(): jnp.take(gvec_map, slab_index % G_ROW)]
  transfers between devices with their start and end apart: 3 -> 2, of which waited for: 3 -> 2; matrix products, arithmetic and copies ran while one was open for 2% -> 5% of each run, Pallas kernels for 6% -> 11%
where the time goes in v2:
time: 325 us; the launch traced here: 323 us
  Pallas kernels  193 us (59%)
  waiting for transfers between devices  94.6 us (29%)
  between operations  13.6 us (4%)
  local copies, waits for them, and re-layouts  12.5 us (4%)
  other arithmetic  9.29 us (3%)
    all_gather x1, waiting for transfers between devices, body(): psi = lax.all_gather(both, 'row', axis=0, tiled=True)  75.3 us
    pallas_call x1, Pallas kernels, chi(): pl.pallas_call(chi_kernel, grid_spec=pltpu.PrefetchScalarGridSpec(num_sca...  54.2 us
    pallas_call x1, Pallas kernels, share(): pl.pallas_call(share_kernel, in_specs=[pl.BlockSpec(memory_space=pl.ANY)]...  52.6 us
    pallas_call x1, Pallas kernels, planes(): pl.pallas_call(planes_kernel, grid=(NX // XB,), in_specs=[pl.BlockSpec((X...  51.8 us
    pallas_call x1, Pallas kernels, lines(): pl.pallas_call(lines_kernel, grid_spec=pltpu.PrefetchScalarGridSpec(num_s...  24.7 us
    all_gather x1, waiting for transfers between devices, body(): lax.all_gather(s_part.reshape(2 * PAIRS, JS), 'row', axis=0, tiled=False)  19.3 us
    pallas_call x1, Pallas kernels, places(): pl.pallas_call(places_kernel, in_specs=[pl.BlockSpec(memory_space=pltpu.V...  10 us
  transfers between devices with their start and end apart: 2, of which 2 were waited for; matrix products, arithmetic and copies ran while one was open for 5% of the time, Pallas kernels for 11%

profile of v2, /device:TPU:1, one launch (start us, length us, event | category | flops | bytes accessed | tf_op | source)
XLA Modules:
  0.0 323.3 jit_solution(15100272152932165987)
XLA Ops:
  6.5 1.2 maximum_bitcast_fusion
  7.9 1.0 rev.4
  8.9 1.0 pad_maximum_fusion
  10.2 6.2 %gather_fusion = s32[1024]{0:T(1024)S(1)} fusion(s32[5120]{0:T(1024)S(1)} %copy-done, s32[1024]{0:T(1024)S(1)} %fusion.27), kind=kCustom, calls=%fused_computation | custom fusion | bytes 12288 | tf_op jit(solution)/shard_map/jit(_take)/gather | solution.py:398
  16.4 0.6 broadcast_in_dim.30.mine
  17.0 10.0 %places.1 = s32[8,128]{1,0:T(8,128)} custom-call(s32[8,8,128]{2,1,0:T(8,128)} %broadcast_in_dim.30.mine), custom_call_target="tpu_custom_call" | custom-call | tf_op jit(solution)/shard_map/places/pallas_call | solution.py:375
  27.1 0.8 compare_select_fusion.1
  27.9 1.1 gather_fusion.1
  29.3 0.6 pad_maximum_fusion.2.rot_ref
  29.9 0.7 fusion.32
  30.7 0.7 multiply_cosine_fusion
  31.4 0.7 pad_maximum_fusion.1.ph_ref
  32.0 0.2 fusion.12
  32.3 0.4 fusion.5
  32.6 1.8 negate_convert_fusion
  34.4 75.3 %all-gather.3.cloned.1.call-done.psi_ref = bf16[48,32,2304]{2,1,0:T(8,128)(2,1)} async-done(((bf16[6,32,2304]{2,1,0:T(8,128)(2,1)}), bf16[48,32,2304]{2,1,0:T(8,128)(2,1)}) %all-gather.3.cloned.1.call-update) | async-done | bytes 7077904 | tf_op jit(solution)/shard_map/all_gather | solution.py:394
  109.8 0.8 broadcast_in_dim.55.w_ref
  110.5 51.8 %planes.1 = (bf16[48,2,256,256]{3,2,1,0:T(8,128)(2,1)}, bf16[2,256,128]{2,1,0:T(8,128)(2,1)}) custom-call(bf16[48,32,2304]{2,1,0:T(8,128)(2,1)} %all-gather.3.cloned.1.call-done.psi_ref, bf16[1152,384]{1,0:T(8,128)(2,1)} %bitcast.21, bf16[1152,384]{1,0:T(8,128)(2,1)} %bitcast.20, f32[2,256]{1,0:T(2,128)} %pad_maximum_fusion.2.rot_ref, ...), custom_call_target="tpu_custom_call" | custom-call | tf_op jit(solution)/shard_map/planes/pallas_call | solution.py:88
  162.5 0.7 maximum_maximum_fusion.t_ref
  163.2 24.7 %lines.1 = bf16[96,256,256]{2,1,0:T(8,128)(2,1)} custom-call(f32[256]{0:T(256)} %copy-done.3, bf16[48,2,256,256]{3,2,1,0:T(8,128)(2,1)} %get-tuple-element.7.y_ref, bf16[96,96]{1,0:T(8,128)(2,1)} %maximum_maximum_fusion.t_ref), custom_call_target="tpu_custom_call" | custom-call | tf_op jit(solution)/shard_map/lines/pallas_call | solution.py:141
  187.9 19.3 %all-gather.5.cloned.1.call-done.s_ref = bf16[8,512,128]{2,1,0:T(8,128)(2,1)} async-done(((bf16[1,512,128]{2,1,0:T(8,128)(2,1)}), bf16[8,512,128]{2,1,0:T(8,128)(2,1)}) %all-gather.5.cloned.1.call-update) | async-done | bytes 1048592 | tf_op jit(solution)/shard_map/all_gather | solution.py:427
  207.2 54.2 %chi.1 = bf16[5120,1024]{1,0:T(8,128)(2,1)} custom-call(s32[5120]{0:T(1024)} %g_ref.1, bf16[2,48,256,256]{3,2,1,0:T(8,128)(2,1)} %bitcast.18, bf16[8,512,128]{2,1,0:T(8,128)(2,1)} %all-gather.5.cloned.1.call-done.s_ref), custom_call_target="tpu_custom_call" | custom-call | tf_op jit(solution)/shard_map/chi/pallas_call | solution.py:202
  261.3 52.6 %share.1 = f32[320,1024]{1,0:T(8,128)} custom-call(bf16[16,320,1024]{2,1,0:T(8,128)(2,1)} %bitcast.19), custom_call_target="tpu_custom_call" | custom-call | tf_op jit(solution)/shard_map/share/pallas_call | solution.py:330
  313.9 2.5 copy.10
  (34 shorter events, 1.0 us)
Async XLA Ops:
  6.5 103.2 %all-gather.3.cloned.1.call-start = ((), (), s32[]{:S(2)}) async-start(), calls=%async_computation | async-start | bytes 7962624 | tf_op jit(solution)/shard_map/all_gather | solution.py:394
  7.8 2.1 copy-start.4
  7.8 2.1 copy-start.5
  7.9 2.3 copy-start.2
  7.9 2.3 copy-start
  9.9 197.3 %all-gather.5.cloned.1.call-start = ((), (), s32[]{:S(2)}) async-start(), calls=%async_computation.1 | async-start | bytes 1179648 | tf_op jit(solution)/shard_map/all_gather | solution.py:427
  10.1 99.6 %copy-start.3 = (f32[256]{0:T(256)}, f32[256]{0:T(256)S(1)}, u32[]{:S(2)}) copy-start(f32[256]{0:T(256)S(1)} %mul.272.w_ref) | copy-start | bytes 3076
  10.2 16.8 %copy-start.1 = (s32[1536]{0:T(1024)S(1)}, s32[1536]{0:T(1024)}, u32[]{:S(2)}) copy-start(s32[1536]{0:T(1024)} %param.11) | copy-start | bytes 18436
Sparse Core Ops, SparseCore 0:
  10.0 99.6 all-gather.2
  162.4 44.7 all-gather.4

commit v3 on v2

--- a/solution.py
+++ b/solution.py
@@ -24,6 +24,7 @@
 XB = 4
 LANES = 256
 VMEM_LIMIT = 60 * 1024 * 1024
+MESH = pl.DeviceIdType.MESH
 
 
 def half_phase(ky, kz):
@@ -39,125 +40,267 @@
     return cos.astype(jnp.bfloat16), sin.astype(jnp.bfloat16)
 
 
-def planes_kernel(psi_ref, tc_ref, ts_ref, rot_ref, ph_ref, w_ref, y_ref, s_ref, pvf, ev, od, sacc):
-    step = pl.program_id(0)
-
-    @pl.when(step == 0)
-    def _():
-        sacc[...] = jnp.zeros_like(sacc)
-
-    for xi in range(XB):
-        pvf[xi] = psi_ref[xi, :NV, :].astype(jnp.float32)
-
-    for xi in range(XB):
-
-        def one(v, carry, xi=xi):
-            row = pvf[xi, pl.ds(v, 1), :]
-            d = jnp.broadcast_to(row, (CL, CELLS)).astype(jnp.bfloat16) * psi_ref[xi, NV:, :]
-            lo, hi = d[:, :HALF], d[:, HALF:]
-            at = pl.ds(pl.multiple_of(xi * PAIRS + v * CL, CL), CL)
-            ev[at, :] = lo + hi
-            od[at, :] = lo - hi
+BLOCKS = 8
+PX = NX // BLOCKS
+PT = 3
+PB = 16
+
+
+def density(vf, cbuf, b, plane, at, even, odd):
+    def one(v, carry):
+        out = pl.ds(pl.multiple_of(at * PAIRS + v * CL, CL), CL)
+        cond = cbuf.at[b, plane]
+        spread = lambda h: jnp.broadcast_to(vf[h, plane, pl.ds(v, 1), :], (CL, HALF)).astype(jnp.bfloat16)
+        lo = spread(0) * cond[:, :HALF]
+        hi = spread(1) * cond[:, HALF:]
+        even[out, :] = lo + hi
+        odd[out, :] = lo - hi
+        return carry
+
+    lax.fori_loop(0, NV, one, 0, unroll=4)
+
+
+def transform(b, first, even, odd, tc, ts, rot, ph, y, sacc):
+    a = jnp.dot(even[...], tc[...], preferred_element_type=jnp.float32)
+    c = jnp.dot(odd[...], ts[...], preferred_element_type=jnp.float32)
+    cosr, sinr = rot[0:1, :], rot[1:2, :]
+    real, imag = sacc[0], sacc[1]
+    for i in range(PT):
+        x = b * PX + first + i
+        rows = slice(i * PAIRS, i * PAIRS + PAIRS)
+        am, cm = a[rows, :LANES], c[rows, :LANES]
+        y[x, 0] = (cosr * am - sinr * cm).astype(jnp.bfloat16)
+        y[x, 1] = (cosr * cm + sinr * am).astype(jnp.bfloat16)
+        av, cv = a[rows, LANES:], c[rows, LANES:]
+        cp, sp = ph[x, 0:1, :], ph[x, 1:2, :]
+        real = real + (cp * av - sp * cv)
+        imag = imag + (cp * cv + sp * av)
+    sacc[0] = real
+    sacc[1] = imag
+
+
+def front_kernel(
+    weights, cond, val, tc, ts, rot, ph, wide, table, m_out, slab_out,
+    cbuf, vbuf, vf, even, odd, y, sacc, sl, yr, yi, mo, mb,
+    lsem, cs, cr, vs, vr, gs, gr, ss, sr, ms,
+):
+    row, col = lax.axis_index("row"), lax.axis_index("col")
+    yh, x = row // 4, row % 4
+    z, yl, core = col // 4, (col // 2) % 2, col % 2
+    zo = z + 1 - 2 * (z % 2)
+    xp = {"row": yh * 4 + (x + 1) % 4, "col": col}
+    xm = {"row": yh * 4 + (x + 3) % 4, "col": col}
+    yc = {"row": (1 - yh) * 4 + x, "col": col}
+    yv = {"row": (1 - yh) * 4 + x, "col": z * 4 + (1 - yl) * 2 + core}
+    group = [
+        {"row": row, "col": zo * 4 + yl * 2 + core},
+        {"row": row, "col": z * 4 + yl * 2 + 1 - core},
+        {"row": row, "col": zo * 4 + yl * 2 + 1 - core},
+    ]
+    across = [{"row": (row + k) % 8, "col": col} for k in range(1, 8)]
+    part = core * 2 + z % 2
+
+    own = [
+        pltpu.make_async_copy(cond, cbuf.at[0], lsem.at[0]),
+        pltpu.make_async_copy(val, vbuf.at[0], lsem.at[1]),
+    ]
+    for copy in own:
+        copy.start()
+    barrier = pltpu.get_barrier_semaphore()
+    for peer in across + group + [yv]:
+        pl.semaphore_signal(barrier, inc=1, device_id=peer, device_id_type=MESH)
+    pl.semaphore_wait(barrier, 11)
+
+    hops = [(0, 3, None), (0, 2, xp), (0, 1, xm), (3, 5, xp), (3, 4, xm), (2, 6, xp), (4, 7, xm)]
+
+    def relay(n):
+        src, dst, peer = hops[n]
+        c = pltpu.make_async_remote_copy(
+            cond if src == 0 else cbuf.at[src], cbuf.at[dst], cs.at[n], cr.at[dst],
+            device_id=peer or yc, device_id_type=MESH,
+        )
+        v = pltpu.make_async_remote_copy(
+            val.at[part] if src == 0 else vbuf.at[src, part], vbuf.at[dst, part], vs.at[n], vr.at[dst],
+            device_id=peer or yv, device_id_type=MESH,
+        )
+        return c, v
+
+    def go(n):
+        for copy in relay(n):
+            copy.start()
+
+    def incoming(dst):
+        return relay([hop[1] for hop in hops].index(dst))
+
+    def spread(b, j):
+        return pltpu.make_async_remote_copy(
+            vbuf.at[b, part], vbuf.at[b, part], gs.at[b * 3 + j], gr.at[b * 3 + j],
+            device_id=group[j], device_id_type=MESH,
+        )
+
+    def land(b, *forward):
+        c, v = incoming(b)
+        v.wait_recv()
+        for j in range(3):
+            spread(b, j).start()
+        c.wait_recv()
+        for n in forward:
+            go(n)
+
+    def ready(b):
+        for j in range(3):
+            spread(b, j).wait_recv()
+
+    for n in range(3):
+        go(n)
+    sacc[...] = jnp.zeros_like(sacc)
+    for copy in own:
+        copy.wait()
+
+    def block(b, carry):
+        @pl.when(b == 1)
+        def _():
+            land(2, 5)
+            land(1)
+            land(3, 3, 4)
+            ready(1)
+
+        @pl.when(b == 2)
+        def _():
+            ready(2)
+
+        @pl.when(b == 3)
+        def _():
+            land(4, 6)
+            ready(3)
+
+        @pl.when(b == 4)
+        def _():
+            land(5)
+            land(6)
+            ready(4)
+
+        @pl.when(b == 5)
+        def _():
+            ready(5)
+
+        @pl.when(b == 6)
+        def _():
+            land(7)
+            ready(6)
+
+        @pl.when(b == 7)
+        def _():
+            ready(7)
+
+        def widen(j, carry):
+            for q in range(4):
+                vf[q % 2, (q // 2) * 3 + j] = vbuf[b, q, j].astype(jnp.float32)
             return carry
 
-        lax.fori_loop(0, NV, one, 0, unroll=2)
-
-    cosr = rot_ref[0:1, :]
-    sinr = rot_ref[1:2, :]
-    for xi in range(XB):
-        rows = pl.ds(xi * PAIRS, PAIRS)
-        a = jnp.dot(ev[rows, :], tc_ref[...], preferred_element_type=jnp.float32)
-        b = jnp.dot(od[rows, :], ts_ref[...], preferred_element_type=jnp.float32)
-        am, bm = a[:, :LANES], b[:, :LANES]
-        y_ref[xi, 0] = (cosr * am - sinr * bm).astype(jnp.bfloat16)
-        y_ref[xi, 1] = (cosr * bm + sinr * am).astype(jnp.bfloat16)
-        asl, bsl = a[:, LANES:], b[:, LANES:]
-        cp = ph_ref[xi, 0:1, :]
-        sp = ph_ref[xi, 1:2, :]
-        sacc[0] += cp * asl - sp * bsl
-        sacc[1] += cp * bsl + sp * asl
-
-    @pl.when(step == pl.num_programs(0) - 1)
-    def _():
-        s_ref[0] = (sacc[0] * w_ref[...]).astype(jnp.bfloat16)
-        s_ref[1] = (sacc[1] * w_ref[...]).astype(jnp.bfloat16)
-
-
-def planes(psi, tc, ts, rot, ph, wide):
-    full = lambda *shape: pl.BlockSpec(shape, lambda i: (0,) * len(shape))
+        lax.fori_loop(0, 3, widen, 0)
+
+        def some(i, carry):
+            for u in range(PT):
+                density(vf, cbuf, b, i * PT + u, u, even, odd)
+            transform(b, i * PT, even, odd, tc, ts, rot, ph, y, sacc)
+            return carry
+
+        lax.fori_loop(0, PX // PT, some, 0)
+        return carry
+
+    lax.fori_loop(0, BLOCKS, block, 0)
+
+    for h in range(2):
+        sl[h * PAIRS : h * PAIRS + PAIRS, :] = (sacc[h] * wide[...]).astype(jnp.bfloat16)
+    keep = pltpu.make_async_copy(sl, slab_out.at[row], lsem.at[2])
+    keep.start()
+    pushes = []
+    for k in range(7):
+        pushes.append(
+            pltpu.make_async_remote_copy(
+                sl, slab_out.at[row], ss.at[k], sr.at[k], device_id=across[k], device_id_type=MESH
+            )
+        )
+        pushes[-1].start()
+
+    def chunk(i, carry):
+        slot = i % 2
+        ps = pl.ds(pl.multiple_of(i * PB, PB), PB)
+        out = pltpu.make_async_copy(mb.at[slot], m_out.at[:, ps, :], ms.at[slot])
+        for h in range(LANES // 128):
+            lanes = slice(h * 128, h * 128 + 128)
+            yr[h] = y[:, 0, ps, lanes].astype(jnp.float32).reshape(NX * PB, 128)
+            yi[h] = y[:, 1, ps, lanes].astype(jnp.float32).reshape(NX * PB, 128)
+        for p in range(PB):
+            at = pl.ds(p, NX, stride=PB)
+            real = jnp.concatenate([yr[0, at, :], yr[1, at, :]], axis=1)
+            imag = jnp.concatenate([yi[0, at, :], yi[1, at, :]], axis=1)
+            rhs = jnp.concatenate([real, imag], axis=0).astype(jnp.bfloat16)
+            res = jnp.dot(table[...], rhs, preferred_element_type=jnp.float32) * weights[i * PB + p]
+            for h in range(LANES // 128):
+                mo[h, pl.ds(p, 2 * NX, stride=PB), :] = res[:, h * 128 : h * 128 + 128]
+
+        @pl.when(i >= 2)
+        def _():
+            out.wait()
+
+        for h in range(LANES // 128):
+            lanes = slice(h * 128, h * 128 + 128)
+            mb[slot, :, :, lanes] = mo[h].reshape(2 * NX, PB, 128).astype(jnp.bfloat16)
+        out.start()
+        return carry
+
+    lax.fori_loop(0, PAIRS // PB, chunk, 0)
+    for slot in range(2):
+        pltpu.make_async_copy(mb.at[slot], m_out.at[:, pl.ds(slot * PB, PB), :], ms.at[slot]).wait()
+    keep.wait()
+    for push in pushes:
+        push.wait_recv()
+        push.wait_send()
+    for n in range(7):
+        for copy in relay(n):
+            copy.wait_send()
+    for b in range(1, BLOCKS):
+        for j in range(3):
+            spread(b, j).wait_send()
+
+
+def front(weights, cond, val, tc, ts, rot, ph, wide, table):
+    dma = pltpu.SemaphoreType.DMA
+    vmem = pl.BlockSpec(memory_space=pltpu.VMEM)
+    hbm = pl.BlockSpec(memory_space=pl.ANY)
+    bf = lambda *shape: pltpu.VMEM(shape, jnp.bfloat16)
+    fl = lambda *shape: pltpu.VMEM(shape, jnp.float32)
     return pl.pallas_call(
-        planes_kernel,
-        grid=(NX // XB,),
-        in_specs=[
-            pl.BlockSpec((XB, NV + CL, CELLS), lambda i: (i, 0, 0)),
-            full(HALF, LANES + JS),
-            full(HALF, LANES + JS),
-            full(2, LANES),
-            pl.BlockSpec((XB, 2, JS), lambda i: (i, 0, 0)),
-            full(PAIRS, JS),
-        ],
-        out_specs=[
-            pl.BlockSpec((XB, 2, PAIRS, LANES), lambda i: (i, 0, 0, 0)),
-            full(2, PAIRS, JS),
-        ],
+        front_kernel,
+        in_specs=[pl.BlockSpec(memory_space=pltpu.SMEM)] + [vmem] * 8,
+        out_specs=[hbm, hbm],
         out_shape=[
-            jax.ShapeDtypeStruct((NX, 2, PAIRS, LANES), jnp.bfloat16),
-            jax.ShapeDtypeStruct((2, PAIRS, JS), jnp.bfloat16),
+            jax.ShapeDtypeStruct((2 * NX, PAIRS, LANES), jnp.bfloat16),
+            jax.ShapeDtypeStruct((BLOCKS, 2 * PAIRS, JS), jnp.bfloat16),
         ],
         scratch_shapes=[
-            pltpu.VMEM((XB, NV, CELLS), jnp.float32),
-            pltpu.VMEM((XB * PAIRS, HALF), jnp.bfloat16),
-            pltpu.VMEM((XB * PAIRS, HALF), jnp.bfloat16),
-            pltpu.VMEM((2, PAIRS, JS), jnp.float32),
+            bf(BLOCKS, PX, CL, CELLS),
+            bf(BLOCKS, 4, PX // 2, NV, HALF),
+            fl(2, PX, NV, HALF),
+            bf(PT * PAIRS, HALF),
+            bf(PT * PAIRS, HALF),
+            bf(NX, 2, PAIRS, LANES),
+            fl(2, PAIRS, JS),
+            bf(2 * PAIRS, JS),
+            fl(2, NX * PB, 128),
+            fl(2, NX * PB, 128),
+            fl(2, 2 * NX * PB, 128),
+            bf(2, 2 * NX, PB, LANES),
+            dma((3,)), dma((7,)), dma((8,)), dma((7,)), dma((8,)),
+            dma((24,)), dma((24,)), dma((7,)), dma((7,)), dma((2,)),
         ],
-        compiler_params=pltpu.CompilerParams(vmem_limit_bytes=VMEM_LIMIT),
-        name="planes",
-    )(psi, tc, ts, rot, ph, wide)
-
-
-PB = 16
-
-
-def lines_kernel(w_ref, y_ref, t_ref, m_ref, yr, yi, mo):
-    base = pl.program_id(0) * PB
-    for h in range(LANES // 128):
-        lanes = slice(h * 128, h * 128 + 128)
-        yr[h] = y_ref[:, 0, :, lanes].astype(jnp.float32).reshape(NX * PB, 128)
-        yi[h] = y_ref[:, 1, :, lanes].astype(jnp.float32).reshape(NX * PB, 128)
-    for p in range(PB):
-        at = pl.ds(p, NX, stride=PB)
-        real = jnp.concatenate([yr[0, at, :], yr[1, at, :]], axis=1)
-        imag = jnp.concatenate([yi[0, at, :], yi[1, at, :]], axis=1)
-        rhs = jnp.concatenate([real, imag], axis=0).astype(jnp.bfloat16)
-        out = jnp.dot(t_ref[...], rhs, preferred_element_type=jnp.float32) * w_ref[base + p]
-        for h in range(LANES // 128):
-            mo[h, pl.ds(p, 2 * NX, stride=PB), :] = out[:, h * 128 : h * 128 + 128]
-    for h in range(LANES // 128):
-        lanes = slice(h * 128, h * 128 + 128)
-        m_ref[:, :, lanes] = mo[h].reshape(2 * NX, PB, 128).astype(jnp.bfloat16)
-
-
-def lines(weights, y, table):
-    return pl.pallas_call(
-        lines_kernel,
-        grid_spec=pltpu.PrefetchScalarGridSpec(
-            num_scalar_prefetch=1,
-            grid=(PAIRS // PB,),
-            in_specs=[
-                pl.BlockSpec((NX, 2, PB, LANES), lambda i, w: (0, 0, i, 0)),
-                pl.BlockSpec((2 * NX, 2 * NX), lambda i, w: (0, 0)),
-            ],
-            out_specs=pl.BlockSpec((2 * NX, PB, LANES), lambda i, w: (0, i, 0)),
-            scratch_shapes=[
-                pltpu.VMEM((2, NX * PB, 128), jnp.float32),
-                pltpu.VMEM((2, NX * PB, 128), jnp.float32),
-                pltpu.VMEM((2, 2 * NX * PB, 128), jnp.float32),
-            ],
+        compiler_params=pltpu.CompilerParams(
+            collective_id=2, has_side_effects=True, vmem_limit_bytes=VMEM_LIMIT
         ),
-        out_shape=jax.ShapeDtypeStruct((2 * NX, PAIRS, LANES), jnp.bfloat16),
-        compiler_params=pltpu.CompilerParams(vmem_limit_bytes=VMEM_LIMIT),
-        name="lines",
-    )(weights, y, table)
+        name="front",
+    )(weights, cond, val, tc, ts, rot, ph, wide, table)
 
 
 GB = 320
@@ -220,7 +363,6 @@
     )(gvec, m, s)
 
 
-MESH = pl.DeviceIdType.MESH
 G_DEV = 320
 HR = G_DEV // 2
 
@@ -389,9 +531,10 @@
 
 def body(psi_val, psi_cond, energy_val, energy_cond, stick_map, gvec_map, slab_index):
     row = lax.axis_index("row")
-    both = jnp.concatenate([psi_val, psi_cond], axis=0).transpose(1, 0, 2)
-    both = jnp.concatenate([both[:, :, :HALF], jnp.flip(both[:, :, HALF:], axis=2)], axis=2)
-    psi = lax.all_gather(both, "row", axis=0, tiled=True)
+    fold = lambda psi: (psi[:, :, :HALF], jnp.flip(psi[:, :, HALF:], axis=2))
+    cond = jnp.concatenate(fold(psi_cond.transpose(1, 0, 2)), axis=2)
+    val = jnp.stack([half.reshape(2, PX // 2, NV, HALF) for half in fold(psi_val.transpose(1, 0, 2))], axis=1)
+    val = val.reshape(4, PX // 2, NV, HALF)
 
     mine = lax.dynamic_slice(stick_map, (row * STK,), (STK,))
     cols = lax.dynamic_slice(slab_index, (row * JS,), (JS,))
@@ -406,7 +549,10 @@
     tc, ts = half_phase(ky, kz)
     turn = ((ky + kz) % 96).astype(jnp.float32) * (math.pi / 48.0)
     rot = jnp.stack([jnp.cos(turn[:LANES]), jnp.sin(turn[:LANES])])
-    xs = jnp.arange(NX, dtype=jnp.int32)
+    dy = jnp.array([0, 0, 0, 1, 1, 1, 0, 1], jnp.int32)
+    dx = jnp.array([0, 1, 3, 0, 1, 3, 2, 2], jnp.int32)
+    source = (row // 4 + dy) % 2 * 4 + (row % 4 + dx) % 4
+    xs = (source[:, None] * PX + jnp.arange(PX, dtype=jnp.int32)[None, :]).reshape(NX)
     theta = (
         ((ky + kz)[None, LANES:] - 2 * (xs[:, None] * col_kx[None, :]) + 96 * NX) % 96
     ).astype(jnp.float32) * (math.pi / 48.0)
@@ -417,15 +563,14 @@
     )
     weight = weight.reshape(PAIRS)
     wide = jnp.broadcast_to(weight[:, None], (PAIRS, JS))
-    ax = (xs[:, None] * xs[None, :] % NX).astype(jnp.float32) * (2.0 * math.pi / NX)
+    freq = jnp.arange(NX, dtype=jnp.int32)
+    ax = (freq[:, None] * xs[None, :] % NX).astype(jnp.float32) * (2.0 * math.pi / NX)
     cx, sx = jnp.cos(ax), jnp.sin(ax)
     table = jnp.concatenate(
         [jnp.concatenate([cx, sx], axis=1), jnp.concatenate([-sx, cx], axis=1)], axis=0
     ).astype(jnp.bfloat16)
 
-    y, s_part = planes(psi, tc, ts, rot, ph, wide)
-    slab = lax.all_gather(s_part.reshape(2 * PAIRS, JS), "row", axis=0, tiled=False)
-    m = lines(weight, y, table)
+    m, slab = front(weight, cond, val, tc, ts, rot, ph, wide, table)
     part = chi(gvec_map, m.reshape(2, NX, PAIRS, LANES), slab)
     return share(part.reshape(G_ROW // G_DEV, G_DEV, NS))
 

time: 325 us -> 241 us (0.74)
  waiting for transfers between devices: 94.6 us -> 0 us
  Pallas kernels: 193 us -> 216 us
  between operations: 13.6 us -> 0.22 us
    all_gather x2 -> x0, waiting for transfers between devices: 94.6 us -> none  [the longest x1 75.3 us: body(): psi = lax.all_gather(both, 'row', axis=0, tiled=True)]
    pallas_call x2 -> x1, Pallas kernels: 76.4 us -> 99.5 us  [front(): pl.pallas_call(front_kernel, in_specs=[pl.BlockSpec(memory_space=pltpu.SM...]
  transfers between devices with their start and end apart: 2 -> 0, of which waited for: 2 -> 0; matrix products, arithmetic and copies ran while one was open for 5% -> 0% of each run, Pallas kernels for 11% -> 0%
where the time goes in v3:
time: 241 us; the launch traced here: 240 us
  Pallas kernels  216 us (90%)
  local copies, waits for them, and re-layouts  14.1 us (6%)
  other arithmetic  10.1 us (4%)
    pallas_call x1, Pallas kernels, front(): pl.pallas_call(front_kernel, in_specs=[pl.BlockSpec(memory_space=pltpu.SM...  99.5 us
    pallas_call x1, Pallas kernels, chi(): pl.pallas_call(chi_kernel, grid_spec=pltpu.PrefetchScalarGridSpec(num_sca...  54.2 us
    pallas_call x1, Pallas kernels, share(): pl.pallas_call(share_kernel, in_specs=[pl.BlockSpec(memory_space=pl.ANY)]...  52.3 us
    pallas_call x1, Pallas kernels, places(): pl.pallas_call(places_kernel, in_specs=[pl.BlockSpec(memory_space=pltpu.V...  10 us
    gather x1, local copies, waits for them, and re-layouts, body(): jnp.take(gvec_map, slab_index % G_ROW)  6.15 us

profile of v3, /device:TPU:1, one launch (start us, length us, event | category | flops | bytes accessed | tf_op | source)
XLA Modules:
  0.0 240.3 jit_solution(5280976969277160299)
XLA Ops:
  0.0 0.7 fusion.36
  0.7 0.8 dynamic_slice.6
  1.6 0.7 fusion.27
  2.4 6.2 %gather_fusion = s32[1024]{0:T(1024)S(1)} fusion(s32[5120]{0:T(1024)S(1)} %copy-done, s32[1024]{0:T(1024)S(1)} %fusion.27), kind=kCustom, calls=%fused_computation | custom fusion | bytes 12288 | tf_op jit(solution)/shard_map/jit(_take)/gather | solution.py:541
  8.8 0.6 broadcast_in_dim.30.mine
  9.4 10.0 %places.1 = s32[8,128]{1,0:T(8,128)} custom-call(s32[8,8,128]{2,1,0:T(8,128)} %broadcast_in_dim.30.mine), custom_call_target="tpu_custom_call" | custom-call | tf_op jit(solution)/shard_map/places/pallas_call | solution.py:517
  19.4 0.8 compare_select_fusion.1
  20.2 0.7 fusion.37
  20.9 1.1 gather_fusion.1
  22.3 0.6 pad_maximum_fusion.3.rot
  23.0 0.7 multiply_cosine_fusion
  23.7 0.7 pad_maximum_fusion.2.ph
  24.5 0.7 maximum_maximum_fusion.table
  25.4 0.8 broadcast_in_dim.55.wide
  26.2 0.4 fusion.5
  26.6 0.9 rev.8
  27.5 0.8 pad_maximum_fusion.1
  28.4 0.9 rev.7
  29.3 0.8 pad_maximum_fusion.cond
  30.1 1.8 negate_convert_fusion
  31.8 99.5 %front.1 = (bf16[96,256,256]{2,1,0:T(8,128)(2,1)}, bf16[8,512,128]{2,1,0:T(8,128)(2,1)}) custom-call(f32[256]{0:T(256)} %copy-done.5, bf16[6,16,2304]{2,1,0:T(8,128)(2,1)} %pad_maximum_fusion.cond, bf16[4,3,16,1152]{3,2,1,0:T(8,128)(2,1)} %bitcast.28, bf16[1152,384]{1,0:T(8,128)(2,1)} %bitcast.27, bf16[1152,384]{1,0:T(8,128)(2,1)} %bitcast.26, ...), custom_call_target="tpu_custom_call" | custom-call | tf_op jit(solution)/shard_map/front/pallas_call | solution.py:275
  131.3 54.2 %chi.1 = bf16[5120,1024]{1,0:T(8,128)(2,1)} custom-call(s32[5120]{0:T(1024)} %g_ref.1, bf16[2,48,256,256]{3,2,1,0:T(8,128)(2,1)} %bitcast.25, bf16[8,512,128]{2,1,0:T(8,128)(2,1)} %get-tuple-element.8.s_ref), custom_call_target="tpu_custom_call" | custom-call | tf_op jit(solution)/shard_map/chi/pallas_call | solution.py:345
  185.5 52.3 %share.1 = f32[320,1024]{1,0:T(8,128)} custom-call(bf16[16,320,1024]{2,1,0:T(8,128)(2,1)} %bitcast.24), custom_call_target="tpu_custom_call" | custom-call | tf_op jit(solution)/shard_map/share/pallas_call | solution.py:472
  237.8 2.5 %copy.18 = f32[320,1024]{1,0:T(8,128)} copy(f32[320,1024]{1,0:T(8,128)} %share.1) | data formatting | bytes 2621440
  (35 shorter events, 1.2 us)
Async XLA Ops:
  0.0 2.3 copy-start
  2.3 6.2 %copy-start.4 = (s32[1024]{0:T(1024)S(1)}, s32[1024]{0:T(1024)}, u32[]{:S(2)}) copy-start(s32[1024]{0:T(1024)} %param.15) | copy-start | bytes 12292
  2.4 6.2 %copy-start.6 = (f32[16]{0:T(128)S(1)}, f32[16]{0:T(128)}, u32[]{:S(2)}) copy-start(f32[16]{0:T(128)} %param.11) | copy-start | bytes 196
  2.4 6.2 %copy-start.7 = (f32[16]{0:T(128)S(1)}, f32[16]{0:T(128)}, u32[]{:S(2)}) copy-start(f32[16]{0:T(128)} %param.12) | copy-start | bytes 196
  2.4 18.5 %copy-start.1 = (s32[1536]{0:T(1024)S(1)}, s32[1536]{0:T(1024)}, u32[]{:S(2)}) copy-start(s32[1536]{0:T(1024)} %param.13) | copy-start | bytes 18436
  2.4 24.2 %copy-start.2 = (bf16[16,6,2304]{2,0,1:T(8,128)(2,1)S(1)}, bf16[16,6,2304]{2,0,1:T(8,128)(2,1)}, u32[]{:S(2)}) copy-start(bf16[16,6,2304]{2,0,1:T(8,128)(2,1)} %param.9) | copy-start | bytes 1327108
  8.8 19.6 %copy-start.5 = (f32[256]{0:T(256)}, f32[256]{0:T(256)S(1)}, u32[]{:S(2)}) copy-start(f32[256]{0:T(256)S(1)} %mul.255.weights) | copy-start | bytes 3076
  8.8 19.6 %copy-start.3 = (bf16[16,6,2304]{2,0,1:T(8,128)(2,1)S(1)}, bf16[16,6,2304]{2,0,1:T(8,128)(2,1)}, u32[]{:S(2)}) copy-start(bf16[16,6,2304]{2,0,1:T(8,128)(2,1)} %param.10) | copy-start | bytes 1327108

commit v4 on v3

--- a/solution.py
+++ b/solution.py
@@ -1,4 +1,3 @@
-import functools
 import math
 
 import jax
@@ -305,79 +304,92 @@
 
 GB = 320
 QS = 2 * PAIRS // 128
-
-
-def chi_kernel(g_ref, m_ref, s_ref, o_ref, mt, sel):
-    step = pl.program_id(0)
-
-    @pl.when(step < NX)
-    def _():
+G_DEV = 320
+HR = G_DEV // 2
+DEPTH = 4
+UNROLL = 16
+
+
+def pick_kernel(g_ref, m, out, mt, mi, sel, lhs, ms, os):
+    def fetch(step):
+        slot = step % DEPTH
+        return pltpu.make_async_copy(m.at[:, step], mi.at[slot], ms.at[slot])
+
+    for step in range(DEPTH):
+        fetch(step).start()
+
+    def turn(step, carry):
+        fetch(step).wait()
         for h in range(2):
             for q in range(2):
-                a = m_ref[h, 0, q * 128 : q * 128 + 128, :].astype(jnp.float32)
-                t = a.T
-                at = pl.ds(step * (STK * QS) + h * 2 + q, STK, stride=QS)
-                mt[at, :] = t[:STK, :]
-
-    @pl.when(step >= NX)
-    def _():
-        base = (step - NX) * GB
-
-        def pick(i, carry):
-            for u in range(8):
-                g = g_ref[base + i * 8 + u]
-                sel[pl.ds(pl.multiple_of(i * 32 + u * QS, QS), QS), :] = mt[
-                    pl.ds(pl.multiple_of(g * QS, QS), QS), :
-                ]
+                t = mi[step % DEPTH, h, q * 128 : q * 128 + 128, :].T.astype(jnp.float32)
+                mt[pl.ds(step * (STK * QS) + h * 2 + q, STK, stride=QS), :] = t[:STK, :]
+
+        @pl.when(step < NX - DEPTH)
+        def _():
+            fetch(step + DEPTH).start()
+
+        return carry
+
+    lax.fori_loop(0, NX, turn, 0)
+    store = lambda n: pltpu.make_async_copy(lhs.at[n % 2], out.at[n], os.at[n % 2])
+
+    def block(n, carry):
+        def rows(i, carry):
+            for u in range(UNROLL):
+                g = g_ref[n * GB + i * UNROLL + u]
+                to = pl.ds(pl.multiple_of((i * UNROLL + u) * QS, QS), QS)
+                sel[to, :] = mt[pl.ds(pl.multiple_of(g * QS, QS), QS), :]
             return carry
 
-        lax.fori_loop(0, GB // 8, pick, 0)
-        lhs = jnp.concatenate(
-            [sel[pl.ds(q, GB, stride=QS), :].astype(jnp.bfloat16) for q in range(QS)], axis=1
-        )
-        scale = -1.0 / math.sqrt(NV * NC)
-        for r in range(NS // JS):
-            out = jnp.dot(lhs, s_ref[r], preferred_element_type=jnp.float32)
-            o_ref[:, r * JS : r * JS + JS] = (out * scale).astype(jnp.bfloat16)
-
-
-def chi(gvec, m, s):
+        lax.fori_loop(0, GB // UNROLL, rows, 0)
+
+        @pl.when(n >= 2)
+        def _():
+            store(n - 2).wait()
+
+        for k in range(QS):
+            lhs[n % 2, :, k * 128 : k * 128 + 128] = sel[pl.ds(k, GB, stride=QS), :].astype(jnp.bfloat16)
+        store(n).start()
+        return carry
+
+    lax.fori_loop(0, G_ROW // GB, block, 0)
+    for n in range(2):
+        store(G_ROW // GB - 2 + n).wait()
+
+
+def pick(gvec, m):
+    dma = pltpu.SemaphoreType.DMA
     return pl.pallas_call(
-        chi_kernel,
-        grid_spec=pltpu.PrefetchScalarGridSpec(
-            num_scalar_prefetch=1,
-            grid=(NX + G_ROW // GB,),
-            in_specs=[
-                pl.BlockSpec((2, 1, PAIRS, LANES), lambda i, g: (0, jnp.minimum(i, NX - 1), 0, 0)),
-                pl.BlockSpec((NS // JS, 2 * PAIRS, JS), lambda i, g: (0, 0, 0)),
-            ],
-            out_specs=pl.BlockSpec((GB, NS), lambda i, g: (jnp.maximum(i - NX, 0), 0)),
-            scratch_shapes=[
-                pltpu.VMEM((NX * STK * QS, 128), jnp.float32),
-                pltpu.VMEM((GB * QS, 128), jnp.float32),
-            ],
-        ),
-        out_shape=jax.ShapeDtypeStruct((G_ROW, NS), jnp.bfloat16),
+        pick_kernel,
+        in_specs=[pl.BlockSpec(memory_space=pltpu.SMEM), pl.BlockSpec(memory_space=pl.ANY)],
+        out_specs=pl.BlockSpec(memory_space=pl.ANY),
+        out_shape=jax.ShapeDtypeStruct((G_ROW // GB, GB, 2 * PAIRS), jnp.bfloat16),
+        scratch_shapes=[
+            pltpu.VMEM((NX * STK * QS, 128), jnp.float32),
+            pltpu.VMEM((DEPTH, 2, PAIRS, LANES), jnp.bfloat16),
+            pltpu.VMEM((GB * QS, 128), jnp.float32),
+            pltpu.VMEM((2, GB, 2 * PAIRS), jnp.bfloat16),
+            dma((DEPTH,)), dma((2,)),
+        ],
         compiler_params=pltpu.CompilerParams(vmem_limit_bytes=VMEM_LIMIT),
-        name="chi",
-    )(gvec, m, s)
-
-
-G_DEV = 320
-HR = G_DEV // 2
-
-
-def add_rows(dst, dst_at, a, b, rows, step=32):
+        name="pick",
+    )(gvec, m)
+
+
+def add_rows(dst, a, b, rows, step=32):
     def one(i, carry):
-        at = pl.ds(pl.multiple_of(dst_at + i * step, 16), step)
-        src = pl.ds(pl.multiple_of(b[1] + i * step, 16), step)
-        dst[at, :] = (a[at, :].astype(jnp.float32) + b[0][src, :].astype(jnp.float32)).astype(dst.dtype)
+        at = pl.ds(pl.multiple_of(i * step, step), step)
+        dst[at, :] = (a[at, :].astype(jnp.float32) + b[at, :].astype(jnp.float32)).astype(dst.dtype)
         return carry
 
     lax.fori_loop(0, rows // step, one, 0)
 
 
-def share_kernel(part, out, acc, r1, zr2, yr1, zr1, yr2, lsem, s1, d1, sz2, dz2, sy1, dy1, sz1, dz1, sy2, dy2):
+def back_kernel(
+    rows, slab, out, sw, lhs, tx, acc, r1, zr2, yr1, zr1, yr2,
+    ms, s1, d1, sz2, dz2, sy1, dy1, sz1, dz1, sy2, dy2,
+):
     row, col = lax.axis_index("row"), lax.axis_index("col")
     z, yl, core = col // 4, (col // 2) % 2, col % 2
     core_peer = {"row": row, "col": z * 4 + yl * 2 + (1 - core)}
@@ -386,129 +398,171 @@
     barrier = pltpu.get_barrier_semaphore()
     for peer in (core_peer, y_peer, z_peer(1), z_peer(2), z_peer(3)):
         pl.semaphore_signal(barrier, inc=1, device_id=peer, device_id_type=MESH)
+
+    for r in range(NS // JS):
+        sw[:, r * JS : r * JS + JS] = slab[r]
+
     pl.semaphore_wait(barrier, 5)
 
-    order = [(k, s) for k in (2, 1, 3, 0) for s in (0, 1)]
-    first, local = {}, {}
-    for k, s in order:
-        slot = k * 2 + s
-        q = ((z + k) % 4) * 4 + (yl if s else 1 - yl) * 2
-        first[slot] = pltpu.make_async_remote_copy(
-            part.at[q + 1 - core], r1.at[slot], s1.at[slot], d1.at[slot], device_id=core_peer, device_id_type=MESH
-        )
-        first[slot].start()
-        local[slot] = pltpu.make_async_copy(part.at[q + core], acc.at[slot], lsem.at[slot])
-        local[slot].start()
-    sends = []
-
-    def send(src, dst, ss, ds, peer):
-        copy = pltpu.make_async_remote_copy(src, dst, ss, ds, device_id=peer, device_id_type=MESH)
-        copy.start()
-        sends.append(copy)
-        return copy
+    scale = -1.0 / math.sqrt(NV * NC)
+    load = lambda q, own: pltpu.make_async_copy(rows.at[q], lhs.at[own], ms.at[own])
+
+    def product(own, dst):
+        value = jnp.dot(lhs[own], sw[...], preferred_element_type=jnp.float32)
+        dst[...] = (value * scale).astype(jnp.bfloat16)
+
+    def remote(src, dst, ss, ds, peer):
+        return pltpu.make_async_remote_copy(src, dst, ss, ds, device_id=peer, device_id_type=MESH)
 
     lo, hi = pl.ds(0, HR), pl.ds(HR, HR)
-    along_y, along_z = {}, {}
-    for k, s in order:
-        slot = k * 2 + s
-        local[slot].wait()
-        first[slot].wait_recv()
-        add_rows(acc.at[slot], 0, acc.at[slot], (r1.at[slot], 0), G_DEV)
+    first = lambda n: remote(tx.at[n], r1.at[n], s1.at[n], d1.at[n], core_peer)
+    along_z = lambda k, s: remote(
+        acc.at[(k + 3) % 4 * 2 + s, hi], zr2.at[(k - 1) * 2 + s], sz2.at[(k - 1) * 2 + s], dz2.at[(k - 1) * 2 + s], z_peer(k)
+    )
+    along_y = lambda k: remote(acc.at[(k + 3) % 4 * 2, lo], yr1.at[k], sy1.at[k], dy1.at[k], y_peer)
+    last_z = lambda k: remote(acc.at[(k + 3) % 4 * 2 + 1, lo], zr1.at[k - 1], sz1.at[k - 1], dz1.at[k - 1], z_peer(k))
+
+    def settle(n):
+        k, s = (n // 2 + 1) % 4, n % 2
+        first(n).wait_recv()
+        add_rows(acc.at[n], acc.at[n], r1.at[n], G_DEV)
+
+        @pl.when(n < 6)
+        def _():
+            along_z(k, s).start()
+
+        @pl.when(s == 0)
+        def _():
+            along_y(k).start()
+
+    def place(n):
+        k, s = (n // 2 + 1) % 4, n % 2
+        return ((z + k) % 4) * 4 + (yl * s + (1 - yl) * (1 - s)) * 2
+
+    def slot(n, carry):
+        load(place(n) + 1 - core, 0).wait()
+        product(0, tx.at[n])
+        first(n).start()
+
+        @pl.when(n < 7)
+        def _():
+            load(place(n + 1) + 1 - core, 0).start()
+
+        load(place(n) + core, 1).wait()
+        product(1, acc.at[n])
+
+        @pl.when(n < 7)
+        def _():
+            load(place(n + 1) + core, 1).start()
+
+        @pl.when(n > 0)
+        def _():
+            settle(n - 1)
+
+        return carry
+
+    load(place(0) + 1 - core, 0).start()
+    load(place(0) + core, 1).start()
+    lax.fori_loop(0, 8, slot, 0)
+    settle(7)
+    for k in (1, 2, 3, 0):
+        along_y(k).wait_recv()
         if k:
-            i = (k - 1) * 2 + s
-            along_z[k, s] = send(acc.at[slot, hi], zr2.at[i], sz2.at[i], dz2.at[i], z_peer(k))
-        if s == 0:
-            along_y[k] = send(acc.at[slot, lo], yr1.at[k], sy1.at[k], dy1.at[k], y_peer)
-    last_z = {}
-    for k in (2, 1, 3, 0):
-        along_y[k].wait_recv()
-        if k:
-            slot = k * 2 + 1
-            add_rows(acc.at[slot], 0, acc.at[slot], (yr1.at[k], 0), HR)
-            last_z[k] = send(acc.at[slot, lo], zr1.at[k - 1], sz1.at[k - 1], dz1.at[k - 1], z_peer(k))
-    for k in (1, 3, 2):
-        along_z[k, 0].wait_recv()
+            at = acc.at[(k + 3) % 4 * 2 + 1]
+            add_rows(at, at, yr1.at[k], HR)
+            last_z(k).start()
+    for k in (1, 2, 3):
+        along_z(k, 0).wait_recv()
 
     def total(i, base, terms):
         at = pl.ds(pl.multiple_of(i * 16, 16), 16)
-        value = base[pl.ds(pl.multiple_of(i * 16, 16), 16), :].astype(jnp.float32)
+        value = base[at, :].astype(jnp.float32)
         for ref in terms:
             value = value + ref[at, :].astype(jnp.float32)
         return at, value
 
-    def turn(i, carry):
-        at, value = total(i, acc.at[0, hi], [zr2.at[0], zr2.at[2], zr2.at[4]])
+    def across(i, carry):
+        at, value = total(i, acc.at[6, hi], [zr2.at[0], zr2.at[2], zr2.at[4]])
         yr2[0, at, :] = value.astype(jnp.bfloat16)
         return carry
 
-    lax.fori_loop(0, HR // 16, turn, 0)
-    last_y = send(yr2.at[0], yr2.at[1], sy2.at[0], dy2.at[0], y_peer)
-    for k in (1, 3, 2):
-        last_z[k].wait_recv()
+    lax.fori_loop(0, HR // 16, across, 0)
+    last_y = remote(yr2.at[0], yr2.at[1], sy2.at[0], dy2.at[0], y_peer)
+    last_y.start()
+    for k in (1, 2, 3):
+        last_z(k).wait_recv()
 
     def low(i, carry):
-        at, value = total(i, acc.at[1, lo], [yr1.at[0], zr1.at[0], zr1.at[1], zr1.at[2]])
+        at, value = total(i, acc.at[7, lo], [yr1.at[0], zr1.at[0], zr1.at[1], zr1.at[2]])
         out[at, :] = value
         return carry
 
     lax.fori_loop(0, HR // 16, low, 0)
-    for k in (1, 3, 2):
-        along_z[k, 1].wait_recv()
+    for k in (1, 2, 3):
+        along_z(k, 1).wait_recv()
     last_y.wait_recv()
 
     def high(i, carry):
-        at, value = total(i, acc.at[1, hi], [zr2.at[1], zr2.at[3], zr2.at[5], yr2.at[1]])
+        at, value = total(i, acc.at[7, hi], [zr2.at[1], zr2.at[3], zr2.at[5], yr2.at[1]])
         out[pl.ds(pl.multiple_of(HR + i * 16, 16), 16), :] = value
         return carry
 
     lax.fori_loop(0, HR // 16, high, 0)
-    for copy in list(first.values()) + sends:
-        copy.wait_send()
-
-
-def share(part):
+    for n in range(8):
+        first(n).wait_send()
+    for k in range(4):
+        along_y(k).wait_send()
+        if k:
+            last_z(k).wait_send()
+            along_z(k, 0).wait_send()
+            along_z(k, 1).wait_send()
+    last_y.wait_send()
+
+
+def back(rows, slab):
     dma = pltpu.SemaphoreType.DMA
+    vmem = pl.BlockSpec(memory_space=pltpu.VMEM)
     half = lambda n: pltpu.VMEM((n, HR, NS), jnp.bfloat16)
     return pl.pallas_call(
-        share_kernel,
-        in_specs=[pl.BlockSpec(memory_space=pl.ANY)],
-        out_specs=pl.BlockSpec(memory_space=pltpu.VMEM),
+        back_kernel,
+        in_specs=[pl.BlockSpec(memory_space=pl.ANY), vmem],
+        out_specs=vmem,
         out_shape=jax.ShapeDtypeStruct((G_DEV, NS), jnp.float32),
         scratch_shapes=[
+            pltpu.VMEM((2 * PAIRS, NS), jnp.bfloat16),
+            pltpu.VMEM((2, GB, 2 * PAIRS), jnp.bfloat16),
+            pltpu.VMEM((8, G_DEV, NS), jnp.bfloat16),
             pltpu.VMEM((8, G_DEV, NS), jnp.bfloat16),
             pltpu.VMEM((8, G_DEV, NS), jnp.bfloat16),
             half(6), half(4), half(3), half(2),
-            dma((8,)), dma((8,)), dma((8,)), dma((6,)), dma((6,)), dma((4,)), dma((4,)),
+            dma((2,)), dma((8,)), dma((8,)), dma((6,)), dma((6,)), dma((4,)), dma((4,)),
             dma((3,)), dma((3,)), dma((1,)), dma((1,)),
         ],
         compiler_params=pltpu.CompilerParams(
             collective_id=3, has_side_effects=True, vmem_limit_bytes=VMEM_LIMIT
         ),
-        name="share",
-    )(part)
-
-
-def places_kernel(mine, out, got, send_sem, recv_sem):
+        name="back",
+    )(rows, slab)
+
+
+def places_kernel(mine, out, send_sem, recv_sem):
     row, col = lax.axis_index("row"), lax.axis_index("col")
     barrier = pltpu.get_barrier_semaphore()
-    for k in range(1, 8):
-        pl.semaphore_signal(barrier, inc=1, device_id={"row": (row + k) % 8, "col": col}, device_id_type=MESH)
+    peers = [{"row": (row + k) % 8, "col": col} for k in range(1, 8)]
+    for peer in peers:
+        pl.semaphore_signal(barrier, inc=1, device_id=peer, device_id_type=MESH)
     pl.semaphore_wait(barrier, 7)
     copies = []
-    for k in range(1, 8):
-        to = (row + k) % 8
+    for k, peer in enumerate(peers):
         copies.append(
             pltpu.make_async_remote_copy(
-                mine.at[to], got.at[k - 1], send_sem.at[k - 1], recv_sem.at[k - 1],
-                device_id={"row": to, "col": col}, device_id_type=MESH,
+                mine, out.at[row], send_sem.at[k], recv_sem.at[k], device_id=peer, device_id_type=MESH
             )
         )
         copies[-1].start()
-    total = mine[row]
-    for k in range(1, 8):
-        copies[k - 1].wait_recv()
-        total = total + got[k - 1]
-    out[...] = total
+    out[row] = mine[...]
+    for copy in copies:
+        copy.wait_recv()
     for copy in copies:
         copy.wait_send()
 
@@ -518,12 +572,8 @@
         places_kernel,
         in_specs=[pl.BlockSpec(memory_space=pltpu.VMEM)],
         out_specs=pl.BlockSpec(memory_space=pltpu.VMEM),
-        out_shape=jax.ShapeDtypeStruct((8, JS), jnp.int32),
-        scratch_shapes=[
-            pltpu.VMEM((7, 8, JS), jnp.int32),
-            pltpu.SemaphoreType.DMA((7,)),
-            pltpu.SemaphoreType.DMA((7,)),
-        ],
+        out_shape=jax.ShapeDtypeStruct((8, G_ROW // 128, 128), jnp.int32),
+        scratch_shapes=[pltpu.SemaphoreType.DMA((7,)), pltpu.SemaphoreType.DMA((7,))],
         compiler_params=pltpu.CompilerParams(collective_id=1, has_side_effects=True),
         name="places",
     )(mine)
@@ -538,9 +588,8 @@
 
     mine = lax.dynamic_slice(stick_map, (row * STK,), (STK,))
     cols = lax.dynamic_slice(slab_index, (row * JS,), (JS,))
-    held = jnp.where(slab_index // G_ROW == row, jnp.take(gvec_map, slab_index % G_ROW), 0)
-    held = jnp.broadcast_to(held.reshape(NS // JS, 1, JS), (NS // JS, 8, JS))
-    place = places(held)[0]
+    maps = places(gvec_map.reshape(G_ROW // 128, 128)).reshape(-1)
+    place = jnp.take(maps, cols)
     col_kx = place // STK
     col_stick = jnp.take(stick_map, cols // G_ROW * STK + place % STK)
     pad = jnp.zeros((LANES - STK,), jnp.int32)
@@ -571,8 +620,7 @@
     ).astype(jnp.bfloat16)
 
     m, slab = front(weight, cond, val, tc, ts, rot, ph, wide, table)
-    part = chi(gvec_map, m.reshape(2, NX, PAIRS, LANES), slab)
-    return share(part.reshape(G_ROW // G_DEV, G_DEV, NS))
+    return back(pick(gvec_map, m.reshape(2, NX, PAIRS, LANES)), slab)
 
 
 def solution(mesh):

time: 241 us -> 211 us (0.88)
  Pallas kernels: 216 us -> 190 us
  local copies, waits for them, and re-layouts: 14.1 us -> 9.61 us
    pallas_call x2, Pallas kernels: 106 us -> 79.7 us  [the longest x1 56.9 us: back(): pl.pallas_call(back_kernel, in_specs=[pl.BlockSpec(memory_space=pl.ANY),...]
    gather x1, local copies, waits for them, and re-layouts: 6.15 us -> 1.9 us  [body(): place = jnp.take(maps, cols)]
where the time goes in v4:
time: 211 us; the launch traced here: 210 us
  Pallas kernels  190 us (90%)
  other arithmetic  10.2 us (5%)
  local copies, waits for them, and re-layouts  9.61 us (5%)
    pallas_call x1, Pallas kernels, front(): pl.pallas_call(front_kernel, in_specs=[pl.BlockSpec(memory_space=pltpu.SM...  99.5 us
    pallas_call x1, Pallas kernels, back(): pl.pallas_call(back_kernel, in_specs=[pl.BlockSpec(memory_space=pl.ANY),...  56.9 us
    pallas_call x1, Pallas kernels, pick(): pl.pallas_call(pick_kernel, in_specs=[pl.BlockSpec(memory_space=pltpu.SME...  22.8 us
    pallas_call x1, Pallas kernels, places(): pl.pallas_call(places_kernel, in_specs=[pl.BlockSpec(memory_space=pltpu.V...  10.8 us

profile of v4, /device:TPU:1, one launch (start us, length us, event | category | flops | bytes accessed | tf_op | source)
XLA Modules:
  0.0 209.8 jit_solution(6906553134950412404)
XLA Ops:
  0.0 0.7 fusion.33
  0.7 0.8 dynamic_slice.6
  1.5 0.8 compare_select_fusion.1
  2.4 0.8 sqrt_multiply_fusion
  3.4 0.7 maximum_maximum_fusion.table
  4.1 0.7 broadcast_in_dim.22.wide
  4.8 10.8 %places.1 = s32[8,40,128]{2,1,0:T(8,128)} custom-call(s32[40,128]{1,0:T(8,128)} %bitcast.27), custom_call_target="tpu_custom_call" | custom-call | tf_op jit(solution)/shard_map/places/pallas_call | solution.py:571
  15.6 1.9 gather_fusion
  17.5 0.8 and_select_fusion
  18.3 1.6 gather_fusion.1
  20.2 0.6 pad_maximum_fusion.3.rot
  20.9 0.7 multiply_cosine_fusion
  21.6 0.7 pad_maximum_fusion.2.ph
  22.3 0.2 fusion.12
  22.5 0.4 fusion.5
  22.9 0.9 rev.8
  23.8 0.8 pad_maximum_fusion.1
  24.7 0.9 rev.7
  25.6 0.8 pad_maximum_fusion.cond
  26.3 1.8 negate_convert_fusion
  28.1 99.5 %front.1 = (bf16[96,256,256]{2,1,0:T(8,128)(2,1)}, bf16[8,512,128]{2,1,0:T(8,128)(2,1)}) custom-call(f32[256]{0:T(256)} %copy-done.2, bf16[6,16,2304]{2,1,0:T(8,128)(2,1)} %pad_maximum_fusion.cond, bf16[4,3,16,1152]{3,2,1,0:T(8,128)(2,1)} %bitcast.21, bf16[1152,384]{1,0:T(8,128)(2,1)} %bitcast.19, bf16[1152,384]{1,0:T(8,128)(2,1)} %bitcast.18, ...), custom_call_target="tpu_custom_call" | custom-call | tf_op jit(solution)/shard_map/front/pallas_call | solution.py:274
  127.6 22.8 %pick.1.rows = bf16[16,320,512]{2,1,0:T(8,128)(2,1)} custom-call(s32[5120]{0:T(1024)} %g_ref.1, bf16[2,48,256,256]{3,2,1,0:T(8,128)(2,1)} %bitcast.17), custom_call_target="tpu_custom_call" | custom-call | tf_op jit(solution)/shard_map/pick/pallas_call | solution.py:363
  150.4 56.9 %back.1 = f32[320,1024]{1,0:T(8,128)} custom-call(bf16[16,320,512]{2,1,0:T(8,128)(2,1)} %pick.1.rows, bf16[8,512,128]{2,1,0:T(8,128)(2,1)} %get-tuple-element.8.slab), custom_call_target="tpu_custom_call" | custom-call | tf_op jit(solution)/shard_map/back/pallas_call | solution.py:526
  207.3 2.5 %copy.18 = f32[320,1024]{1,0:T(8,128)} copy(f32[320,1024]{1,0:T(8,128)} %back.1) | data formatting | bytes 2621440
  (23 shorter events, 0.8 us)
Async XLA Ops:
  0.0 22.9 %copy-start = (bf16[16,6,2304]{2,0,1:T(8,128)(2,1)S(1)}, bf16[16,6,2304]{2,0,1:T(8,128)(2,1)}, u32[]{:S(2)}) copy-start(bf16[16,6,2304]{2,0,1:T(8,128)(2,1)} %param.9) | copy-start | bytes 1327108
  3.3 21.3 %copy-start.2 = (f32[256]{0:T(256)}, f32[256]{0:T(256)S(1)}, u32[]{:S(2)}) copy-start(f32[256]{0:T(256)S(1)} %mul.253.weights) | copy-start | bytes 3076
  15.6 9.0 %copy-start.1 = (bf16[16,6,2304]{2,0,1:T(8,128)(2,1)S(1)}, bf16[16,6,2304]{2,0,1:T(8,128)(2,1)}, u32[]{:S(2)}) copy-start(bf16[16,6,2304]{2,0,1:T(8,128)(2,1)} %param.10) | copy-start | bytes 1327108

commit v5 on v4

--- a/solution.py
+++ b/solution.py
@@ -79,9 +79,9 @@
 
 
 def front_kernel(
-    weights, cond, val, tc, ts, rot, ph, wide, table, m_out, slab_out,
+    weights, cond, val, cond_y, val_y, tc, ts, rot, ph, wide, table, m_out, slab_out,
     cbuf, vbuf, vf, even, odd, y, sacc, sl, yr, yi, mo, mb,
-    lsem, cs, cr, vs, vr, gs, gr, ss, sr, ms,
+    lsem, cs, cr, vs, vr, gs, gr, ss, sr, fs, fr, ms,
 ):
     row, col = lax.axis_index("row"), lax.axis_index("col")
     yh, x = row // 4, row % 4
@@ -89,8 +89,6 @@
     zo = z + 1 - 2 * (z % 2)
     xp = {"row": yh * 4 + (x + 1) % 4, "col": col}
     xm = {"row": yh * 4 + (x + 3) % 4, "col": col}
-    yc = {"row": (1 - yh) * 4 + x, "col": col}
-    yv = {"row": (1 - yh) * 4 + x, "col": z * 4 + (1 - yl) * 2 + core}
     group = [
         {"row": row, "col": zo * 4 + yl * 2 + core},
         {"row": row, "col": z * 4 + yl * 2 + 1 - core},
@@ -102,27 +100,29 @@
     own = [
         pltpu.make_async_copy(cond, cbuf.at[0], lsem.at[0]),
         pltpu.make_async_copy(val, vbuf.at[0], lsem.at[1]),
+        pltpu.make_async_copy(cond_y, cbuf.at[1], lsem.at[2]),
+        pltpu.make_async_copy(val_y, vbuf.at[1, part], lsem.at[3]),
     ]
     for copy in own:
         copy.start()
     barrier = pltpu.get_barrier_semaphore()
-    for peer in across + group + [yv]:
+    for peer in across + group:
         pl.semaphore_signal(barrier, inc=1, device_id=peer, device_id_type=MESH)
-    pl.semaphore_wait(barrier, 11)
-
-    hops = [(0, 3, None), (0, 2, xp), (0, 1, xm), (3, 5, xp), (3, 4, xm), (2, 6, xp), (4, 7, xm)]
+    pl.semaphore_wait(barrier, 10)
+
+    hops = [(0, 3, xp), (0, 2, xm), (1, 5, xp), (1, 4, xm), (3, 6, xp), (4, 7, xm)]
 
     def relay(n):
         src, dst, peer = hops[n]
         c = pltpu.make_async_remote_copy(
-            cond if src == 0 else cbuf.at[src], cbuf.at[dst], cs.at[n], cr.at[dst],
-            device_id=peer or yc, device_id_type=MESH,
+            (cond, cond_y)[src] if src < 2 else cbuf.at[src], cbuf.at[dst], cs.at[n], cr.at[dst],
+            device_id=peer, device_id_type=MESH,
         )
         v = pltpu.make_async_remote_copy(
-            val.at[part] if src == 0 else vbuf.at[src, part], vbuf.at[dst, part], vs.at[n], vr.at[dst],
-            device_id=peer or yv, device_id_type=MESH,
+            (val.at[part], val_y)[src] if src < 2 else vbuf.at[src, part], vbuf.at[dst, part], vs.at[n], vr.at[dst],
+            device_id=peer, device_id_type=MESH,
         )
-        return c, v
+        return v, c
 
     def go(n):
         for copy in relay(n):
@@ -138,7 +138,7 @@
         )
 
     def land(b, *forward):
-        c, v = incoming(b)
+        v, c = incoming(b)
         v.wait_recv()
         for j in range(3):
             spread(b, j).start()
@@ -150,46 +150,49 @@
         for j in range(3):
             spread(b, j).wait_recv()
 
-    for n in range(3):
+    for n in range(2):
+        go(n)
+    for copy in own:
+        copy.wait()
+    for j in range(3):
+        spread(1, j).start()
+    for n in range(2, 4):
         go(n)
     sacc[...] = jnp.zeros_like(sacc)
-    for copy in own:
-        copy.wait()
 
     def block(b, carry):
         @pl.when(b == 1)
         def _():
-            land(2, 5)
-            land(1)
-            land(3, 3, 4)
             ready(1)
 
         @pl.when(b == 2)
         def _():
+            land(3, 4)
+            land(2)
             ready(2)
 
         @pl.when(b == 3)
         def _():
-            land(4, 6)
             ready(3)
 
         @pl.when(b == 4)
         def _():
+            land(4, 5)
             land(5)
+            ready(4)
+
+        @pl.when(b == 5)
+        def _():
+            ready(5)
+
+        @pl.when(b == 6)
+        def _():
             land(6)
-            ready(4)
-
-        @pl.when(b == 5)
-        def _():
-            ready(5)
-
-        @pl.when(b == 6)
+            ready(6)
+
+        @pl.when(b == 7)
         def _():
             land(7)
-            ready(6)
-
-        @pl.when(b == 7)
-        def _():
             ready(7)
 
         def widen(j, carry):
@@ -212,18 +215,33 @@
 
     for h in range(2):
         sl[h * PAIRS : h * PAIRS + PAIRS, :] = (sacc[h] * wide[...]).astype(jnp.bfloat16)
-    keep = pltpu.make_async_copy(sl, slab_out.at[row], lsem.at[2])
+    keep = pltpu.make_async_copy(sl, slab_out.at[0, row], lsem.at[4])
     keep.start()
-    pushes = []
+
+    def push(k):
+        return pltpu.make_async_remote_copy(
+            sl, slab_out.at[0, row], ss.at[k], sr.at[k], device_id=across[k], device_id_type=MESH
+        )
+
+    def hand(k):
+        at = (row + 7 - k) % 8
+        return pltpu.make_async_remote_copy(
+            sl if k == 7 else slab_out.at[0, at], slab_out.at[1, at], fs.at[k], fr.at[k],
+            device_id=group[1], device_id_type=MESH,
+        )
+
     for k in range(7):
-        pushes.append(
-            pltpu.make_async_remote_copy(
-                sl, slab_out.at[row], ss.at[k], sr.at[k], device_id=across[k], device_id_type=MESH
-            )
-        )
-        pushes[-1].start()
+        push(k).start()
+    hand(7).start()
 
     def chunk(i, carry):
+        for k in range(7):
+
+            @pl.when(i == 5 + k)
+            def _():
+                push(k).wait_recv()
+                hand(k).start()
+
         slot = i % 2
         ps = pl.ds(pl.multiple_of(i * PB, PB), PB)
         out = pltpu.make_async_copy(mb.at[slot], m_out.at[:, ps, :], ms.at[slot])
@@ -254,10 +272,12 @@
     for slot in range(2):
         pltpu.make_async_copy(mb.at[slot], m_out.at[:, pl.ds(slot * PB, PB), :], ms.at[slot]).wait()
     keep.wait()
-    for push in pushes:
-        push.wait_recv()
-        push.wait_send()
-    for n in range(7):
+    for k in range(8):
+        hand(k).wait_recv()
+        hand(k).wait_send()
+    for k in range(7):
+        push(k).wait_send()
+    for n in range(len(hops)):
         for copy in relay(n):
             copy.wait_send()
     for b in range(1, BLOCKS):
@@ -265,7 +285,7 @@
             spread(b, j).wait_send()
 
 
-def front(weights, cond, val, tc, ts, rot, ph, wide, table):
+def front(weights, cond, val, cond_y, val_y, tc, ts, rot, ph, wide, table):
     dma = pltpu.SemaphoreType.DMA
     vmem = pl.BlockSpec(memory_space=pltpu.VMEM)
     hbm = pl.BlockSpec(memory_space=pl.ANY)
@@ -273,11 +293,11 @@
     fl = lambda *shape: pltpu.VMEM(shape, jnp.float32)
     return pl.pallas_call(
         front_kernel,
-        in_specs=[pl.BlockSpec(memory_space=pltpu.SMEM)] + [vmem] * 8,
+        in_specs=[pl.BlockSpec(memory_space=pltpu.SMEM)] + [vmem] * 10,
         out_specs=[hbm, hbm],
         out_shape=[
             jax.ShapeDtypeStruct((2 * NX, PAIRS, LANES), jnp.bfloat16),
-            jax.ShapeDtypeStruct((BLOCKS, 2 * PAIRS, JS), jnp.bfloat16),
+            jax.ShapeDtypeStruct((2, BLOCKS, 2 * PAIRS, JS), jnp.bfloat16),
         ],
         scratch_shapes=[
             bf(BLOCKS, PX, CL, CELLS),
@@ -292,14 +312,14 @@
             fl(2, NX * PB, 128),
             fl(2, 2 * NX * PB, 128),
             bf(2, 2 * NX, PB, LANES),
-            dma((3,)), dma((7,)), dma((8,)), dma((7,)), dma((8,)),
-            dma((24,)), dma((24,)), dma((7,)), dma((7,)), dma((2,)),
+            dma((5,)), dma((6,)), dma((8,)), dma((6,)), dma((8,)),
+            dma((24,)), dma((24,)), dma((7,)), dma((7,)), dma((8,)), dma((8,)), dma((2,)),
         ],
         compiler_params=pltpu.CompilerParams(
             collective_id=2, has_side_effects=True, vmem_limit_bytes=VMEM_LIMIT
         ),
         name="front",
-    )(weights, cond, val, tc, ts, rot, ph, wide, table)
+    )(weights, cond, val, cond_y, val_y, tc, ts, rot, ph, wide, table)
 
 
 GB = 320
@@ -387,7 +407,7 @@
 
 
 def back_kernel(
-    rows, slab, out, sw, lhs, tx, acc, r1, zr2, yr1, zr1, yr2,
+    rows, slab, out, sw, ours, theirs, acc, zr2, yr1, zr1, yr2,
     ms, s1, d1, sz2, dz2, sy1, dy1, sz1, dz1, sy2, dy2,
 ):
     row, col = lax.axis_index("row"), lax.axis_index("col")
@@ -399,33 +419,38 @@
     for peer in (core_peer, y_peer, z_peer(1), z_peer(2), z_peer(3)):
         pl.semaphore_signal(barrier, inc=1, device_id=peer, device_id_type=MESH)
 
-    for r in range(NS // JS):
-        sw[:, r * JS : r * JS + JS] = slab[r]
-
+    def place(n):
+        k, s = (n // 2 + 1) % 4, n % 2
+        return ((z + k) % 4) * 4 + (yl * s + (1 - yl) * (1 - s)) * 2
+
+    load = lambda n: pltpu.make_async_copy(rows.at[place(n) + core], ours.at[n], ms.at[n])
+    for n in range(8):
+        load(n).start()
     pl.semaphore_wait(barrier, 5)
 
     scale = -1.0 / math.sqrt(NV * NC)
-    load = lambda q, own: pltpu.make_async_copy(rows.at[q], lhs.at[own], ms.at[own])
-
-    def product(own, dst):
-        value = jnp.dot(lhs[own], sw[...], preferred_element_type=jnp.float32)
-        dst[...] = (value * scale).astype(jnp.bfloat16)
-
     def remote(src, dst, ss, ds, peer):
         return pltpu.make_async_remote_copy(src, dst, ss, ds, device_id=peer, device_id_type=MESH)
 
     lo, hi = pl.ds(0, HR), pl.ds(HR, HR)
-    first = lambda n: remote(tx.at[n], r1.at[n], s1.at[n], d1.at[n], core_peer)
+    first = lambda n: remote(rows.at[place(n) + 1 - core], theirs.at[n], s1.at[n], d1.at[n], core_peer)
+    for n in range(8):
+        first(n).start()
+    for h in range(2):
+        for r in range(NS // JS):
+            sw[h * 2 * PAIRS : (h + 1) * 2 * PAIRS, r * JS : r * JS + JS] = slab[h, r]
     along_z = lambda k, s: remote(
         acc.at[(k + 3) % 4 * 2 + s, hi], zr2.at[(k - 1) * 2 + s], sz2.at[(k - 1) * 2 + s], dz2.at[(k - 1) * 2 + s], z_peer(k)
     )
     along_y = lambda k: remote(acc.at[(k + 3) % 4 * 2, lo], yr1.at[k], sy1.at[k], dy1.at[k], y_peer)
     last_z = lambda k: remote(acc.at[(k + 3) % 4 * 2 + 1, lo], zr1.at[k - 1], sz1.at[k - 1], dz1.at[k - 1], z_peer(k))
 
-    def settle(n):
+    def slot(n, carry):
         k, s = (n // 2 + 1) % 4, n % 2
+        load(n).wait()
         first(n).wait_recv()
-        add_rows(acc.at[n], acc.at[n], r1.at[n], G_DEV)
+        lhs = jnp.concatenate([ours[n], theirs[n]], axis=1)
+        acc[n] = (jnp.dot(lhs, sw[...], preferred_element_type=jnp.float32) * scale).astype(jnp.bfloat16)
 
         @pl.when(n < 6)
         def _():
@@ -435,36 +460,9 @@
         def _():
             along_y(k).start()
 
-    def place(n):
-        k, s = (n // 2 + 1) % 4, n % 2
-        return ((z + k) % 4) * 4 + (yl * s + (1 - yl) * (1 - s)) * 2
-
-    def slot(n, carry):
-        load(place(n) + 1 - core, 0).wait()
-        product(0, tx.at[n])
-        first(n).start()
-
-        @pl.when(n < 7)
-        def _():
-            load(place(n + 1) + 1 - core, 0).start()
-
-        load(place(n) + core, 1).wait()
-        product(1, acc.at[n])
-
-        @pl.when(n < 7)
-        def _():
-            load(place(n + 1) + core, 1).start()
-
-        @pl.when(n > 0)
-        def _():
-            settle(n - 1)
-
-        return carry
-
-    load(place(0) + 1 - core, 0).start()
-    load(place(0) + core, 1).start()
+        return carry
+
     lax.fori_loop(0, 8, slot, 0)
-    settle(7)
     for k in (1, 2, 3, 0):
         along_y(k).wait_recv()
         if k:
@@ -529,13 +527,12 @@
         out_specs=vmem,
         out_shape=jax.ShapeDtypeStruct((G_DEV, NS), jnp.float32),
         scratch_shapes=[
-            pltpu.VMEM((2 * PAIRS, NS), jnp.bfloat16),
-            pltpu.VMEM((2, GB, 2 * PAIRS), jnp.bfloat16),
-            pltpu.VMEM((8, G_DEV, NS), jnp.bfloat16),
-            pltpu.VMEM((8, G_DEV, NS), jnp.bfloat16),
+            pltpu.VMEM((4 * PAIRS, NS), jnp.bfloat16),
+            pltpu.VMEM((8, GB, 2 * PAIRS), jnp.bfloat16),
+            pltpu.VMEM((8, GB, 2 * PAIRS), jnp.bfloat16),
             pltpu.VMEM((8, G_DEV, NS), jnp.bfloat16),
             half(6), half(4), half(3), half(2),
-            dma((2,)), dma((8,)), dma((8,)), dma((6,)), dma((6,)), dma((4,)), dma((4,)),
+            dma((8,)), dma((8,)), dma((8,)), dma((6,)), dma((6,)), dma((4,)), dma((4,)),
             dma((3,)), dma((3,)), dma((1,)), dma((1,)),
         ],
         compiler_params=pltpu.CompilerParams(
@@ -545,21 +542,32 @@
     )(rows, slab)
 
 
-def places_kernel(mine, out, send_sem, recv_sem):
+def places_kernel(mine, cond, val, out, cond_out, val_out, send_sem, recv_sem, ys, yr):
     row, col = lax.axis_index("row"), lax.axis_index("col")
+    z, yl, core = col // 4, (col // 2) % 2, col % 2
     barrier = pltpu.get_barrier_semaphore()
     peers = [{"row": (row + k) % 8, "col": col} for k in range(1, 8)]
-    for peer in peers:
+    yc = {"row": (row + 4) % 8, "col": col}
+    yv = {"row": (row + 4) % 8, "col": z * 4 + (1 - yl) * 2 + core}
+    for peer in peers + [yv]:
         pl.semaphore_signal(barrier, inc=1, device_id=peer, device_id_type=MESH)
-    pl.semaphore_wait(barrier, 7)
-    copies = []
+    pl.semaphore_wait(barrier, 8)
+    copies = [
+        pltpu.make_async_remote_copy(
+            cond, cond_out, ys.at[0], yr.at[0], device_id=yc, device_id_type=MESH
+        ),
+        pltpu.make_async_remote_copy(
+            val.at[core * 2 + z % 2], val_out, ys.at[1], yr.at[1], device_id=yv, device_id_type=MESH
+        ),
+    ]
     for k, peer in enumerate(peers):
         copies.append(
             pltpu.make_async_remote_copy(
                 mine, out.at[row], send_sem.at[k], recv_sem.at[k], device_id=peer, device_id_type=MESH
             )
         )
-        copies[-1].start()
+    for copy in copies:
+        copy.start()
     out[row] = mine[...]
     for copy in copies:
         copy.wait_recv()
@@ -567,16 +575,22 @@
         copy.wait_send()
 
 
-def places(mine):
+def places(mine, cond, val):
+    dma = pltpu.SemaphoreType.DMA
+    vmem = pl.BlockSpec(memory_space=pltpu.VMEM)
     return pl.pallas_call(
         places_kernel,
-        in_specs=[pl.BlockSpec(memory_space=pltpu.VMEM)],
-        out_specs=pl.BlockSpec(memory_space=pltpu.VMEM),
-        out_shape=jax.ShapeDtypeStruct((8, G_ROW // 128, 128), jnp.int32),
-        scratch_shapes=[pltpu.SemaphoreType.DMA((7,)), pltpu.SemaphoreType.DMA((7,))],
+        in_specs=[vmem] * 3,
+        out_specs=[vmem] * 3,
+        out_shape=[
+            jax.ShapeDtypeStruct((8, G_ROW // 128, 128), jnp.int32),
+            jax.ShapeDtypeStruct((PX, CL, CELLS), jnp.bfloat16),
+            jax.ShapeDtypeStruct((PX // 2, NV, HALF), jnp.bfloat16),
+        ],
+        scratch_shapes=[dma((7,)), dma((7,)), dma((2,)), dma((2,))],
         compiler_params=pltpu.CompilerParams(collective_id=1, has_side_effects=True),
         name="places",
-    )(mine)
+    )(mine, cond, val)
 
 
 def body(psi_val, psi_cond, energy_val, energy_cond, stick_map, gvec_map, slab_index):
@@ -588,7 +602,8 @@
 
     mine = lax.dynamic_slice(stick_map, (row * STK,), (STK,))
     cols = lax.dynamic_slice(slab_index, (row * JS,), (JS,))
-    maps = places(gvec_map.reshape(G_ROW // 128, 128)).reshape(-1)
+    maps, cond_y, val_y = places(gvec_map.reshape(G_ROW // 128, 128), cond, val)
+    maps = maps.reshape(-1)
     place = jnp.take(maps, cols)
     col_kx = place // STK
     col_stick = jnp.take(stick_map, cols // G_ROW * STK + place % STK)
@@ -598,8 +613,8 @@
     tc, ts = half_phase(ky, kz)
     turn = ((ky + kz) % 96).astype(jnp.float32) * (math.pi / 48.0)
     rot = jnp.stack([jnp.cos(turn[:LANES]), jnp.sin(turn[:LANES])])
-    dy = jnp.array([0, 0, 0, 1, 1, 1, 0, 1], jnp.int32)
-    dx = jnp.array([0, 1, 3, 0, 1, 3, 2, 2], jnp.int32)
+    dy = jnp.array([0, 1, 0, 0, 1, 1, 0, 1], jnp.int32)
+    dx = jnp.array([0, 0, 1, 3, 1, 3, 2, 2], jnp.int32)
     source = (row // 4 + dy) % 2 * 4 + (row % 4 + dx) % 4
     xs = (source[:, None] * PX + jnp.arange(PX, dtype=jnp.int32)[None, :]).reshape(NX)
     theta = (
@@ -619,7 +634,7 @@
         [jnp.concatenate([cx, sx], axis=1), jnp.concatenate([-sx, cx], axis=1)], axis=0
     ).astype(jnp.bfloat16)
 
-    m, slab = front(weight, cond, val, tc, ts, rot, ph, wide, table)
+    m, slab = front(weight, cond, val, cond_y, val_y, tc, ts, rot, ph, wide, table)
     return back(pick(gvec_map, m.reshape(2, NX, PAIRS, LANES)), slab)
 
 

time: 211 us -> 238 us (1.13)
  Pallas kernels: 190 us -> 217 us
    pallas_call x1, Pallas kernels: 99.5 us -> 116 us  [front(): pl.pallas_call(front_kernel, in_specs=[pl.BlockSpec(memory_space=pltpu.SM...]
    pallas_call x1, Pallas kernels: 10.8 us -> 23.4 us  [places(): pl.pallas_call(places_kernel, in_specs=[vmem] * 3, out_specs=[vmem] * 3,...]
where the time goes in v5:
time: 238 us; the launch traced here: 237 us
  Pallas kernels  217 us (91%)
  other arithmetic  10.2 us (4%)
  local copies, waits for them, and re-layouts  10.1 us (4%)
    pallas_call x1, Pallas kernels, front(): pl.pallas_call(front_kernel, in_specs=[pl.BlockSpec(memory_space=pltpu.SM...  116 us
    pallas_call x1, Pallas kernels, back(): pl.pallas_call(back_kernel, in_specs=[pl.BlockSpec(memory_space=pl.ANY),...  54.9 us
    pallas_call x1, Pallas kernels, places(): pl.pallas_call(places_kernel, in_specs=[vmem] * 3, out_specs=[vmem] * 3,...  23.4 us
    pallas_call x1, Pallas kernels, pick(): pl.pallas_call(pick_kernel, in_specs=[pl.BlockSpec(memory_space=pltpu.SME...  22.8 us

profile of v5, /device:TPU:1, one launch (start us, length us, event | category | flops | bytes accessed | tf_op | source)
XLA Modules:
  0.0 237.2 jit_solution(12836580432282256733)
XLA Ops:
  0.0 0.7 fusion.33
  0.7 0.8 dynamic_slice.6
  1.5 0.8 compare_select_fusion.1
  2.4 0.8 sqrt_multiply_fusion
  3.4 0.7 maximum_maximum_fusion.table
  4.1 0.8 broadcast_in_dim.22.wide
  4.9 1.1 fusion.36
  5.9 0.9 rev.8
  6.8 0.8 pad_maximum_fusion.1
  7.7 0.9 rev.7
  8.6 0.8 pad_maximum_fusion.cond
  9.4 23.4 %places.1 = (s32[8,40,128]{2,1,0:T(8,128)}, bf16[6,16,2304]{2,1,0:T(8,128)(2,1)}, bf16[3,16,1152]{2,1,0:T(8,128)(2,1)}) custom-call(s32[40,128]{1,0:T(8,128)} %bitcast.28, bf16[6,16,2304]{2,1,0:T(8,128)(2,1)} %pad_maximum_fusion.cond, bf16[4,3,16,1152]{3,2,1,0:T(8,128)(2,1)} %bitcast.18), custom_call_target="tpu_custom_call" | custom-call | tf_op jit(solution)/shard_map/places/pallas_call | solution.py:581
  32.8 1.8 gather_fusion
  34.7 0.8 and_select_fusion
  35.5 1.1 gather_fusion.1
  36.9 0.6 pad_maximum_fusion.3.rot
  37.6 0.7 multiply_cosine_fusion
  38.3 0.7 pad_maximum_fusion.2.ph
  39.2 0.4 fusion.5
  39.6 1.8 negate_convert_fusion
  41.3 115.6 %front.1 = (bf16[96,256,256]{2,1,0:T(8,128)(2,1)}, bf16[2,8,512,128]{3,2,1,0:T(8,128)(2,1)}) custom-call(f32[256]{0:T(256)} %copy-done.2, bf16[6,16,2304]{2,1,0:T(8,128)(2,1)} %pad_maximum_fusion.cond, bf16[4,3,16,1152]{3,2,1,0:T(8,128)(2,1)} %bitcast.19, bf16[6,16,2304]{2,1,0:T(8,128)(2,1)} %get-tuple-element.10.cond_y, ...), custom_call_target="tpu_custom_call" | custom-call | tf_op jit(solution)/shard_map/front/pallas_call | solution.py:294
  157.0 22.8 %pick.1.rows = bf16[16,320,512]{2,1,0:T(8,128)(2,1)} custom-call(s32[5120]{0:T(1024)} %g_ref.1, bf16[2,48,256,256]{3,2,1,0:T(8,128)(2,1)} %bitcast.17), custom_call_target="tpu_custom_call" | custom-call | tf_op jit(solution)/shard_map/pick/pallas_call | solution.py:383
  179.7 54.9 %back.1 = f32[320,1024]{1,0:T(8,128)} custom-call(bf16[16,320,512]{2,1,0:T(8,128)(2,1)} %pick.1.rows, bf16[2,8,512,128]{3,2,1,0:T(8,128)(2,1)} %get-tuple-element.14.slab), custom_call_target="tpu_custom_call" | custom-call | tf_op jit(solution)/shard_map/back/pallas_call | solution.py:524
  234.7 2.5 %copy.18 = f32[320,1024]{1,0:T(8,128)} copy(f32[320,1024]{1,0:T(8,128)} %back.1) | data formatting | bytes 2621440
  (23 shorter events, 1.0 us)
Async XLA Ops:
  0.0 7.6 %copy-start.1 = (bf16[16,6,2304]{2,0,1:T(8,128)(2,1)S(1)}, bf16[16,6,2304]{2,0,1:T(8,128)(2,1)}, u32[]{:S(2)}) copy-start(bf16[16,6,2304]{2,0,1:T(8,128)(2,1)} %param.10) | copy-start | bytes 1327108
  3.3 5.3 %copy-start.2 = (f32[256]{0:T(256)}, f32[256]{0:T(256)S(1)}, u32[]{:S(2)}) copy-start(f32[256]{0:T(256)S(1)} %mul.253.weights) | copy-start | bytes 3076
  7.6 27.8 %copy-start = (s32[1536]{0:T(1024)S(1)}, s32[1536]{0:T(1024)}, u32[]{:S(2)}) copy-start(s32[1536]{0:T(1024)} %param.13) | copy-start | bytes 18436

commit v6 on v5

--- a/solution.py
+++ b/solution.py
@@ -46,17 +46,14 @@
 
 
 def density(vf, cbuf, b, plane, at, even, odd):
-    def one(v, carry):
-        out = pl.ds(pl.multiple_of(at * PAIRS + v * CL, CL), CL)
-        cond = cbuf.at[b, plane]
-        spread = lambda h: jnp.broadcast_to(vf[h, plane, pl.ds(v, 1), :], (CL, HALF)).astype(jnp.bfloat16)
+    cond = cbuf.at[b, plane]
+    for v in range(NV):
+        out = slice(at * PAIRS + v * CL, at * PAIRS + v * CL + CL)
+        spread = lambda h: jnp.broadcast_to(vf[h, plane, v : v + 1, :], (CL, HALF)).astype(jnp.bfloat16)
         lo = spread(0) * cond[:, :HALF]
         hi = spread(1) * cond[:, HALF:]
         even[out, :] = lo + hi
         odd[out, :] = lo - hi
-        return carry
-
-    lax.fori_loop(0, NV, one, 0, unroll=4)
 
 
 def transform(b, first, even, odd, tc, ts, rot, ph, y, sacc):
@@ -79,7 +76,7 @@
 
 
 def front_kernel(
-    weights, cond, val, cond_y, val_y, tc, ts, rot, ph, wide, table, m_out, slab_out,
+    weights, cond, val, tc, ts, rot, ph, wide, table, m_out, slab_out,
     cbuf, vbuf, vf, even, odd, y, sacc, sl, yr, yi, mo, mb,
     lsem, cs, cr, vs, vr, gs, gr, ss, sr, fs, fr, ms,
 ):
@@ -89,6 +86,8 @@
     zo = z + 1 - 2 * (z % 2)
     xp = {"row": yh * 4 + (x + 1) % 4, "col": col}
     xm = {"row": yh * 4 + (x + 3) % 4, "col": col}
+    yc = {"row": (1 - yh) * 4 + x, "col": col}
+    yv = {"row": (1 - yh) * 4 + x, "col": z * 4 + (1 - yl) * 2 + core}
     group = [
         {"row": row, "col": zo * 4 + yl * 2 + core},
         {"row": row, "col": z * 4 + yl * 2 + 1 - core},
@@ -100,36 +99,30 @@
     own = [
         pltpu.make_async_copy(cond, cbuf.at[0], lsem.at[0]),
         pltpu.make_async_copy(val, vbuf.at[0], lsem.at[1]),
-        pltpu.make_async_copy(cond_y, cbuf.at[1], lsem.at[2]),
-        pltpu.make_async_copy(val_y, vbuf.at[1, part], lsem.at[3]),
     ]
     for copy in own:
         copy.start()
     barrier = pltpu.get_barrier_semaphore()
-    for peer in across + group:
+    for peer in across + group + [yv]:
         pl.semaphore_signal(barrier, inc=1, device_id=peer, device_id_type=MESH)
-    pl.semaphore_wait(barrier, 10)
-
-    hops = [(0, 3, xp), (0, 2, xm), (1, 5, xp), (1, 4, xm), (3, 6, xp), (4, 7, xm)]
-
-    def relay(n):
+    pl.semaphore_wait(barrier, 11)
+
+    hops = [(0, 3, None), (0, 2, xp), (0, 1, xm), (3, 6, xp), (3, 5, xm), (2, 4, xp), (5, 7, xm)]
+    hop_to = [hop[1] for hop in hops]
+
+    def cond_hop(n):
         src, dst, peer = hops[n]
-        c = pltpu.make_async_remote_copy(
-            (cond, cond_y)[src] if src < 2 else cbuf.at[src], cbuf.at[dst], cs.at[n], cr.at[dst],
-            device_id=peer, device_id_type=MESH,
+        return pltpu.make_async_remote_copy(
+            cbuf.at[src] if src else cond, cbuf.at[dst], cs.at[n], cr.at[dst],
+            device_id=peer or yc, device_id_type=MESH,
         )
-        v = pltpu.make_async_remote_copy(
-            (val.at[part], val_y)[src] if src < 2 else vbuf.at[src, part], vbuf.at[dst, part], vs.at[n], vr.at[dst],
-            device_id=peer, device_id_type=MESH,
+
+    def val_hop(n):
+        src, dst, peer = hops[n]
+        return pltpu.make_async_remote_copy(
+            vbuf.at[src, part] if src else val.at[part], vbuf.at[dst, part], vs.at[n], vr.at[dst],
+            device_id=peer or yv, device_id_type=MESH,
         )
-        return v, c
-
-    def go(n):
-        for copy in relay(n):
-            copy.start()
-
-    def incoming(dst):
-        return relay([hop[1] for hop in hops].index(dst))
 
     def spread(b, j):
         return pltpu.make_async_remote_copy(
@@ -137,57 +130,66 @@
             device_id=group[j], device_id_type=MESH,
         )
 
-    def land(b, *forward):
-        v, c = incoming(b)
-        v.wait_recv()
+    def land_val(b, *forward):
+        val_hop(hop_to.index(b)).wait_recv()
+        for n in forward:
+            val_hop(n).start()
         for j in range(3):
             spread(b, j).start()
-        c.wait_recv()
+
+    def land(b, *forward):
+        cond_hop(hop_to.index(b)).wait_recv()
         for n in forward:
-            go(n)
+            cond_hop(n).start()
 
     def ready(b):
         for j in range(3):
             spread(b, j).wait_recv()
 
-    for n in range(2):
-        go(n)
+    for n in range(3):
+        val_hop(n).start()
+    for n in range(3):
+        cond_hop(n).start()
+    sacc[...] = jnp.zeros_like(sacc)
     for copy in own:
         copy.wait()
-    for j in range(3):
-        spread(1, j).start()
-    for n in range(2, 4):
-        go(n)
-    sacc[...] = jnp.zeros_like(sacc)
 
     def block(b, carry):
         @pl.when(b == 1)
         def _():
+            land_val(1)
+            land_val(2, 5)
+            land_val(3, 3, 4)
+            land(2, 5)
+            land(1)
             ready(1)
 
         @pl.when(b == 2)
         def _():
-            land(3, 4)
-            land(2)
+            land(3, 3, 4)
+            land_val(4)
+            land_val(5, 6)
+            land_val(6)
             ready(2)
 
         @pl.when(b == 3)
         def _():
+            land_val(7)
             ready(3)
 
         @pl.when(b == 4)
         def _():
-            land(4, 5)
-            land(5)
+            land(4)
             ready(4)
 
         @pl.when(b == 5)
         def _():
+            land(5, 6)
+            land(6)
             ready(5)
 
         @pl.when(b == 6)
         def _():
-            land(6)
             ready(6)
 
         @pl.when(b == 7)
@@ -215,7 +217,7 @@
 
     for h in range(2):
         sl[h * PAIRS : h * PAIRS + PAIRS, :] = (sacc[h] * wide[...]).astype(jnp.bfloat16)
-    keep = pltpu.make_async_copy(sl, slab_out.at[0, row], lsem.at[4])
+    keep = pltpu.make_async_copy(sl, slab_out.at[0, row], lsem.at[2])
     keep.start()
 
     def push(k):
@@ -278,14 +280,14 @@
     for k in range(7):
         push(k).wait_send()
     for n in range(len(hops)):
-        for copy in relay(n):
-            copy.wait_send()
+        val_hop(n).wait_send()
+        cond_hop(n).wait_send()
     for b in range(1, BLOCKS):
         for j in range(3):
             spread(b, j).wait_send()
 
 
-def front(weights, cond, val, cond_y, val_y, tc, ts, rot, ph, wide, table):
+def front(weights, cond, val, tc, ts, rot, ph, wide, table):
     dma = pltpu.SemaphoreType.DMA
     vmem = pl.BlockSpec(memory_space=pltpu.VMEM)
     hbm = pl.BlockSpec(memory_space=pl.ANY)
@@ -293,7 +295,7 @@
     fl = lambda *shape: pltpu.VMEM(shape, jnp.float32)
     return pl.pallas_call(
         front_kernel,
-        in_specs=[pl.BlockSpec(memory_space=pltpu.SMEM)] + [vmem] * 10,
+        in_specs=[pl.BlockSpec(memory_space=pltpu.SMEM)] + [vmem] * 8,
         out_specs=[hbm, hbm],
         out_shape=[
             jax.ShapeDtypeStruct((2 * NX, PAIRS, LANES), jnp.bfloat16),
@@ -312,20 +314,21 @@
             fl(2, NX * PB, 128),
             fl(2, 2 * NX * PB, 128),
             bf(2, 2 * NX, PB, LANES),
-            dma((5,)), dma((6,)), dma((8,)), dma((6,)), dma((8,)),
+            dma((3,)), dma((7,)), dma((8,)), dma((7,)), dma((8,)),
             dma((24,)), dma((24,)), dma((7,)), dma((7,)), dma((8,)), dma((8,)), dma((2,)),
         ],
         compiler_params=pltpu.CompilerParams(
             collective_id=2, has_side_effects=True, vmem_limit_bytes=VMEM_LIMIT
         ),
         name="front",
-    )(weights, cond, val, cond_y, val_y, tc, ts, rot, ph, wide, table)
+    )(weights, cond, val, tc, ts, rot, ph, wide, table)
 
 
 GB = 320
 QS = 2 * PAIRS // 128
 G_DEV = 320
-HR = G_DEV // 2
+LO = 192
+HI = G_DEV - LO
 DEPTH = 4
 UNROLL = 16
 
@@ -432,7 +435,7 @@
     def remote(src, dst, ss, ds, peer):
         return pltpu.make_async_remote_copy(src, dst, ss, ds, device_id=peer, device_id_type=MESH)
 
-    lo, hi = pl.ds(0, HR), pl.ds(HR, HR)
+    lo, hi = pl.ds(0, LO), pl.ds(LO, HI)
     first = lambda n: remote(rows.at[place(n) + 1 - core], theirs.at[n], s1.at[n], d1.at[n], core_peer)
     for n in range(8):
         first(n).start()
@@ -467,7 +470,7 @@
         along_y(k).wait_recv()
         if k:
             at = acc.at[(k + 3) % 4 * 2 + 1]
-            add_rows(at, at, yr1.at[k], HR)
+            add_rows(at, at, yr1.at[k], LO)
             last_z(k).start()
     for k in (1, 2, 3):
         along_z(k, 0).wait_recv()
@@ -484,7 +487,7 @@
         yr2[0, at, :] = value.astype(jnp.bfloat16)
         return carry
 
-    lax.fori_loop(0, HR // 16, across, 0)
+    lax.fori_loop(0, HI // 16, across, 0)
     last_y = remote(yr2.at[0], yr2.at[1], sy2.at[0], dy2.at[0], y_peer)
     last_y.start()
     for k in (1, 2, 3):
@@ -495,17 +498,17 @@
         out[at, :] = value
         return carry
 
-    lax.fori_loop(0, HR // 16, low, 0)
+    lax.fori_loop(0, LO // 16, low, 0)
     for k in (1, 2, 3):
         along_z(k, 1).wait_recv()
     last_y.wait_recv()
 
     def high(i, carry):
         at, value = total(i, acc.at[7, hi], [zr2.at[1], zr2.at[3], zr2.at[5], yr2.at[1]])
-        out[pl.ds(pl.multiple_of(HR + i * 16, 16), 16), :] = value
-        return carry
-
-    lax.fori_loop(0, HR // 16, high, 0)
+        out[pl.ds(pl.multiple_of(LO + i * 16, 16), 16), :] = value
+        return carry
+
+    lax.fori_loop(0, HI // 16, high, 0)
     for n in range(8):
         first(n).wait_send()
     for k in range(4):
@@ -520,7 +523,7 @@
 def back(rows, slab):
     dma = pltpu.SemaphoreType.DMA
     vmem = pl.BlockSpec(memory_space=pltpu.VMEM)
-    half = lambda n: pltpu.VMEM((n, HR, NS), jnp.bfloat16)
+    part = lambda n, rows: pltpu.VMEM((n, rows, NS), jnp.bfloat16)
     return pl.pallas_call(
         back_kernel,
         in_specs=[pl.BlockSpec(memory_space=pl.ANY), vmem],
@@ -531,7 +534,7 @@
             pltpu.VMEM((8, GB, 2 * PAIRS), jnp.bfloat16),
             pltpu.VMEM((8, GB, 2 * PAIRS), jnp.bfloat16),
             pltpu.VMEM((8, G_DEV, NS), jnp.bfloat16),
-            half(6), half(4), half(3), half(2),
+            part(6, HI), part(4, LO), part(3, LO), part(2, HI),
             dma((8,)), dma((8,)), dma((8,)), dma((6,)), dma((6,)), dma((4,)), dma((4,)),
             dma((3,)), dma((3,)), dma((1,)), dma((1,)),
         ],
@@ -542,32 +545,21 @@
     )(rows, slab)
 
 
-def places_kernel(mine, cond, val, out, cond_out, val_out, send_sem, recv_sem, ys, yr):
+def places_kernel(mine, out, send_sem, recv_sem):
     row, col = lax.axis_index("row"), lax.axis_index("col")
-    z, yl, core = col // 4, (col // 2) % 2, col % 2
     barrier = pltpu.get_barrier_semaphore()
     peers = [{"row": (row + k) % 8, "col": col} for k in range(1, 8)]
-    yc = {"row": (row + 4) % 8, "col": col}
-    yv = {"row": (row + 4) % 8, "col": z * 4 + (1 - yl) * 2 + core}
-    for peer in peers + [yv]:
+    for peer in peers:
         pl.semaphore_signal(barrier, inc=1, device_id=peer, device_id_type=MESH)
-    pl.semaphore_wait(barrier, 8)
-    copies = [
-        pltpu.make_async_remote_copy(
-            cond, cond_out, ys.at[0], yr.at[0], device_id=yc, device_id_type=MESH
-        ),
-        pltpu.make_async_remote_copy(
-            val.at[core * 2 + z % 2], val_out, ys.at[1], yr.at[1], device_id=yv, device_id_type=MESH
-        ),
-    ]
+    pl.semaphore_wait(barrier, 7)
+    copies = []
     for k, peer in enumerate(peers):
         copies.append(
             pltpu.make_async_remote_copy(
                 mine, out.at[row], send_sem.at[k], recv_sem.at[k], device_id=peer, device_id_type=MESH
             )
         )
-    for copy in copies:
-        copy.start()
+        copies[-1].start()
     out[row] = mine[...]
     for copy in copies:
         copy.wait_recv()
@@ -575,22 +567,16 @@
         copy.wait_send()
 
 
-def places(mine, cond, val):
-    dma = pltpu.SemaphoreType.DMA
-    vmem = pl.BlockSpec(memory_space=pltpu.VMEM)
+def places(mine):
     return pl.pallas_call(
         places_kernel,
-        in_specs=[vmem] * 3,
-        out_specs=[vmem] * 3,
-        out_shape=[
-            jax.ShapeDtypeStruct((8, G_ROW // 128, 128), jnp.int32),
-            jax.ShapeDtypeStruct((PX, CL, CELLS), jnp.bfloat16),
-            jax.ShapeDtypeStruct((PX // 2, NV, HALF), jnp.bfloat16),
-        ],
-        scratch_shapes=[dma((7,)), dma((7,)), dma((2,)), dma((2,))],
+        in_specs=[pl.BlockSpec(memory_space=pltpu.VMEM)],
+        out_specs=pl.BlockSpec(memory_space=pltpu.VMEM),
+        out_shape=jax.ShapeDtypeStruct((8, G_ROW // 128, 128), jnp.int32),
+        scratch_shapes=[pltpu.SemaphoreType.DMA((7,)), pltpu.SemaphoreType.DMA((7,))],
         compiler_params=pltpu.CompilerParams(collective_id=1, has_side_effects=True),
         name="places",
-    )(mine, cond, val)
+    )(mine)
 
 
 def body(psi_val, psi_cond, energy_val, energy_cond, stick_map, gvec_map, slab_index):
@@ -602,8 +588,7 @@
 
     mine = lax.dynamic_slice(stick_map, (row * STK,), (STK,))
     cols = lax.dynamic_slice(slab_index, (row * JS,), (JS,))
-    maps, cond_y, val_y = places(gvec_map.reshape(G_ROW // 128, 128), cond, val)
-    maps = maps.reshape(-1)
+    maps = places(gvec_map.reshape(G_ROW // 128, 128)).reshape(-1)
     place = jnp.take(maps, cols)
     col_kx = place // STK
     col_stick = jnp.take(stick_map, cols // G_ROW * STK + place % STK)
@@ -613,8 +598,8 @@
     tc, ts = half_phase(ky, kz)
     turn = ((ky + kz) % 96).astype(jnp.float32) * (math.pi / 48.0)
     rot = jnp.stack([jnp.cos(turn[:LANES]), jnp.sin(turn[:LANES])])
-    dy = jnp.array([0, 1, 0, 0, 1, 1, 0, 1], jnp.int32)
-    dx = jnp.array([0, 0, 1, 3, 1, 3, 2, 2], jnp.int32)
+    dy = jnp.array([0, 0, 0, 1, 0, 1, 1, 1], jnp.int32)
+    dx = jnp.array([0, 1, 3, 0, 2, 1, 3, 2], jnp.int32)
     source = (row // 4 + dy) % 2 * 4 + (row % 4 + dx) % 4
     xs = (source[:, None] * PX + jnp.arange(PX, dtype=jnp.int32)[None, :]).reshape(NX)
     theta = (
@@ -634,7 +619,7 @@
         [jnp.concatenate([cx, sx], axis=1), jnp.concatenate([-sx, cx], axis=1)], axis=0
     ).astype(jnp.bfloat16)
 
-    m, slab = front(weight, cond, val, cond_y, val_y, tc, ts, rot, ph, wide, table)
+    m, slab = front(weight, cond, val, tc, ts, rot, ph, wide, table)
     return back(pick(gvec_map, m.reshape(2, NX, PAIRS, LANES)), slab)
 
 

time: 238 us -> 197 us (0.83)
  Pallas kernels: 217 us -> 176 us
    pallas_call x1, Pallas kernels: 116 us -> 86.8 us  [front(): pl.pallas_call(front_kernel, in_specs=[pl.BlockSpec(memory_space=pltpu.SM...]
    pallas_call x1, Pallas kernels: 23.4 us -> 10.8 us  [places(): pl.pallas_call(places_kernel, in_specs=[pl.BlockSpec(memory_space=pltpu.V...]
where the time goes in v6:
time: 197 us; the launch traced here: 196 us
  Pallas kernels  176 us (89%)
  other arithmetic  10.2 us (5%)
  local copies, waits for them, and re-layouts  9.61 us (5%)
    pallas_call x1, Pallas kernels, front(): pl.pallas_call(front_kernel, in_specs=[pl.BlockSpec(memory_space=pltpu.SM...  86.8 us
    pallas_call x1, Pallas kernels, back(): pl.pallas_call(back_kernel, in_specs=[pl.BlockSpec(memory_space=pl.ANY),...  55.9 us
    pallas_call x1, Pallas kernels, pick(): pl.pallas_call(pick_kernel, in_specs=[pl.BlockSpec(memory_space=pltpu.SME...  22.8 us
    pallas_call x1, Pallas kernels, places(): pl.pallas_call(places_kernel, in_specs=[pl.BlockSpec(memory_space=pltpu.V...  10.8 us

profile of v6, /device:TPU:1, one launch (start us, length us, event | category | flops | bytes accessed | tf_op | source)
XLA Modules:
  0.0 196.1 jit_solution(8143776971434734295)
XLA Ops:
  0.0 0.7 fusion.33
  0.7 0.8 dynamic_slice.6
  1.5 0.8 compare_select_fusion.1
  2.4 0.8 sqrt_multiply_fusion
  3.4 0.7 maximum_maximum_fusion.table
  4.1 0.7 broadcast_in_dim.22.wide
  4.8 10.8 %places.1 = s32[8,40,128]{2,1,0:T(8,128)} custom-call(s32[40,128]{1,0:T(8,128)} %bitcast.27), custom_call_target="tpu_custom_call" | custom-call | tf_op jit(solution)/shard_map/places/pallas_call | solution.py:571
  15.6 1.9 gather_fusion
  17.5 0.8 and_select_fusion
  18.3 1.6 gather_fusion.1
  20.2 0.6 pad_maximum_fusion.3.rot
  20.9 0.7 multiply_cosine_fusion
  21.6 0.7 pad_maximum_fusion.2.ph
  22.3 0.2 fusion.12
  22.5 0.4 fusion.5
  22.9 0.9 rev.8
  23.8 0.8 pad_maximum_fusion.1
  24.7 0.9 rev.7
  25.6 0.8 pad_maximum_fusion.cond
  26.3 1.8 negate_convert_fusion
  28.1 86.8 %front.1 = (bf16[96,256,256]{2,1,0:T(8,128)(2,1)}, bf16[2,8,512,128]{3,2,1,0:T(8,128)(2,1)}) custom-call(f32[256]{0:T(256)} %copy-done.2, bf16[6,16,2304]{2,1,0:T(8,128)(2,1)} %pad_maximum_fusion.cond, bf16[4,3,16,1152]{3,2,1,0:T(8,128)(2,1)} %bitcast.21, bf16[1152,384]{1,0:T(8,128)(2,1)} %bitcast.19, bf16[1152,384]{1,0:T(8,128)(2,1)} %bitcast.18, ...), custom_call_target="tpu_custom_call" | custom-call | tf_op jit(solution)/shard_map/front/pallas_call | solution.py:296
  114.9 22.8 %pick.1.rows = bf16[16,320,512]{2,1,0:T(8,128)(2,1)} custom-call(s32[5120]{0:T(1024)} %g_ref.1, bf16[2,48,256,256]{3,2,1,0:T(8,128)(2,1)} %bitcast.17), custom_call_target="tpu_custom_call" | custom-call | tf_op jit(solution)/shard_map/pick/pallas_call | solution.py:386
  137.7 55.9 %back.1 = f32[320,1024]{1,0:T(8,128)} custom-call(bf16[16,320,512]{2,1,0:T(8,128)(2,1)} %pick.1.rows, bf16[2,8,512,128]{3,2,1,0:T(8,128)(2,1)} %get-tuple-element.8.slab), custom_call_target="tpu_custom_call" | custom-call | tf_op jit(solution)/shard_map/back/pallas_call | solution.py:527
  193.6 2.5 %copy.18 = f32[320,1024]{1,0:T(8,128)} copy(f32[320,1024]{1,0:T(8,128)} %back.1) | data formatting | bytes 2621440
  (23 shorter events, 0.8 us)
Async XLA Ops:
  0.0 22.9 %copy-start = (bf16[16,6,2304]{2,0,1:T(8,128)(2,1)S(1)}, bf16[16,6,2304]{2,0,1:T(8,128)(2,1)}, u32[]{:S(2)}) copy-start(bf16[16,6,2304]{2,0,1:T(8,128)(2,1)} %param.9) | copy-start | bytes 1327108
  3.3 21.3 %copy-start.2 = (f32[256]{0:T(256)}, f32[256]{0:T(256)S(1)}, u32[]{:S(2)}) copy-start(f32[256]{0:T(256)S(1)} %mul.253.weights) | copy-start | bytes 3076
  15.6 9.0 %copy-start.1 = (bf16[16,6,2304]{2,0,1:T(8,128)(2,1)S(1)}, bf16[16,6,2304]{2,0,1:T(8,128)(2,1)}, u32[]{:S(2)}) copy-start(bf16[16,6,2304]{2,0,1:T(8,128)(2,1)} %param.10) | copy-start | bytes 1327108

commit v7 on v6

--- a/solution.py
+++ b/solution.py
@@ -42,7 +42,9 @@
 BLOCKS = 8
 PX = NX // BLOCKS
 PT = 3
+YS = PAIRS + 8
 PB = 16
+MS = PB + 8
 
 
 def density(vf, cbuf, b, plane, at, even, odd):
@@ -65,8 +67,10 @@
         x = b * PX + first + i
         rows = slice(i * PAIRS, i * PAIRS + PAIRS)
         am, cm = a[rows, :LANES], c[rows, :LANES]
-        y[x, 0] = (cosr * am - sinr * cm).astype(jnp.bfloat16)
-        y[x, 1] = (cosr * cm + sinr * am).astype(jnp.bfloat16)
+        to = pl.ds(pl.multiple_of(x * YS, 8), PAIRS)
+        for k, value in enumerate((cosr * am - sinr * cm, cosr * cm + sinr * am)):
+            for h in range(LANES // 128):
+                y[k, h, to, :] = value[:, h * 128 : h * 128 + 128]
         av, cv = a[rows, LANES:], c[rows, LANES:]
         cp, sp = ph[x, 0:1, :], ph[x, 1:2, :]
         real = real + (cp * av - sp * cv)
@@ -77,7 +81,7 @@
 
 def front_kernel(
     weights, cond, val, tc, ts, rot, ph, wide, table, m_out, slab_out,
-    cbuf, vbuf, vf, even, odd, y, sacc, sl, yr, yi, mo, mb,
+    cbuf, vbuf, vf, even, odd, y, sacc, sl, mo, mb,
     lsem, cs, cr, vs, vr, gs, gr, ss, sr, fs, fr, ms,
 ):
     row, col = lax.axis_index("row"), lax.axis_index("col")
@@ -162,11 +166,11 @@
             land_val(3, 3, 4)
             land(2, 5)
             land(1)
+            land(3, 3, 4)
             ready(1)
 
         @pl.when(b == 2)
         def _():
-            land(3, 3, 4)
             land_val(4)
             land_val(5, 6)
             land_val(6)
@@ -180,11 +184,11 @@
         @pl.when(b == 4)
         def _():
             land(4)
+            land(5, 6)
             ready(4)
 
         @pl.when(b == 5)
         def _():
-            land(5, 6)
             land(6)
             ready(5)
 
@@ -247,26 +251,22 @@
         slot = i % 2
         ps = pl.ds(pl.multiple_of(i * PB, PB), PB)
         out = pltpu.make_async_copy(mb.at[slot], m_out.at[:, ps, :], ms.at[slot])
+        for p in range(PB):
+            at = pl.ds(i * PB + p, NX, stride=YS)
+            rhs = jnp.concatenate(
+                [jnp.concatenate([y[k, 0, at, :], y[k, 1, at, :]], axis=1) for k in range(2)], axis=0
+            ).astype(jnp.bfloat16)
+            res = jnp.dot(table[...], rhs, preferred_element_type=jnp.float32) * weights[i * PB + p]
+            for h in range(LANES // 128):
+                mo[h, pl.ds(p, 2 * NX, stride=MS), :] = res[:, h * 128 : h * 128 + 128]
+
+        @pl.when(i >= 2)
+        def _():
+            out.wait()
+
         for h in range(LANES // 128):
             lanes = slice(h * 128, h * 128 + 128)
-            yr[h] = y[:, 0, ps, lanes].astype(jnp.float32).reshape(NX * PB, 128)
-            yi[h] = y[:, 1, ps, lanes].astype(jnp.float32).reshape(NX * PB, 128)
-        for p in range(PB):
-            at = pl.ds(p, NX, stride=PB)
-            real = jnp.concatenate([yr[0, at, :], yr[1, at, :]], axis=1)
-            imag = jnp.concatenate([yi[0, at, :], yi[1, at, :]], axis=1)
-            rhs = jnp.concatenate([real, imag], axis=0).astype(jnp.bfloat16)
-            res = jnp.dot(table[...], rhs, preferred_element_type=jnp.float32) * weights[i * PB + p]
-            for h in range(LANES // 128):
-                mo[h, pl.ds(p, 2 * NX, stride=PB), :] = res[:, h * 128 : h * 128 + 128]
-
-        @pl.when(i >= 2)
-        def _():
-            out.wait()
-
-        for h in range(LANES // 128):
-            lanes = slice(h * 128, h * 128 + 128)
-            mb[slot, :, :, lanes] = mo[h].reshape(2 * NX, PB, 128).astype(jnp.bfloat16)
+            mb[slot, :, :, lanes] = mo[h].reshape(2 * NX, MS, 128)[:, :PB].astype(jnp.bfloat16)
         out.start()
         return carry
 
@@ -307,12 +307,10 @@
             fl(2, PX, NV, HALF),
             bf(PT * PAIRS, HALF),
             bf(PT * PAIRS, HALF),
-            bf(NX, 2, PAIRS, LANES),
+            fl(2, LANES // 128, NX * YS, 128),
             fl(2, PAIRS, JS),
             bf(2 * PAIRS, JS),
-            fl(2, NX * PB, 128),
-            fl(2, NX * PB, 128),
-            fl(2, 2 * NX * PB, 128),
+            fl(2, 2 * NX * MS, 128),
             bf(2, 2 * NX, PB, LANES),
             dma((3,)), dma((7,)), dma((8,)), dma((7,)), dma((8,)),
             dma((24,)), dma((24,)), dma((7,)), dma((7,)), dma((8,)), dma((8,)), dma((2,)),
@@ -329,8 +327,8 @@
 G_DEV = 320
 LO = 192
 HI = G_DEV - LO
-DEPTH = 4
-UNROLL = 16
+DEPTH = 16
+UNROLL = 32
 
 
 def pick_kernel(g_ref, m, out, mt, mi, sel, lhs, ms, os):
@@ -354,7 +352,7 @@
 
         return carry
 
-    lax.fori_loop(0, NX, turn, 0)
+    lax.fori_loop(0, NX, turn, 0, unroll=4)
     store = lambda n: pltpu.make_async_copy(lhs.at[n % 2], out.at[n], os.at[n % 2])
 
     def block(n, carry):
@@ -545,7 +543,7 @@
     )(rows, slab)
 
 
-def places_kernel(mine, out, send_sem, recv_sem):
+def places_kernel(mine, cond, val, out, cond_out, val_out, send_sem, recv_sem):
     row, col = lax.axis_index("row"), lax.axis_index("col")
     barrier = pltpu.get_barrier_semaphore()
     peers = [{"row": (row + k) % 8, "col": col} for k in range(1, 8)]
@@ -561,34 +559,53 @@
         )
         copies[-1].start()
     out[row] = mine[...]
+    r = lax.broadcasted_iota(jnp.int32, (128, 128), 0)
+    c = lax.broadcasted_iota(jnp.int32, (128, 128), 1)
+    back = (r + c == 127).astype(jnp.bfloat16)
+    half = PX // 2
+    cond_out[:, :, :HALF] = cond[:, :, :HALF]
+    for p in range(2):
+        val_out[2 * p] = val[p * half : p * half + half, :, :HALF]
+    for b in range(HALF // 128):
+        source = slice(CELLS - b * 128 - 128, CELLS - b * 128)
+        to = slice(b * 128, b * 128 + 128)
+        flip = lambda ref: jnp.dot(
+            ref[:, :, source].reshape(PX * CL, 128), back, preferred_element_type=jnp.float32
+        ).astype(jnp.bfloat16).reshape(PX, CL, 128)
+        cond_out[:, :, HALF + b * 128 : HALF + b * 128 + 128] = flip(cond)
+        turned = flip(val)
+        for p in range(2):
+            val_out[2 * p + 1, :, :, to] = turned[p * half : p * half + half]
     for copy in copies:
         copy.wait_recv()
     for copy in copies:
         copy.wait_send()
 
 
-def places(mine):
+def places(mine, cond, val):
     return pl.pallas_call(
         places_kernel,
-        in_specs=[pl.BlockSpec(memory_space=pltpu.VMEM)],
-        out_specs=pl.BlockSpec(memory_space=pltpu.VMEM),
-        out_shape=jax.ShapeDtypeStruct((8, G_ROW // 128, 128), jnp.int32),
+        in_specs=[pl.BlockSpec(memory_space=pltpu.VMEM)] * 3,
+        out_specs=[pl.BlockSpec(memory_space=pltpu.VMEM)] * 3,
+        out_shape=[
+            jax.ShapeDtypeStruct((8, G_ROW // 128, 128), jnp.int32),
+            jax.ShapeDtypeStruct((PX, CL, CELLS), jnp.bfloat16),
+            jax.ShapeDtypeStruct((4, PX // 2, NV, HALF), jnp.bfloat16),
+        ],
         scratch_shapes=[pltpu.SemaphoreType.DMA((7,)), pltpu.SemaphoreType.DMA((7,))],
         compiler_params=pltpu.CompilerParams(collective_id=1, has_side_effects=True),
         name="places",
-    )(mine)
+    )(mine, cond, val)
 
 
 def body(psi_val, psi_cond, energy_val, energy_cond, stick_map, gvec_map, slab_index):
     row = lax.axis_index("row")
-    fold = lambda psi: (psi[:, :, :HALF], jnp.flip(psi[:, :, HALF:], axis=2))
-    cond = jnp.concatenate(fold(psi_cond.transpose(1, 0, 2)), axis=2)
-    val = jnp.stack([half.reshape(2, PX // 2, NV, HALF) for half in fold(psi_val.transpose(1, 0, 2))], axis=1)
-    val = val.reshape(4, PX // 2, NV, HALF)
-
     mine = lax.dynamic_slice(stick_map, (row * STK,), (STK,))
     cols = lax.dynamic_slice(slab_index, (row * JS,), (JS,))
-    maps = places(gvec_map.reshape(G_ROW // 128, 128)).reshape(-1)
+    maps, cond, val = places(
+        gvec_map.reshape(G_ROW // 128, 128), psi_cond.transpose(1, 0, 2), psi_val.transpose(1, 0, 2)
+    )
+    maps = maps.reshape(-1)
     place = jnp.take(maps, cols)
     col_kx = place // STK
     col_stick = jnp.take(stick_map, cols // G_ROW * STK + place % STK)

time: 197 us -> 179 us (0.909)
  Pallas kernels: 176 us -> 163 us
  local copies, waits for them, and re-layouts: 9.61 us -> 7.26 us
    pallas_call x1, Pallas kernels: 86.8 us -> 79.6 us  [front(): pl.pallas_call(front_kernel, in_specs=[pl.BlockSpec(memory_space=pltpu.SM...]
    pallas_call x1, Pallas kernels: 22.8 us -> 15.7 us  [pick(): pl.pallas_call(pick_kernel, in_specs=[pl.BlockSpec(memory_space=pltpu.SME...]
where the time goes in v7:
time: 179 us
  Pallas kernels  163 us (91%)
  other arithmetic  8.54 us (5%)
  local copies, waits for them, and re-layouts  7.26 us (4%)
    pallas_call x1, Pallas kernels, front(): pl.pallas_call(front_kernel, in_specs=[pl.BlockSpec(memory_space=pltpu.SM...  79.6 us
    pallas_call x1, Pallas kernels, back(): pl.pallas_call(back_kernel, in_specs=[pl.BlockSpec(memory_space=pl.ANY),...  56.2 us
    pallas_call x1, Pallas kernels, pick(): pl.pallas_call(pick_kernel, in_specs=[pl.BlockSpec(memory_space=pltpu.SME...  15.7 us
    pallas_call x1, Pallas kernels, places(): pl.pallas_call(places_kernel, in_specs=[pl.BlockSpec(memory_space=pltpu.V...  11.5 us

profile of v7, /device:TPU:1, one launch (start us, length us, event | category | flops | bytes accessed | tf_op | source)
XLA Modules:
  0.0 178.8 jit_solution(11966310111650508214)
XLA Ops:
  0.0 0.7 fusion.33
  0.7 0.8 dynamic_slice.6
  1.5 0.8 compare_select_fusion.1
  2.4 0.8 sqrt_multiply_fusion
  3.2 0.1 fusion.20
  3.4 0.7 maximum_maximum_fusion.table
  4.1 0.8 broadcast_in_dim.22.wide
  4.8 11.5 %places.1 = (s32[8,40,128]{2,1,0:T(8,128)}, bf16[6,16,2304]{2,1,0:T(8,128)(2,1)}, bf16[4,3,16,1152]{3,2,1,0:T(8,128)(2,1)}) custom-call(s32[40,128]{1,0:T(8,128)} %bitcast.17, bf16[6,16,2304]{2,1,0:T(8,128)(2,1)} %bitcast.14, bf16[6,16,2304]{2,1,0:T(8,128)(2,1)} %bitcast.15), custom_call_target="tpu_custom_call" | custom-call | tf_op jit(solution)/shard_map/places/pallas_call | solution.py:586
  16.3 1.8 %gather_fusion = s32[128]{0:T(128)S(1)} fusion(s32[40960]{0:T(1024)} %bitcast.13, s32[1024]{0:T(1024)S(1)} %pad_clamp_fusion.1), kind=kCustom, calls=%fused_computation | custom fusion | bytes 1536 | tf_op jit(solution)/shard_map/jit(_take)/gather | solution.py:609
  18.2 0.8 and_select_fusion
  19.0 1.1 gather_fusion.1
  20.2 0.1 add_select_fusion.5
  20.2 0.1 fusion.26
  20.4 0.6 pad_maximum_fusion.1.rot
  21.0 0.1 fusion.14
  21.1 0.7 multiply_cosine_fusion
  21.8 0.7 pad_maximum_fusion.ph
  22.5 0.2 fusion.12
  22.7 0.4 fusion.5
  23.1 1.8 negate_convert_fusion
  24.9 79.6 %front.1 = (bf16[96,256,256]{2,1,0:T(8,128)(2,1)}, bf16[2,8,512,128]{3,2,1,0:T(8,128)(2,1)}) custom-call(f32[256]{0:T(256)} %copy-done.1, bf16[6,16,2304]{2,1,0:T(8,128)(2,1)} %get-tuple-element.10.cond, bf16[4,3,16,1152]{3,2,1,0:T(8,128)(2,1)} %get-tuple-element.11.val, bf16[1152,384]{1,0:T(8,128)(2,1)} %bitcast.12, bf16[1152,384]{1,0:T(8,128)(2,1)} %bitcast.11, ...), custom_call_target="tpu_custom_call" | custom-call | tf_op jit(solution)/shard_map/front/pallas_call | solution.py:296
  104.4 15.7 %pick.1.rows = bf16[16,320,512]{2,1,0:T(8,128)(2,1)} custom-call(s32[5120]{0:T(1024)} %g_ref.1, bf16[2,48,256,256]{3,2,1,0:T(8,128)(2,1)} %bitcast.10), custom_call_target="tpu_custom_call" | custom-call | tf_op jit(solution)/shard_map/pick/pallas_call | solution.py:384
  120.1 56.2 %back.1 = f32[320,1024]{1,0:T(8,128)} custom-call(bf16[16,320,512]{2,1,0:T(8,128)(2,1)} %pick.1.rows, bf16[2,8,512,128]{3,2,1,0:T(8,128)(2,1)} %get-tuple-element.14.slab), custom_call_target="tpu_custom_call" | custom-call | tf_op jit(solution)/shard_map/back/pallas_call | solution.py:525
  176.3 2.5 %copy.12 = f32[320,1024]{1,0:T(8,128)} copy(f32[320,1024]{1,0:T(8,128)} %back.1) | data formatting | bytes 2621440
  (15 shorter events, 0.3 us)
Async XLA Ops:
  0.0 19.0 %copy-start = (s32[1536]{0:T(1024)S(1)}, s32[1536]{0:T(1024)}, u32[]{:S(2)}) copy-start(s32[1536]{0:T(1024)} %param.13) | copy-start | bytes 18436
  3.2 21.6 %copy-start.1 = (f32[256]{0:T(256)}, f32[256]{0:T(256)S(1)}, u32[]{:S(2)}) copy-start(f32[256]{0:T(256)S(1)} %mul.253.weights) | copy-start | bytes 3076

commit v8 on v7

--- a/solution.py
+++ b/solution.py
@@ -26,17 +26,31 @@
 MESH = pl.DeviceIdType.MESH
 
 
-def half_phase(ky, kz):
-    unit = math.pi / 48.0
-    y = 2 * jnp.arange(NY // 2, dtype=jnp.int32) + 1
-    z = 2 * jnp.arange(NZ, dtype=jnp.int32) + 1
-    ay = ((y[:, None] * ky[None, :]) % 96).astype(jnp.float32) * unit
-    az = ((z[:, None] * kz[None, :]) % 96).astype(jnp.float32) * unit
-    cy, sy = jnp.cos(ay)[:, None, :], jnp.sin(ay)[:, None, :]
-    cz, sz = jnp.cos(az)[None, :, :], jnp.sin(az)[None, :, :]
-    cos = (cy * cz - sy * sz).reshape(HALF, -1)
-    sin = -(sy * cz + cy * sz).reshape(HALF, -1)
-    return cos.astype(jnp.bfloat16), sin.astype(jnp.bfloat16)
+def turn_angle(t):
+    return (t - 96.0 * jnp.floor((t + 0.5) * (1.0 / 96.0))) * (math.pi / 48.0)
+
+
+def make_tables(ks, rows_of_blocks, tc, ts, rot, ph):
+    width = LANES + JS
+    ky, kz = ks[0:1, :], ks[1:2, :]
+    odd = lambda n: 2.0 * lax.broadcasted_iota(jnp.int32, (n, width), 0).astype(jnp.float32) + 1.0
+    ay, az = turn_angle(odd(NY // 2) * ky), turn_angle(odd(NZ) * kz)
+    cy, sy, cz, sz = jnp.cos(ay), jnp.sin(ay), jnp.cos(az), jnp.sin(az)
+    for y in range(NY // 2):
+        to = slice(y * NZ, y * NZ + NZ)
+        tc[to, :] = (cy[y : y + 1, :] * cz - sy[y : y + 1, :] * sz).astype(jnp.bfloat16)
+        ts[to, :] = -(sy[y : y + 1, :] * cz + cy[y : y + 1, :] * sz).astype(jnp.bfloat16)
+    shift = turn_angle(ky + kz)
+    rot[0:1, :] = jnp.cos(shift[:, :LANES])
+    rot[1:2, :] = jnp.sin(shift[:, :LANES])
+    plane = lax.broadcasted_iota(jnp.int32, (NX, JS), 0)
+    xs = plane
+    for b, block_row in enumerate(rows_of_blocks):
+        inside = (plane >= b * PX) & (plane < b * PX + PX)
+        xs = jnp.where(inside, plane + (block_row - b) * PX, xs)
+    theta = turn_angle((ky + kz)[:, LANES:] - 2.0 * xs.astype(jnp.float32) * ks[2:3, LANES:])
+    ph[0] = jnp.cos(theta)
+    ph[1] = jnp.sin(theta)
 
 
 BLOCKS = 8
@@ -72,7 +86,7 @@
             for h in range(LANES // 128):
                 y[k, h, to, :] = value[:, h * 128 : h * 128 + 128]
         av, cv = a[rows, LANES:], c[rows, LANES:]
-        cp, sp = ph[x, 0:1, :], ph[x, 1:2, :]
+        cp, sp = ph[0, pl.ds(x, 1), :], ph[1, pl.ds(x, 1), :]
         real = real + (cp * av - sp * cv)
         imag = imag + (cp * cv + sp * av)
     sacc[0] = real
@@ -80,8 +94,8 @@
 
 
 def front_kernel(
-    weights, cond, val, tc, ts, rot, ph, wide, table, m_out, slab_out,
-    cbuf, vbuf, vf, even, odd, y, sacc, sl, mo, mb,
+    weights, cond, val, ks, wide, table, m_out, slab_out,
+    tc, ts, rot, ph, cbuf, vbuf, vf, even, odd, y, sacc, sl, mo, mb,
     lsem, cs, cr, vs, vr, gs, gr, ss, sr, fs, fr, ms,
 ):
     row, col = lax.axis_index("row"), lax.axis_index("col")
@@ -155,6 +169,8 @@
     for n in range(3):
         cond_hop(n).start()
     sacc[...] = jnp.zeros_like(sacc)
+    steps = [(0, 0), (0, 1), (0, 3), (1, 0), (0, 2), (1, 1), (1, 3), (1, 2)]
+    make_tables(ks, [(yh + dy) % 2 * 4 + (x + dx) % 4 for dy, dx in steps], tc, ts, rot, ph)
     for copy in own:
         copy.wait()
 
@@ -287,7 +303,7 @@
             spread(b, j).wait_send()
 
 
-def front(weights, cond, val, tc, ts, rot, ph, wide, table):
+def front(weights, cond, val, ks, wide, table):
     dma = pltpu.SemaphoreType.DMA
     vmem = pl.BlockSpec(memory_space=pltpu.VMEM)
     hbm = pl.BlockSpec(memory_space=pl.ANY)
@@ -295,13 +311,17 @@
     fl = lambda *shape: pltpu.VMEM(shape, jnp.float32)
     return pl.pallas_call(
         front_kernel,
-        in_specs=[pl.BlockSpec(memory_space=pltpu.SMEM)] + [vmem] * 8,
+        in_specs=[pl.BlockSpec(memory_space=pltpu.SMEM)] + [vmem] * 5,
         out_specs=[hbm, hbm],
         out_shape=[
             jax.ShapeDtypeStruct((2 * NX, PAIRS, LANES), jnp.bfloat16),
             jax.ShapeDtypeStruct((2, BLOCKS, 2 * PAIRS, JS), jnp.bfloat16),
         ],
         scratch_shapes=[
+            bf(HALF, LANES + JS),
+            bf(HALF, LANES + JS),
+            fl(2, LANES),
+            fl(2, NX, JS),
             bf(BLOCKS, PX, CL, CELLS),
             bf(BLOCKS, 4, PX // 2, NV, HALF),
             fl(2, PX, NV, HALF),
@@ -319,7 +339,7 @@
             collective_id=2, has_side_effects=True, vmem_limit_bytes=VMEM_LIMIT
         ),
         name="front",
-    )(weights, cond, val, tc, ts, rot, ph, wide, table)
+    )(weights, cond, val, ks, wide, table)
 
 
 GB = 320
@@ -612,18 +632,12 @@
     pad = jnp.zeros((LANES - STK,), jnp.int32)
     flat = jnp.concatenate([mine, pad, col_stick])
     ky, kz = flat // NZ, flat % NZ
-    tc, ts = half_phase(ky, kz)
-    turn = ((ky + kz) % 96).astype(jnp.float32) * (math.pi / 48.0)
-    rot = jnp.stack([jnp.cos(turn[:LANES]), jnp.sin(turn[:LANES])])
+    full_kx = jnp.concatenate([jnp.zeros((LANES,), jnp.int32), col_kx])
+    ks = jnp.stack([ky, kz, full_kx]).astype(jnp.float32)
     dy = jnp.array([0, 0, 0, 1, 0, 1, 1, 1], jnp.int32)
     dx = jnp.array([0, 1, 3, 0, 2, 1, 3, 2], jnp.int32)
     source = (row // 4 + dy) % 2 * 4 + (row % 4 + dx) % 4
     xs = (source[:, None] * PX + jnp.arange(PX, dtype=jnp.int32)[None, :]).reshape(NX)
-    theta = (
-        ((ky + kz)[None, LANES:] - 2 * (xs[:, None] * col_kx[None, :]) + 96 * NX) % 96
-    ).astype(jnp.float32) * (math.pi / 48.0)
-    ph = jnp.stack([jnp.cos(theta), jnp.sin(theta)], axis=1)
-
     weight = jnp.sqrt(2.0 / (energy_cond[None, :] - energy_val[:, None])) * (
         1.0 / (math.sqrt(NY * NZ) * math.sqrt(NX))
     )
@@ -636,7 +650,7 @@
         [jnp.concatenate([cx, sx], axis=1), jnp.concatenate([-sx, cx], axis=1)], axis=0
     ).astype(jnp.bfloat16)
 
-    m, slab = front(weight, cond, val, tc, ts, rot, ph, wide, table)
+    m, slab = front(weight, cond, val, ks, wide, table)
     return back(pick(gvec_map, m.reshape(2, NX, PAIRS, LANES)), slab)
 
 

time: 179 us -> 175 us (0.978)
  other arithmetic: 8.54 us -> 4.53 us
where the time goes in v8:
time: 175 us
  Pallas kernels  163 us (93%)
  local copies, waits for them, and re-layouts  7.3 us (4%)
  other arithmetic  4.53 us (3%)
    pallas_call x1, Pallas kernels, front(): pl.pallas_call(front_kernel, in_specs=[pl.BlockSpec(memory_space=pltpu.SM...  79.2 us
    pallas_call x1, Pallas kernels, back(): pl.pallas_call(back_kernel, in_specs=[pl.BlockSpec(memory_space=pl.ANY),...  56.3 us
    pallas_call x1, Pallas kernels, pick(): pl.pallas_call(pick_kernel, in_specs=[pl.BlockSpec(memory_space=pltpu.SME...  15.7 us
    pallas_call x1, Pallas kernels, places(): pl.pallas_call(places_kernel, in_specs=[pl.BlockSpec(memory_space=pltpu.V...  11.6 us

profile of v8, /device:TPU:1, one launch (start us, length us, event | category | flops | bytes accessed | tf_op | source)
XLA Modules:
  0.0 174.7 jit_solution(14385365187970689960)
XLA Ops:
  0.0 0.0 copy-start
  0.0 0.7 fusion.13
  0.7 0.8 dynamic_slice.6
  1.5 0.8 compare_select_fusion.1
  2.2 0.1 pad.9.clone
  2.3 0.1 iota_add_fusion
  2.4 0.1 add.132
  2.5 0.8 sqrt_multiply_fusion
  3.2 0.1 mul.54.weights
  3.3 0.0 copy-start.1
  3.3 0.1 fusion.5
  3.4 0.7 maximum_maximum_fusion.table
  4.1 0.8 broadcast_in_dim.32.wide
  4.9 11.6 %places.1 = (s32[8,40,128]{2,1,0:T(8,128)}, bf16[6,16,2304]{2,1,0:T(8,128)(2,1)}, bf16[4,3,16,1152]{3,2,1,0:T(8,128)(2,1)}) custom-call(s32[40,128]{1,0:T(8,128)} %bitcast.12, bf16[6,16,2304]{2,1,0:T(8,128)(2,1)} %bitcast.10, bf16[6,16,2304]{2,1,0:T(8,128)(2,1)} %bitcast.11), custom_call_target="tpu_custom_call" | custom-call | tf_op jit(solution)/shard_map/places/pallas_call | solution.py:606
  16.5 1.8 %gather_fusion = s32[128]{0:T(128)S(1)} fusion(s32[40960]{0:T(1024)} %bitcast.9, s32[1024]{0:T(1024)S(1)} %pad_clamp_fusion.1), kind=kCustom, calls=%fused_computation | custom fusion | bytes 1536 | tf_op jit(solution)/shard_map/jit(_take)/gather | solution.py:629
  18.3 0.8 compare_select_fusion
  19.1 0.0 copy-done
  19.1 1.1 gather_fusion.1
  20.4 0.6 add_convert_fusion.ks
  21.0 0.0 copy-done.1
  21.0 79.2 %front.1 = (bf16[96,256,256]{2,1,0:T(8,128)(2,1)}, bf16[2,8,512,128]{3,2,1,0:T(8,128)(2,1)}) custom-call(f32[256]{0:T(256)} %copy-done.1, bf16[6,16,2304]{2,1,0:T(8,128)(2,1)} %get-tuple-element.10.cond, bf16[4,3,16,1152]{3,2,1,0:T(8,128)(2,1)} %get-tuple-element.11.val, f32[3,384]{1,0:T(4,128)} %add_convert_fusion.ks, f32[256,128]{1,0:T(8,128)} %broadcast_in_dim.32.wide, ...), custom_call_target="tpu_custom_call" | custom-call | tf_op jit(solution)/shard_map/front/pallas_call | solution.py:312
  100.2 15.7 %pick.1.rows = bf16[16,320,512]{2,1,0:T(8,128)(2,1)} custom-call(s32[5120]{0:T(1024)} %g_ref.1, bf16[2,48,256,256]{3,2,1,0:T(8,128)(2,1)} %bitcast.8), custom_call_target="tpu_custom_call" | custom-call | tf_op jit(solution)/shard_map/pick/pallas_call | solution.py:404
  115.9 56.3 %back.1 = f32[320,1024]{1,0:T(8,128)} custom-call(bf16[16,320,512]{2,1,0:T(8,128)(2,1)} %pick.1.rows, bf16[2,8,512,128]{3,2,1,0:T(8,128)(2,1)} %get-tuple-element.14.slab), custom_call_target="tpu_custom_call" | custom-call | tf_op jit(solution)/shard_map/back/pallas_call | solution.py:545
  172.2 2.5 %copy.11 = f32[320,1024]{1,0:T(8,128)} copy(f32[320,1024]{1,0:T(8,128)} %back.1) | data formatting | bytes 2621440
  (8 shorter events, 0.1 us)
Async XLA Ops:
  0.0 19.1 %copy-start = (s32[1536]{0:T(1024)S(1)}, s32[1536]{0:T(1024)}, u32[]{:S(2)}) copy-start(s32[1536]{0:T(1024)} %param.13) | copy-start | bytes 18436
  3.3 17.7 %copy-start.1 = (f32[256]{0:T(256)}, f32[256]{0:T(256)S(1)}, u32[]{:S(2)}) copy-start(f32[256]{0:T(256)S(1)} %mul.54.weights) | copy-start | bytes 3076

commit v9 on v8

--- a/solution.py
+++ b/solution.py
@@ -94,7 +94,7 @@
 
 
 def front_kernel(
-    weights, cond, val, ks, wide, table, m_out, slab_out,
+    weights, cond, val, near_cond, near_val, ks, wide, table, m_out, slab_out,
     tc, ts, rot, ph, cbuf, vbuf, vf, even, odd, y, sacc, sl, mo, mb,
     lsem, cs, cr, vs, vr, gs, gr, ss, sr, fs, fr, ms,
 ):
@@ -104,8 +104,6 @@
     zo = z + 1 - 2 * (z % 2)
     xp = {"row": yh * 4 + (x + 1) % 4, "col": col}
     xm = {"row": yh * 4 + (x + 3) % 4, "col": col}
-    yc = {"row": (1 - yh) * 4 + x, "col": col}
-    yv = {"row": (1 - yh) * 4 + x, "col": z * 4 + (1 - yl) * 2 + core}
     group = [
         {"row": row, "col": zo * 4 + yl * 2 + core},
         {"row": row, "col": z * 4 + yl * 2 + 1 - core},
@@ -117,29 +115,30 @@
     own = [
         pltpu.make_async_copy(cond, cbuf.at[0], lsem.at[0]),
         pltpu.make_async_copy(val, vbuf.at[0], lsem.at[1]),
+        pltpu.make_async_copy(near_cond, cbuf.at[pl.ds(1, 3)], lsem.at[2]),
     ]
+    for k in range(3):
+        own.append(pltpu.make_async_copy(near_val.at[k], vbuf.at[k + 1, part], lsem.at[3 + k]))
     for copy in own:
         copy.start()
     barrier = pltpu.get_barrier_semaphore()
-    for peer in across + group + [yv]:
+    for peer in across + group:
         pl.semaphore_signal(barrier, inc=1, device_id=peer, device_id_type=MESH)
-    pl.semaphore_wait(barrier, 11)
-
-    hops = [(0, 3, None), (0, 2, xp), (0, 1, xm), (3, 6, xp), (3, 5, xm), (2, 4, xp), (5, 7, xm)]
+    pl.semaphore_wait(barrier, 10)
+
+    hops = [(3, 6, xp), (3, 5, xm), (2, 4, xp), (5, 7, xm)]
     hop_to = [hop[1] for hop in hops]
 
     def cond_hop(n):
         src, dst, peer = hops[n]
         return pltpu.make_async_remote_copy(
-            cbuf.at[src] if src else cond, cbuf.at[dst], cs.at[n], cr.at[dst],
-            device_id=peer or yc, device_id_type=MESH,
+            cbuf.at[src], cbuf.at[dst], cs.at[n], cr.at[dst], device_id=peer, device_id_type=MESH
         )
 
     def val_hop(n):
         src, dst, peer = hops[n]
         return pltpu.make_async_remote_copy(
-            vbuf.at[src, part] if src else val.at[part], vbuf.at[dst, part], vs.at[n], vr.at[dst],
-            device_id=peer or yv, device_id_type=MESH,
+            vbuf.at[src, part], vbuf.at[dst, part], vs.at[n], vr.at[dst], device_id=peer, device_id_type=MESH
         )
 
     def spread(b, j):
@@ -164,52 +163,49 @@
         for j in range(3):
             spread(b, j).wait_recv()
 
+    for copy in own:
+        copy.wait()
     for n in range(3):
         val_hop(n).start()
-    for n in range(3):
+    for n in (1, 2, 0):
         cond_hop(n).start()
+    for b in range(1, 4):
+        for j in range(3):
+            spread(b, j).start()
     sacc[...] = jnp.zeros_like(sacc)
     steps = [(0, 0), (0, 1), (0, 3), (1, 0), (0, 2), (1, 1), (1, 3), (1, 2)]
     make_tables(ks, [(yh + dy) % 2 * 4 + (x + dx) % 4 for dy, dx in steps], tc, ts, rot, ph)
-    for copy in own:
-        copy.wait()
 
     def block(b, carry):
         @pl.when(b == 1)
         def _():
-            land_val(1)
-            land_val(2, 5)
-            land_val(3, 3, 4)
-            land(2, 5)
-            land(1)
-            land(3, 3, 4)
             ready(1)
+            land_val(5, 3)
+            land_val(4)
+            land_val(6)
 
         @pl.when(b == 2)
         def _():
-            land_val(4)
-            land_val(5, 6)
-            land_val(6)
             ready(2)
+            land_val(7)
+            land(5, 3)
 
         @pl.when(b == 3)
         def _():
-            land_val(7)
             ready(3)
 
         @pl.when(b == 4)
         def _():
             land(4)
-            land(5, 6)
             ready(4)
 
         @pl.when(b == 5)
         def _():
+            ready(5)
+
+        @pl.when(b == 6)
+        def _():
             land(6)
-            ready(5)
-
-        @pl.when(b == 6)
-        def _():
             ready(6)
 
         @pl.when(b == 7)
@@ -237,7 +233,7 @@
 
     for h in range(2):
         sl[h * PAIRS : h * PAIRS + PAIRS, :] = (sacc[h] * wide[...]).astype(jnp.bfloat16)
-    keep = pltpu.make_async_copy(sl, slab_out.at[0, row], lsem.at[2])
+    keep = pltpu.make_async_copy(sl, slab_out.at[0, row], lsem.at[6])
     keep.start()
 
     def push(k):
@@ -303,7 +299,7 @@
             spread(b, j).wait_send()
 
 
-def front(weights, cond, val, ks, wide, table):
+def front(weights, cond, val, near_cond, near_val, ks, wide, table):
     dma = pltpu.SemaphoreType.DMA
     vmem = pl.BlockSpec(memory_space=pltpu.VMEM)
     hbm = pl.BlockSpec(memory_space=pl.ANY)
@@ -311,7 +307,7 @@
     fl = lambda *shape: pltpu.VMEM(shape, jnp.float32)
     return pl.pallas_call(
         front_kernel,
-        in_specs=[pl.BlockSpec(memory_space=pltpu.SMEM)] + [vmem] * 5,
+        in_specs=[pl.BlockSpec(memory_space=pltpu.SMEM)] + [hbm] * 4 + [vmem] * 3,
         out_specs=[hbm, hbm],
         out_shape=[
             jax.ShapeDtypeStruct((2 * NX, PAIRS, LANES), jnp.bfloat16),
@@ -332,14 +328,14 @@
             bf(2 * PAIRS, JS),
             fl(2, 2 * NX * MS, 128),
             bf(2, 2 * NX, PB, LANES),
-            dma((3,)), dma((7,)), dma((8,)), dma((7,)), dma((8,)),
+            dma((7,)), dma((4,)), dma((8,)), dma((4,)), dma((8,)),
             dma((24,)), dma((24,)), dma((7,)), dma((7,)), dma((8,)), dma((8,)), dma((2,)),
         ],
         compiler_params=pltpu.CompilerParams(
             collective_id=2, has_side_effects=True, vmem_limit_bytes=VMEM_LIMIT
         ),
         name="front",
-    )(weights, cond, val, ks, wide, table)
+    )(weights, cond, val, near_cond, near_val, ks, wide, table)
 
 
 GB = 320
@@ -563,22 +559,21 @@
     )(rows, slab)
 
 
-def places_kernel(mine, cond, val, out, cond_out, val_out, send_sem, recv_sem):
+def places_kernel(
+    mine, cond, val, out, cond_out, val_out, near_cond, near_val, send_sem, recv_sem, cs, cr, vs, vr
+):
     row, col = lax.axis_index("row"), lax.axis_index("col")
+    yh, x = row // 4, row % 4
+    z, yl, core = col // 4, (col // 2) % 2, col % 2
+    part = core * 2 + z % 2
     barrier = pltpu.get_barrier_semaphore()
     peers = [{"row": (row + k) % 8, "col": col} for k in range(1, 8)]
-    for peer in peers:
+    xp = {"row": yh * 4 + (x + 1) % 4, "col": col}
+    xm = {"row": yh * 4 + (x + 3) % 4, "col": col}
+    yc = {"row": (1 - yh) * 4 + x, "col": col}
+    yv = {"row": (1 - yh) * 4 + x, "col": z * 4 + (1 - yl) * 2 + core}
+    for peer in peers + [yv]:
         pl.semaphore_signal(barrier, inc=1, device_id=peer, device_id_type=MESH)
-    pl.semaphore_wait(barrier, 7)
-    copies = []
-    for k, peer in enumerate(peers):
-        copies.append(
-            pltpu.make_async_remote_copy(
-                mine, out.at[row], send_sem.at[k], recv_sem.at[k], device_id=peer, device_id_type=MESH
-            )
-        )
-        copies[-1].start()
-    out[row] = mine[...]
     r = lax.broadcasted_iota(jnp.int32, (128, 128), 0)
     c = lax.broadcasted_iota(jnp.int32, (128, 128), 1)
     back = (r + c == 127).astype(jnp.bfloat16)
@@ -596,6 +591,29 @@
         turned = flip(val)
         for p in range(2):
             val_out[2 * p + 1, :, :, to] = turned[p * half : p * half + half]
+    pl.semaphore_wait(barrier, 8)
+    copies = []
+    for k, peer in enumerate(peers):
+        copies.append(
+            pltpu.make_async_remote_copy(
+                mine, out.at[row], send_sem.at[k], recv_sem.at[k], device_id=peer, device_id_type=MESH
+            )
+        )
+    for k, peer in enumerate((xm, xp, yv)):
+        copies.append(
+            pltpu.make_async_remote_copy(
+                val_out.at[part], near_val.at[k], vs.at[k], vr.at[k], device_id=peer, device_id_type=MESH
+            )
+        )
+    for k, peer in enumerate((xm, xp, yc)):
+        copies.append(
+            pltpu.make_async_remote_copy(
+                cond_out, near_cond.at[k], cs.at[k], cr.at[k], device_id=peer, device_id_type=MESH
+            )
+        )
+    for copy in copies:
+        copy.start()
+    out[row] = mine[...]
     for copy in copies:
         copy.wait_recv()
     for copy in copies:
@@ -606,13 +624,15 @@
     return pl.pallas_call(
         places_kernel,
         in_specs=[pl.BlockSpec(memory_space=pltpu.VMEM)] * 3,
-        out_specs=[pl.BlockSpec(memory_space=pltpu.VMEM)] * 3,
+        out_specs=[pl.BlockSpec(memory_space=pltpu.VMEM)] * 5,
         out_shape=[
             jax.ShapeDtypeStruct((8, G_ROW // 128, 128), jnp.int32),
             jax.ShapeDtypeStruct((PX, CL, CELLS), jnp.bfloat16),
             jax.ShapeDtypeStruct((4, PX // 2, NV, HALF), jnp.bfloat16),
+            jax.ShapeDtypeStruct((3, PX, CL, CELLS), jnp.bfloat16),
+            jax.ShapeDtypeStruct((3, PX // 2, NV, HALF), jnp.bfloat16),
         ],
-        scratch_shapes=[pltpu.SemaphoreType.DMA((7,)), pltpu.SemaphoreType.DMA((7,))],
+        scratch_shapes=[pltpu.SemaphoreType.DMA((n,)) for n in (7, 7, 3, 3, 3, 3)],
         compiler_params=pltpu.CompilerParams(collective_id=1, has_side_effects=True),
         name="places",
     )(mine, cond, val)
@@ -622,7 +642,7 @@
     row = lax.axis_index("row")
     mine = lax.dynamic_slice(stick_map, (row * STK,), (STK,))
     cols = lax.dynamic_slice(slab_index, (row * JS,), (JS,))
-    maps, cond, val = places(
+    maps, *near = places(
         gvec_map.reshape(G_ROW // 128, 128), psi_cond.transpose(1, 0, 2), psi_val.transpose(1, 0, 2)
     )
     maps = maps.reshape(-1)
@@ -650,7 +670,7 @@
         [jnp.concatenate([cx, sx], axis=1), jnp.concatenate([-sx, cx], axis=1)], axis=0
     ).astype(jnp.bfloat16)
 
-    m, slab = front(weight, cond, val, ks, wide, table)
+    m, slab = front(weight, *near, ks, wide, table)
     return back(pick(gvec_map, m.reshape(2, NX, PAIRS, LANES)), slab)
 
 

time: 175 us -> 177 us (1.011)
  Pallas kernels: 163 us -> 165 us
    pallas_call x1, Pallas kernels: 11.6 us -> 24.2 us  [places(): pl.pallas_call(places_kernel, in_specs=[pl.BlockSpec(memory_space=pltpu.V...]
    pallas_call x1, Pallas kernels: 79.2 us -> 71.8 us  [front(): pl.pallas_call(front_kernel, in_specs=[pl.BlockSpec(memory_space=pltpu.SM...]
    pallas_call x1, Pallas kernels: 56.3 us -> 52.9 us  [back(): pl.pallas_call(back_kernel, in_specs=[pl.BlockSpec(memory_space=pl.ANY),...]
where the time goes in v9:
time: 177 us
  Pallas kernels  165 us (93%)
  local copies, waits for them, and re-layouts  7.3 us (4%)
  other arithmetic  4.54 us (3%)
    pallas_call x1, Pallas kernels, front(): pl.pallas_call(front_kernel, in_specs=[pl.BlockSpec(memory_space=pltpu.SM...  71.8 us
    pallas_call x1, Pallas kernels, back(): pl.pallas_call(back_kernel, in_specs=[pl.BlockSpec(memory_space=pl.ANY),...  52.9 us
    pallas_call x1, Pallas kernels, places(): pl.pallas_call(places_kernel, in_specs=[pl.BlockSpec(memory_space=pltpu.V...  24.2 us
    pallas_call x1, Pallas kernels, pick(): pl.pallas_call(pick_kernel, in_specs=[pl.BlockSpec(memory_space=pltpu.SME...  15.7 us

profile of v9, /device:TPU:1, one launch (start us, length us, event | category | flops | bytes accessed | tf_op | source)
XLA Modules:
  0.0 176.5 jit_solution(14253740993060652167)
XLA Ops:
  0.0 0.0 copy-start
  0.0 0.7 fusion.13
  0.7 0.8 dynamic_slice.6
  1.5 0.8 compare_select_fusion.1
  2.2 0.1 pad.9.clone
  2.3 0.1 iota_add_fusion
  2.4 0.1 add.132
  2.5 0.8 sqrt_multiply_fusion
  3.2 0.1 mul.54.weights
  3.3 0.0 copy-start.1
  3.3 0.1 fusion.5
  3.4 0.7 maximum_maximum_fusion.table
  4.1 0.8 broadcast_in_dim.32.wide
  4.9 24.2 %places.1 = (s32[8,40,128]{2,1,0:T(8,128)}, bf16[6,16,2304]{2,1,0:T(8,128)(2,1)}, bf16[4,3,16,1152]{3,2,1,0:T(8,128)(2,1)}, bf16[3,6,16,2304]{3,2,1,0:T(8,128)(2,1)}, bf16[3,3,16,1152]{3,2,1,0:T(8,128)(2,1)}) custom-call(s32[40,128]{1,0:T(8,128)} %bitcast.12, bf16[6,16,2304]{2,1,0:T(8,128)(2,1)} %bitcast.10, bf16[6,16,2304]{2,1,0:T(8,128)(2,1)} %bitcast.11), custom_call_target="tpu_custom_call" | custom-call | tf_op jit(solution)/shard_map/places/pallas_call | solution.py:624
  29.1 1.8 %gather_fusion = s32[128]{0:T(128)S(1)} fusion(s32[40960]{0:T(1024)} %bitcast.9, s32[1024]{0:T(1024)S(1)} %pad_clamp_fusion.1), kind=kCustom, calls=%fused_computation | custom fusion | bytes 1536 | tf_op jit(solution)/shard_map/jit(_take)/gather | solution.py:649
  30.9 0.8 compare_select_fusion
  31.8 0.0 copy-done
  31.8 1.1 gather_fusion.1
  33.0 0.6 add_convert_fusion.ks
  33.6 0.0 copy-done.1
  33.6 71.8 %front.1 = (bf16[96,256,256]{2,1,0:T(8,128)(2,1)}, bf16[2,8,512,128]{3,2,1,0:T(8,128)(2,1)}) custom-call(f32[256]{0:T(256)} %copy-done.1, bf16[6,16,2304]{2,1,0:T(8,128)(2,1)} %get-tuple-element.12.cond, bf16[4,3,16,1152]{3,2,1,0:T(8,128)(2,1)} %get-tuple-element.13.val, bf16[3,6,16,2304]{3,2,1,0:T(8,128)(2,1)} %get-tuple-element.14.near_cond, ...), custom_call_target="tpu_custom_call" | custom-call | tf_op jit(solution)/shard_map/front/pallas_call | solution.py:308
  105.4 15.7 %pick.1.rows = bf16[16,320,512]{2,1,0:T(8,128)(2,1)} custom-call(s32[5120]{0:T(1024)} %g_ref.1, bf16[2,48,256,256]{3,2,1,0:T(8,128)(2,1)} %bitcast.8), custom_call_target="tpu_custom_call" | custom-call | tf_op jit(solution)/shard_map/pick/pallas_call | solution.py:400
  121.1 52.9 %back.1 = f32[320,1024]{1,0:T(8,128)} custom-call(bf16[16,320,512]{2,1,0:T(8,128)(2,1)} %pick.1.rows, bf16[2,8,512,128]{3,2,1,0:T(8,128)(2,1)} %get-tuple-element.18.slab), custom_call_target="tpu_custom_call" | custom-call | tf_op jit(solution)/shard_map/back/pallas_call | solution.py:541
  174.0 2.5 %copy.11 = f32[320,1024]{1,0:T(8,128)} copy(f32[320,1024]{1,0:T(8,128)} %back.1) | data formatting | bytes 2621440
  (8 shorter events, 0.1 us)
Async XLA Ops:
  0.0 31.8 %copy-start = (s32[1536]{0:T(1024)S(1)}, s32[1536]{0:T(1024)}, u32[]{:S(2)}) copy-start(s32[1536]{0:T(1024)} %param.13) | copy-start | bytes 18436
  3.3 30.3 %copy-start.1 = (f32[256]{0:T(256)}, f32[256]{0:T(256)S(1)}, u32[]{:S(2)}) copy-start(f32[256]{0:T(256)S(1)} %mul.54.weights) | copy-start | bytes 3076

commit v10 on v8

--- a/solution.py
+++ b/solution.py
@@ -30,7 +30,7 @@
     return (t - 96.0 * jnp.floor((t + 0.5) * (1.0 / 96.0))) * (math.pi / 48.0)
 
 
-def make_tables(ks, rows_of_blocks, tc, ts, rot, ph):
+def make_tables(ks, rows_of_blocks, tc, ts, rot, ph, table):
     width = LANES + JS
     ky, kz = ks[0:1, :], ks[1:2, :]
     odd = lambda n: 2.0 * lax.broadcasted_iota(jnp.int32, (n, width), 0).astype(jnp.float32) + 1.0
@@ -43,14 +43,25 @@
     shift = turn_angle(ky + kz)
     rot[0:1, :] = jnp.cos(shift[:, :LANES])
     rot[1:2, :] = jnp.sin(shift[:, :LANES])
-    plane = lax.broadcasted_iota(jnp.int32, (NX, JS), 0)
-    xs = plane
-    for b, block_row in enumerate(rows_of_blocks):
-        inside = (plane >= b * PX) & (plane < b * PX + PX)
-        xs = jnp.where(inside, plane + (block_row - b) * PX, xs)
-    theta = turn_angle((ky + kz)[:, LANES:] - 2.0 * xs.astype(jnp.float32) * ks[2:3, LANES:])
+
+    def true_plane(plane):
+        xs = plane
+        for b, block_row in enumerate(rows_of_blocks):
+            inside = (plane >= b * PX) & (plane < b * PX + PX)
+            xs = jnp.where(inside, plane + (block_row - b) * PX, xs)
+        return xs.astype(jnp.float32)
+
+    xs = true_plane(lax.broadcasted_iota(jnp.int32, (NX, JS), 0))
+    theta = turn_angle((ky + kz)[:, LANES:] - 2.0 * xs * ks[2:3, LANES:])
     ph[0] = jnp.cos(theta)
     ph[1] = jnp.sin(theta)
+    r = lax.broadcasted_iota(jnp.int32, (2 * NX, 2 * NX), 0)
+    c = lax.broadcasted_iota(jnp.int32, (2 * NX, 2 * NX), 1)
+    low, left = r < NX, c < NX
+    freq = jnp.where(low, r, r - NX).astype(jnp.float32)
+    angle = turn_angle(2.0 * freq * true_plane(jnp.where(left, c, c - NX)))
+    sine = jnp.sin(angle)
+    table[...] = jnp.where(low == left, jnp.cos(angle), jnp.where(low, sine, -sine)).astype(jnp.bfloat16)
 
 
 BLOCKS = 8
@@ -94,8 +105,8 @@
 
 
 def front_kernel(
-    weights, cond, val, ks, wide, table, m_out, slab_out,
-    tc, ts, rot, ph, cbuf, vbuf, vf, even, odd, y, sacc, sl, mo, mb,
+    weights, cond, val, ks, m_out, slab_out,
+    tc, ts, rot, ph, table, cbuf, vbuf, vf, even, odd, y, sacc, sl, mo, mb,
     lsem, cs, cr, vs, vr, gs, gr, ss, sr, fs, fr, ms,
 ):
     row, col = lax.axis_index("row"), lax.axis_index("col")
@@ -170,7 +181,7 @@
         cond_hop(n).start()
     sacc[...] = jnp.zeros_like(sacc)
     steps = [(0, 0), (0, 1), (0, 3), (1, 0), (0, 2), (1, 1), (1, 3), (1, 2)]
-    make_tables(ks, [(yh + dy) % 2 * 4 + (x + dx) % 4 for dy, dx in steps], tc, ts, rot, ph)
+    make_tables(ks, [(yh + dy) % 2 * 4 + (x + dx) % 4 for dy, dx in steps], tc, ts, rot, ph, table)
     for copy in own:
         copy.wait()
 
@@ -236,7 +247,7 @@
     lax.fori_loop(0, BLOCKS, block, 0)
 
     for h in range(2):
-        sl[h * PAIRS : h * PAIRS + PAIRS, :] = (sacc[h] * wide[...]).astype(jnp.bfloat16)
+        sl[h * PAIRS : h * PAIRS + PAIRS, :] = sacc[h].astype(jnp.bfloat16)
     keep = pltpu.make_async_copy(sl, slab_out.at[0, row], lsem.at[2])
     keep.start()
 
@@ -303,7 +314,7 @@
             spread(b, j).wait_send()
 
 
-def front(weights, cond, val, ks, wide, table):
+def front(weights, cond, val, ks):
     dma = pltpu.SemaphoreType.DMA
     vmem = pl.BlockSpec(memory_space=pltpu.VMEM)
     hbm = pl.BlockSpec(memory_space=pl.ANY)
@@ -311,7 +322,7 @@
     fl = lambda *shape: pltpu.VMEM(shape, jnp.float32)
     return pl.pallas_call(
         front_kernel,
-        in_specs=[pl.BlockSpec(memory_space=pltpu.SMEM)] + [vmem] * 5,
+        in_specs=[pl.BlockSpec(memory_space=pltpu.SMEM)] + [vmem] * 3,
         out_specs=[hbm, hbm],
         out_shape=[
             jax.ShapeDtypeStruct((2 * NX, PAIRS, LANES), jnp.bfloat16),
@@ -322,6 +333,7 @@
             bf(HALF, LANES + JS),
             fl(2, LANES),
             fl(2, NX, JS),
+            bf(2 * NX, 2 * NX),
             bf(BLOCKS, PX, CL, CELLS),
             bf(BLOCKS, 4, PX // 2, NV, HALF),
             fl(2, PX, NV, HALF),
@@ -339,7 +351,7 @@
             collective_id=2, has_side_effects=True, vmem_limit_bytes=VMEM_LIMIT
         ),
         name="front",
-    )(weights, cond, val, ks, wide, table)
+    )(weights, cond, val, ks)
 
 
 GB = 320
@@ -455,7 +467,7 @@
 
     lo, hi = pl.ds(0, LO), pl.ds(LO, HI)
     first = lambda n: remote(rows.at[place(n) + 1 - core], theirs.at[n], s1.at[n], d1.at[n], core_peer)
-    for n in range(8):
+    for n in range(2):
         first(n).start()
     for h in range(2):
         for r in range(NS // JS):
@@ -470,6 +482,11 @@
         k, s = (n // 2 + 1) % 4, n % 2
         load(n).wait()
         first(n).wait_recv()
+
+        @pl.when(n < 6)
+        def _():
+            first(n + 2).start()
+
         lhs = jnp.concatenate([ours[n], theirs[n]], axis=1)
         acc[n] = (jnp.dot(lhs, sw[...], preferred_element_type=jnp.float32) * scale).astype(jnp.bfloat16)
 
@@ -634,23 +651,8 @@
     ky, kz = flat // NZ, flat % NZ
     full_kx = jnp.concatenate([jnp.zeros((LANES,), jnp.int32), col_kx])
     ks = jnp.stack([ky, kz, full_kx]).astype(jnp.float32)
-    dy = jnp.array([0, 0, 0, 1, 0, 1, 1, 1], jnp.int32)
-    dx = jnp.array([0, 1, 3, 0, 2, 1, 3, 2], jnp.int32)
-    source = (row // 4 + dy) % 2 * 4 + (row % 4 + dx) % 4
-    xs = (source[:, None] * PX + jnp.arange(PX, dtype=jnp.int32)[None, :]).reshape(NX)
-    weight = jnp.sqrt(2.0 / (energy_cond[None, :] - energy_val[:, None])) * (
-        1.0 / (math.sqrt(NY * NZ) * math.sqrt(NX))
-    )
-    weight = weight.reshape(PAIRS)
-    wide = jnp.broadcast_to(weight[:, None], (PAIRS, JS))
-    freq = jnp.arange(NX, dtype=jnp.int32)
-    ax = (freq[:, None] * xs[None, :] % NX).astype(jnp.float32) * (2.0 * math.pi / NX)
-    cx, sx = jnp.cos(ax), jnp.sin(ax)
-    table = jnp.concatenate(
-        [jnp.concatenate([cx, sx], axis=1), jnp.concatenate([-sx, cx], axis=1)], axis=0
-    ).astype(jnp.bfloat16)
-
-    m, slab = front(weight, cond, val, ks, wide, table)
+    weight = (2.0 / (NY * NZ * NX)) / (energy_cond[None, :] - energy_val[:, None])
+    m, slab = front(weight.reshape(PAIRS), cond, val, ks)
     return back(pick(gvec_map, m.reshape(2, NX, PAIRS, LANES)), slab)
 
 

time: 175 us -> 174 us (level)
  no operation moved by 1% of the time
where the time goes in v10:
time: 174 us; the launch traced here: 173 us
  Pallas kernels  163 us (94%)
  local copies, waits for them, and re-layouts  7.48 us (4%)
  other arithmetic  2.94 us (2%)
    pallas_call x1, Pallas kernels, front(): pl.pallas_call(front_kernel, in_specs=[pl.BlockSpec(memory_space=pltpu.SM...  79.1 us
    pallas_call x1, Pallas kernels, back(): pl.pallas_call(back_kernel, in_specs=[pl.BlockSpec(memory_space=pl.ANY),...  56.3 us
    pallas_call x1, Pallas kernels, pick(): pl.pallas_call(pick_kernel, in_specs=[pl.BlockSpec(memory_space=pltpu.SME...  15.7 us
    pallas_call x1, Pallas kernels, places(): pl.pallas_call(places_kernel, in_specs=[pl.BlockSpec(memory_space=pltpu.V...  11.6 us

profile of v10, /device:TPU:1, one launch (start us, length us, event | category | flops | bytes accessed | tf_op | source)
XLA Modules:
  0.0 173.1 jit_solution(8440727932988339209)
XLA Ops:
  0.0 0.8 dynamic_slice.6
  0.8 0.8 compare_select_fusion.1
  1.5 0.1 pad.5.clone
  1.6 0.7 subtract_divide_fusion
  2.4 0.6 div.35.weights
  3.0 11.6 %places.1 = (s32[8,40,128]{2,1,0:T(8,128)}, bf16[6,16,2304]{2,1,0:T(8,128)(2,1)}, bf16[4,3,16,1152]{3,2,1,0:T(8,128)(2,1)}) custom-call(s32[40,128]{1,0:T(8,128)} %bitcast.12, bf16[6,16,2304]{2,1,0:T(8,128)(2,1)} %bitcast.10, bf16[6,16,2304]{2,1,0:T(8,128)(2,1)} %bitcast.11), custom_call_target="tpu_custom_call" | custom-call | tf_op jit(solution)/shard_map/places/pallas_call | solution.py:623
  14.6 1.8 %gather_fusion = s32[128]{0:T(128)S(1)} fusion(s32[40960]{0:T(1024)} %bitcast.9, s32[1024]{0:T(1024)S(1)} %pad_clamp_fusion.1), kind=kCustom, calls=%fused_computation | custom fusion | bytes 1536 | tf_op jit(solution)/shard_map/jit(_take)/gather | solution.py:646
  16.4 0.8 compare_select_fusion
  17.2 1.6 gather_fusion.1
  18.9 0.6 add_convert_fusion.ks
  19.5 79.1 %front.1 = (bf16[96,256,256]{2,1,0:T(8,128)(2,1)}, bf16[2,8,512,128]{3,2,1,0:T(8,128)(2,1)}) custom-call(f32[256]{0:T(256)} %div.35.weights, bf16[6,16,2304]{2,1,0:T(8,128)(2,1)} %get-tuple-element.10.cond, bf16[4,3,16,1152]{3,2,1,0:T(8,128)(2,1)} %get-tuple-element.11.val, f32[3,384]{1,0:T(4,128)} %add_convert_fusion.ks), custom_call_target="tpu_custom_call" | custom-call | tf_op jit(solution)/shard_map/front/pallas_call | solution.py:323
  98.7 15.7 %pick.1.rows = bf16[16,320,512]{2,1,0:T(8,128)(2,1)} custom-call(s32[5120]{0:T(1024)} %g_ref.1, bf16[2,48,256,256]{3,2,1,0:T(8,128)(2,1)} %bitcast.8), custom_call_target="tpu_custom_call" | custom-call | tf_op jit(solution)/shard_map/pick/pallas_call | solution.py:416
  114.3 56.3 %back.1 = f32[320,1024]{1,0:T(8,128)} custom-call(bf16[16,320,512]{2,1,0:T(8,128)(2,1)} %pick.1.rows, bf16[2,8,512,128]{3,2,1,0:T(8,128)(2,1)} %get-tuple-element.14.slab), custom_call_target="tpu_custom_call" | custom-call | tf_op jit(solution)/shard_map/back/pallas_call | solution.py:562
  170.6 2.5 %copy.9 = f32[320,1024]{1,0:T(8,128)} copy(f32[320,1024]{1,0:T(8,128)} %back.1) | data formatting | bytes 2621440
  (8 shorter events, 0.1 us)

commit v11 on v10

--- a/solution.py
+++ b/solution.py
@@ -359,8 +359,8 @@
 G_DEV = 320
 LO = 192
 HI = G_DEV - LO
-DEPTH = 16
-UNROLL = 32
+DEPTH = 24
+UNROLL = 64
 
 
 def pick_kernel(g_ref, m, out, mt, mi, sel, lhs, ms, os):
@@ -384,7 +384,7 @@
 
         return carry
 
-    lax.fori_loop(0, NX, turn, 0, unroll=4)
+    lax.fori_loop(0, NX, turn, 0, unroll=8)
     store = lambda n: pltpu.make_async_copy(lhs.at[n % 2], out.at[n], os.at[n % 2])
 
     def block(n, carry):

time: 174 us -> 174 us (level)
  no operation moved by 1% of the time
where the time goes in v11:
time: 174 us; the launch traced here: 173 us
  Pallas kernels  162 us (93%)
  local copies, waits for them, and re-layouts  7.48 us (4%)
  other arithmetic  2.94 us (2%)
    pallas_call x1, Pallas kernels, front(): pl.pallas_call(front_kernel, in_specs=[pl.BlockSpec(memory_space=pltpu.SM...  79.1 us
    pallas_call x1, Pallas kernels, back(): pl.pallas_call(back_kernel, in_specs=[pl.BlockSpec(memory_space=pl.ANY),...  56.3 us
    pallas_call x1, Pallas kernels, pick(): pl.pallas_call(pick_kernel, in_specs=[pl.BlockSpec(memory_space=pltpu.SME...  15.5 us
    pallas_call x1, Pallas kernels, places(): pl.pallas_call(places_kernel, in_specs=[pl.BlockSpec(memory_space=pltpu.V...  11.6 us

profile of v11, /device:TPU:1, one launch (start us, length us, event | category | flops | bytes accessed | tf_op | source)
XLA Modules:
  0.0 173.0 jit_solution(7454358750592286751)
XLA Ops:
  0.0 0.8 dynamic_slice.6
  0.8 0.8 compare_select_fusion.1
  1.5 0.1 pad.5.clone
  1.6 0.7 subtract_divide_fusion
  2.4 0.6 div.35.weights
  3.0 11.6 %places.1 = (s32[8,40,128]{2,1,0:T(8,128)}, bf16[6,16,2304]{2,1,0:T(8,128)(2,1)}, bf16[4,3,16,1152]{3,2,1,0:T(8,128)(2,1)}) custom-call(s32[40,128]{1,0:T(8,128)} %bitcast.12, bf16[6,16,2304]{2,1,0:T(8,128)(2,1)} %bitcast.10, bf16[6,16,2304]{2,1,0:T(8,128)(2,1)} %bitcast.11), custom_call_target="tpu_custom_call" | custom-call | tf_op jit(solution)/shard_map/places/pallas_call | solution.py:623
  14.6 1.8 %gather_fusion = s32[128]{0:T(128)S(1)} fusion(s32[40960]{0:T(1024)} %bitcast.9, s32[1024]{0:T(1024)S(1)} %pad_clamp_fusion.1), kind=kCustom, calls=%fused_computation | custom fusion | bytes 1536 | tf_op jit(solution)/shard_map/jit(_take)/gather | solution.py:646
  16.4 0.8 compare_select_fusion
  17.2 1.6 gather_fusion.1
  18.9 0.6 add_convert_fusion.ks
  19.5 79.1 %front.1 = (bf16[96,256,256]{2,1,0:T(8,128)(2,1)}, bf16[2,8,512,128]{3,2,1,0:T(8,128)(2,1)}) custom-call(f32[256]{0:T(256)} %div.35.weights, bf16[6,16,2304]{2,1,0:T(8,128)(2,1)} %get-tuple-element.10.cond, bf16[4,3,16,1152]{3,2,1,0:T(8,128)(2,1)} %get-tuple-element.11.val, f32[3,384]{1,0:T(4,128)} %add_convert_fusion.ks), custom_call_target="tpu_custom_call" | custom-call | tf_op jit(solution)/shard_map/front/pallas_call | solution.py:323
  98.6 15.5 %pick.1.rows = bf16[16,320,512]{2,1,0:T(8,128)(2,1)} custom-call(s32[5120]{0:T(1024)} %g_ref.1, bf16[2,48,256,256]{3,2,1,0:T(8,128)(2,1)} %bitcast.8), custom_call_target="tpu_custom_call" | custom-call | tf_op jit(solution)/shard_map/pick/pallas_call | solution.py:416
  114.2 56.3 %back.1 = f32[320,1024]{1,0:T(8,128)} custom-call(bf16[16,320,512]{2,1,0:T(8,128)(2,1)} %pick.1.rows, bf16[2,8,512,128]{3,2,1,0:T(8,128)(2,1)} %get-tuple-element.14.slab), custom_call_target="tpu_custom_call" | custom-call | tf_op jit(solution)/shard_map/back/pallas_call | solution.py:562
  170.5 2.5 %copy.9 = f32[320,1024]{1,0:T(8,128)} copy(f32[320,1024]{1,0:T(8,128)} %back.1) | data formatting | bytes 2621440
  (8 shorter events, 0.1 us)

commit v12 on v11

--- a/solution.py
+++ b/solution.py
@@ -293,7 +293,7 @@
 
         for h in range(LANES // 128):
             lanes = slice(h * 128, h * 128 + 128)
-            mb[slot, :, :, lanes] = mo[h].reshape(2 * NX, MS, 128)[:, :PB].astype(jnp.bfloat16)
+            mb[slot, :, :, lanes] = mo[h, : 2 * NX * MS, :].reshape(2 * NX, MS, 128)[:, :PB].astype(jnp.bfloat16)
         out.start()
         return carry
 
@@ -339,10 +339,10 @@
             fl(2, PX, NV, HALF),
             bf(PT * PAIRS, HALF),
             bf(PT * PAIRS, HALF),
-            fl(2, LANES // 128, NX * YS, 128),
+            fl(2, LANES // 128, NX * YS + YS, 128),
             fl(2, PAIRS, JS),
             bf(2 * PAIRS, JS),
-            fl(2, 2 * NX * MS, 128),
+            fl(2, 2 * NX * MS + MS, 128),
             bf(2, 2 * NX, PB, LANES),
             dma((3,)), dma((7,)), dma((8,)), dma((7,)), dma((8,)),
             dma((24,)), dma((24,)), dma((7,)), dma((7,)), dma((8,)), dma((8,)), dma((2,)),
@@ -419,9 +419,9 @@
         out_specs=pl.BlockSpec(memory_space=pl.ANY),
         out_shape=jax.ShapeDtypeStruct((G_ROW // GB, GB, 2 * PAIRS), jnp.bfloat16),
         scratch_shapes=[
-            pltpu.VMEM((NX * STK * QS, 128), jnp.float32),
+            pltpu.VMEM((NX * STK * QS + 8, 128), jnp.float32),
             pltpu.VMEM((DEPTH, 2, PAIRS, LANES), jnp.bfloat16),
-            pltpu.VMEM((GB * QS, 128), jnp.float32),
+            pltpu.VMEM((GB * QS + 8, 128), jnp.float32),
             pltpu.VMEM((2, GB, 2 * PAIRS), jnp.bfloat16),
             dma((DEPTH,)), dma((2,)),
         ],

time: 174 us -> 174 us (level)
  no operation moved by 1% of the time
where the time goes in v12:
time: 174 us; the launch traced here: 173 us
  Pallas kernels  162 us (93%)
  local copies, waits for them, and re-layouts  7.48 us (4%)
  other arithmetic  2.94 us (2%)
    pallas_call x1, Pallas kernels, front(): pl.pallas_call(front_kernel, in_specs=[pl.BlockSpec(memory_space=pltpu.SM...  79.1 us
    pallas_call x1, Pallas kernels, back(): pl.pallas_call(back_kernel, in_specs=[pl.BlockSpec(memory_space=pl.ANY),...  56.3 us
    pallas_call x1, Pallas kernels, pick(): pl.pallas_call(pick_kernel, in_specs=[pl.BlockSpec(memory_space=pltpu.SME...  15.5 us
    pallas_call x1, Pallas kernels, places(): pl.pallas_call(places_kernel, in_specs=[pl.BlockSpec(memory_space=pltpu.V...  11.6 us

profile of v12, /device:TPU:1, one launch (start us, length us, event | category | flops | bytes accessed | tf_op | source)
XLA Modules:
  0.0 173.0 jit_solution(6236050392999042820)
XLA Ops:
  0.0 0.8 dynamic_slice.6
  0.8 0.8 compare_select_fusion.1
  1.5 0.1 pad.5.clone
  1.6 0.7 subtract_divide_fusion
  2.4 0.6 div.35.weights
  3.0 11.6 %places.1 = (s32[8,40,128]{2,1,0:T(8,128)}, bf16[6,16,2304]{2,1,0:T(8,128)(2,1)}, bf16[4,3,16,1152]{3,2,1,0:T(8,128)(2,1)}) custom-call(s32[40,128]{1,0:T(8,128)} %bitcast.12, bf16[6,16,2304]{2,1,0:T(8,128)(2,1)} %bitcast.10, bf16[6,16,2304]{2,1,0:T(8,128)(2,1)} %bitcast.11), custom_call_target="tpu_custom_call" | custom-call | tf_op jit(solution)/shard_map/places/pallas_call | solution.py:623
  14.6 1.8 %gather_fusion = s32[128]{0:T(128)S(1)} fusion(s32[40960]{0:T(1024)} %bitcast.9, s32[1024]{0:T(1024)S(1)} %pad_clamp_fusion.1), kind=kCustom, calls=%fused_computation | custom fusion | bytes 1536 | tf_op jit(solution)/shard_map/jit(_take)/gather | solution.py:646
  16.4 0.8 compare_select_fusion
  17.2 1.6 gather_fusion.1
  18.9 0.6 add_convert_fusion.ks
  19.5 79.1 %front.1 = (bf16[96,256,256]{2,1,0:T(8,128)(2,1)}, bf16[2,8,512,128]{3,2,1,0:T(8,128)(2,1)}) custom-call(f32[256]{0:T(256)} %div.35.weights, bf16[6,16,2304]{2,1,0:T(8,128)(2,1)} %get-tuple-element.10.cond, bf16[4,3,16,1152]{3,2,1,0:T(8,128)(2,1)} %get-tuple-element.11.val, f32[3,384]{1,0:T(4,128)} %add_convert_fusion.ks), custom_call_target="tpu_custom_call" | custom-call | tf_op jit(solution)/shard_map/front/pallas_call | solution.py:323
  98.6 15.5 %pick.1.rows = bf16[16,320,512]{2,1,0:T(8,128)(2,1)} custom-call(s32[5120]{0:T(1024)} %g_ref.1, bf16[2,48,256,256]{3,2,1,0:T(8,128)(2,1)} %bitcast.8), custom_call_target="tpu_custom_call" | custom-call | tf_op jit(solution)/shard_map/pick/pallas_call | solution.py:416
  114.2 56.3 %back.1 = f32[320,1024]{1,0:T(8,128)} custom-call(bf16[16,320,512]{2,1,0:T(8,128)(2,1)} %pick.1.rows, bf16[2,8,512,128]{3,2,1,0:T(8,128)(2,1)} %get-tuple-element.14.slab), custom_call_target="tpu_custom_call" | custom-call | tf_op jit(solution)/shard_map/back/pallas_call | solution.py:562
  170.4 2.5 %copy.9 = f32[320,1024]{1,0:T(8,128)} copy(f32[320,1024]{1,0:T(8,128)} %back.1) | data formatting | bytes 2621440
  (8 shorter events, 0.1 us)
